TPU v7x, 128 devices: a whole 4x4x4 slice. The times are simulated.
128 devices in a mesh: wide: 8 (over y, core), narrow: 16 (over z, x).
Axes of the slice: x: 4, y: 4, z: 4, core: 2. Of those that a mesh axis runs over, the one named last changes fastest.
Arguments:
- positions: float32 [3, 1048576], P(None, ('wide', 'narrow')), may hold values from 0 to 1
- masses: float32 [1048576], P(('wide', 'narrow')), may hold values from 0.001 to 0.01
- node_mass: float32 [32768], P(('wide', 'narrow')), may hold values from 0.01 to 0.1
- node_centre: float32 [3, 32768], P(None, ('wide', 'narrow')), may hold values from 0 to 1
- node_quad: float32 [6, 32768], P(None, ('wide', 'narrow')), may hold values from -0.018 to 0.018
- local_leaves: int32 [8192, 8], P(('wide', 'narrow')), may hold values from 0 to 63
- node_lists: int32 [8192, 64], P(('wide', 'narrow')), may hold values from 0 to 32767
- export_block: int32 [16384], P(('wide', 'narrow')), may hold values from 0 to 63
- export_dest: int32 [16384, 1], P(('wide', 'narrow')), may hold values from 0 to 127; in each aligned block of 128 rows (0 to 127, 128 to 255, ...) at most 2 rows name the same one
- export_leaves: int32 [16384, 8], P(('wide', 'narrow')), may hold values from 0 to 63
Outputs:
- accel: float32 [3, 1048576], P(None, ('wide', 'narrow'))
Inputs may be any that keep to these rules, and one draw needn't show every extreme that they name: `export_dest`: in the exports of one device no destination appears more than 2 times, and some destination appears exactly 2 times.
All inputs are finite; a program needn't handle non-finite values.
Results may differ from a plain program's by a relative error of at most 0.00014.
Values sent between devices are 32-bit elements; how exact they have to be, the bound alone decides.
No kernel may reach another device: no remote copies, remote signals or barrier semaphores. Data moves between devices by JAX's collectives and lax.ppermute only.
A program may use at most 128 MiB of HBM per device.

v0:
```python
import jax
import jax.numpy as jnp
from jax import lax
from jax.sharding import PartitionSpec as P

ROWS = 128
LEAF_N = 8
CAP = 2


soften_sq = 0.01


def pair_pull(target, sources, source_mass):
    delta = sources[:, :, None, :] - target[None, :, :, None]
    spread = jnp.sum(delta * delta, axis=1) + soften_sq
    factor = source_mass[:, None, :] / (spread * jnp.sqrt(spread))
    return jnp.sum(delta * factor[:, None, :, :], axis=(0, 3))


def node_pull(target, mass_list, centre_list, quad_list):
    relative = target[:, None, :] - centre_list[:, :, None]
    along_x = relative[0]
    along_y = relative[1]
    along_z = relative[2]
    spread = along_x * along_x + along_y * along_y + along_z * along_z + soften_sq
    quads = quad_list[:, :, None]
    quad_x = quads[0] * along_x + quads[3] * along_y + quads[4] * along_z
    quad_y = quads[3] * along_x + quads[1] * along_y + quads[5] * along_z
    quad_z = quads[4] * along_x + quads[5] * along_y + quads[2] * along_z
    inverse = 1.0 / spread
    cubed = inverse * jnp.sqrt(inverse)
    scalar = along_x * quad_x + along_y * quad_y + along_z * quad_z
    radial = -mass_list[:, None] * cubed - 2.5 * scalar * cubed * inverse * inverse
    quad_vec = jnp.stack([quad_x, quad_y, quad_z])
    total = radial[None] * relative + quad_vec * (cubed * inverse)[None]
    return jnp.sum(total, axis=1)


def per_device(
    positions,
    masses,
    node_mass,
    node_centre,
    node_quad,
    local_leaves,
    node_lists,
    export_block,
    export_dest,
    export_leaves,
):
    block_count = masses.shape[0] // ROWS
    blocks = positions.reshape(3, block_count, ROWS).transpose(1, 0, 2)
    block_mass = masses.reshape(block_count, ROWS)
    groups = lax.axis_size("wide")
    members = lax.axis_size("narrow")
    devices = groups * members
    export_count = export_block.shape[0]
    target_dev = export_dest[:, 0]
    same_dest = target_dev[:, None] == target_dev[None, :]
    earlier = lax.broadcasted_iota(
        jnp.int32, (export_count, export_count), 1
    ) < lax.broadcasted_iota(jnp.int32, (export_count, export_count), 0)
    slot_index = jnp.sum((same_dest & earlier).astype(jnp.int32), axis=1)
    flat_slot = target_dev * CAP + slot_index
    payload = blocks[export_block]
    outgoing = jnp.zeros((devices * CAP, 3, ROWS), jnp.float32).at[flat_slot].set(payload)
    outgoing_ids = jnp.zeros((devices * CAP, LEAF_N), jnp.int32).at[flat_slot].set(export_leaves)
    arrived = lax.all_to_all(
        outgoing.reshape(devices, CAP, 3, ROWS),
        ("wide", "narrow"),
        split_axis=0,
        concat_axis=0,
        tiled=True,
    )
    arrived_ids = lax.all_to_all(
        outgoing_ids.reshape(devices, CAP, LEAF_N),
        ("wide", "narrow"),
        split_axis=0,
        concat_axis=0,
        tiled=True,
    )
    leading = arrived.shape[0]
    slots_here = arrived.shape[1]
    visiting_arrived = arrived.reshape(leading * slots_here, 3, ROWS)
    visiting_arrived_ids = arrived_ids.reshape(leading * slots_here, LEAF_N)

    def single(packed):
        visitor, leaf_ids = packed
        return pair_pull(visitor, blocks[leaf_ids], block_mass[leaf_ids])

    pull_sums = lax.map(single, (visiting_arrived, visiting_arrived_ids), batch_size=16)
    pull_sums = pull_sums.reshape(leading, slots_here, 3, ROWS)
    answers = lax.all_to_all(pull_sums, ("wide", "narrow"), split_axis=0, concat_axis=0, tiled=True)
    returned = answers.reshape(devices * CAP, 3, ROWS)[flat_slot]
    selector = (
        export_block[None, :] == lax.broadcasted_iota(jnp.int32, (block_count, export_count), 0)
    ).astype(jnp.float32)
    imported = jnp.einsum("be,ecr->bcr", selector, returned, precision=lax.Precision.HIGHEST)
    all_mass, all_centre, all_quad = (
        lax.all_gather(node_mass, ("wide", "narrow"), axis=0, tiled=True),
        lax.all_gather(node_centre, ("wide", "narrow"), axis=1, tiled=True),
        lax.all_gather(node_quad, ("wide", "narrow"), axis=1, tiled=True),
    )

    def local_term(packed):
        places, leaf_ids, node_ids = packed
        direct = pair_pull(places, blocks[leaf_ids], block_mass[leaf_ids])
        return direct + node_pull(
            places, all_mass[node_ids], all_centre[:, node_ids], all_quad[:, node_ids]
        )

    local = lax.map(local_term, (blocks, local_leaves, node_lists), batch_size=16)
    total = local + imported
    return total.transpose(1, 0, 2).reshape(3, block_count * ROWS)


def solution(mesh):
    return jax.shard_map(
        per_device,
        mesh=mesh,
        in_specs=(
            P(None, ("wide", "narrow")),
            P(("wide", "narrow")),
            P(("wide", "narrow")),
            P(None, ("wide", "narrow")),
            P(None, ("wide", "narrow")),
            P(("wide", "narrow"), None),
            P(("wide", "narrow"), None),
            P(("wide", "narrow")),
            P(("wide", "narrow"), None),
            P(("wide", "narrow"), None),
        ),
        out_specs=P(None, ("wide", "narrow")),
        check_vma=False,
    )
```

profile of v0, /device:TPU:1, one launch (start us, length us, event | category | flops | bytes accessed | tf_op | source)
XLA Modules:
  0.0 924.6 jit_solution(10419341576825148934)
XLA Ops:
  3.8 11.5 %all-to-all-start = ((s32[128,2,8]{2,1,0:T(2,128)}), s32[128,2,8]{2,1,0:T(2,128)S(1)}, u32[]{:S(2)}, u32[]{:S(2)}) async-start(s32[128,2,8]{2,1,0:T(2,128)} %bitcast.42), calls=%async_computation | async-start | bytes 262144 | tf_op jit(solution)/shard_map/all_to_all | solution.py:76
  16.2 107.0 %all_gather.10 = f32[3,32768]{0,1:T(8,128)} all-gather(f32[3,256]{0,1:T(8,128)S(1)} %copy.130), channel_id=1, replica_groups=mesh['wide'=8,'narrow'=16] {'wide','narrow'}, dimensions={1}, use_global_device_ids=true | all-gather | bytes 396288 | tf_op jit(solution)/shard_map/all_gather | solution.py:102
  123.3 51.7 %all-gather = f32[128,1,256]{2,1,0:T(1,128)S(1)} all-gather(f32[1,1,256]{2,1,0:T(1,128)S(1)} %bitcast.188), channel_id=1, replica_groups=mesh['wide'=8,'narrow'=16] {'wide','narrow'}, dimensions={0}, use_global_device_ids=true | all-gather | bytes 132096 | tf_op jit(solution)/shard_map/all_gather | solution.py:101
  188.6 107.1 %all_gather.11 = f32[6,32768]{0,1:T(8,128)} all-gather(f32[6,256]{0,1:T(8,128)S(1)} %copy.131), channel_id=1, replica_groups=mesh['wide'=8,'narrow'=16] {'wide','narrow'}, dimensions={1}, use_global_device_ids=true | all-gather | bytes 792576 | tf_op jit(solution)/shard_map/all_gather | solution.py:103
  295.9 390.1 %while.21 = (s32[]{:T(128)}, f32[16,16,3,128]{3,2,1,0:T(4,128)S(1)}, s32[16,16,8]{1,2,0:T(8,128)S(1)}, f32[64,3,128]{2,1,0:T(4,128)S(1)}, f32[16,16,3,128]{3,1,0...) while((s32[]{:T(128)}, f32[16,16,3,128]{3,2,1,0:T(4,128)S(1)}, s32[16,16,8]{1,2,0:T(8,128)S(1)}, ...), condition=%wide.region_11.12_spmd, body=%wide.region_8.11_spmd.sunk | while | flops 41938304 | bytes 34783840 | solution.py:92
  296.9 6.7 fusion.48
  304.2 9.6 %fusion.49 = f32[16,8,128,128]{3,2,1,0:T(8,128)} fusion(f32[16,8,128,128]{3,2,1,0:T(8,128)} %fusion.48, f32[16,8,128]{2,1,0:T(8,128)S(1)} %bitcast.178), kind=kLoop, calls=%fused_computation.66.clone.1 | loop fusion | flops 6291456 | bytes 16842752 | tf_op jit(solution)/shard_map/while/body/eval_jaxpr/vmap()/div | solution.py:17
  321.3 6.7 fusion.48
  328.6 9.6 %fusion.49 = f32[16,8,128,128]{3,2,1,0:T(8,128)} fusion(f32[16,8,128,128]{3,2,1,0:T(8,128)} %fusion.48, f32[16,8,128]{2,1,0:T(8,128)S(1)} %bitcast.178), kind=kLoop, calls=%fused_computation.66.clone.1 | loop fusion | flops 6291456 | bytes 16842752 | tf_op jit(solution)/shard_map/while/body/eval_jaxpr/vmap()/div | solution.py:17
  345.6 6.7 fusion.48
  353.0 9.6 %fusion.49 = f32[16,8,128,128]{3,2,1,0:T(8,128)} fusion(f32[16,8,128,128]{3,2,1,0:T(8,128)} %fusion.48, f32[16,8,128]{2,1,0:T(8,128)S(1)} %bitcast.178), kind=kLoop, calls=%fused_computation.66.clone.1 | loop fusion | flops 6291456 | bytes 16842752 | tf_op jit(solution)/shard_map/while/body/eval_jaxpr/vmap()/div | solution.py:17
  370.0 6.7 fusion.48
  377.4 9.6 %fusion.49 = f32[16,8,128,128]{3,2,1,0:T(8,128)} fusion(f32[16,8,128,128]{3,2,1,0:T(8,128)} %fusion.48, f32[16,8,128]{2,1,0:T(8,128)S(1)} %bitcast.178), kind=kLoop, calls=%fused_computation.66.clone.1 | loop fusion | flops 6291456 | bytes 16842752 | tf_op jit(solution)/shard_map/while/body/eval_jaxpr/vmap()/div | solution.py:17
  394.4 6.7 fusion.48
  401.8 9.6 %fusion.49 = f32[16,8,128,128]{3,2,1,0:T(8,128)} fusion(f32[16,8,128,128]{3,2,1,0:T(8,128)} %fusion.48, f32[16,8,128]{2,1,0:T(8,128)S(1)} %bitcast.178), kind=kLoop, calls=%fused_computation.66.clone.1 | loop fusion | flops 6291456 | bytes 16842752 | tf_op jit(solution)/shard_map/while/body/eval_jaxpr/vmap()/div | solution.py:17
  418.8 6.7 fusion.48
  426.2 9.6 %fusion.49 = f32[16,8,128,128]{3,2,1,0:T(8,128)} fusion(f32[16,8,128,128]{3,2,1,0:T(8,128)} %fusion.48, f32[16,8,128]{2,1,0:T(8,128)S(1)} %bitcast.178), kind=kLoop, calls=%fused_computation.66.clone.1 | loop fusion | flops 6291456 | bytes 16842752 | tf_op jit(solution)/shard_map/while/body/eval_jaxpr/vmap()/div | solution.py:17
  443.2 6.7 fusion.48
  450.5 9.6 %fusion.49 = f32[16,8,128,128]{3,2,1,0:T(8,128)} fusion(f32[16,8,128,128]{3,2,1,0:T(8,128)} %fusion.48, f32[16,8,128]{2,1,0:T(8,128)S(1)} %bitcast.178), kind=kLoop, calls=%fused_computation.66.clone.1 | loop fusion | flops 6291456 | bytes 16842752 | tf_op jit(solution)/shard_map/while/body/eval_jaxpr/vmap()/div | solution.py:17
  467.5 6.7 fusion.48
  474.9 9.6 %fusion.49 = f32[16,8,128,128]{3,2,1,0:T(8,128)} fusion(f32[16,8,128,128]{3,2,1,0:T(8,128)} %fusion.48, f32[16,8,128]{2,1,0:T(8,128)S(1)} %bitcast.178), kind=kLoop, calls=%fused_computation.66.clone.1 | loop fusion | flops 6291456 | bytes 16842752 | tf_op jit(solution)/shard_map/while/body/eval_jaxpr/vmap()/div | solution.py:17
  499.3 9.6 %fusion.49 = f32[16,8,128,128]{3,2,1,0:T(8,128)} fusion(f32[16,8,128,128]{3,2,1,0:T(8,128)} %fusion.48, f32[16,8,128]{2,1,0:T(8,128)S(1)} %bitcast.178), kind=kLoop, calls=%fused_computation.66.clone.1 | loop fusion | flops 6291456 | bytes 16842752 | tf_op jit(solution)/shard_map/while/body/eval_jaxpr/vmap()/div | solution.py:17
  523.7 9.6 %fusion.49 = f32[16,8,128,128]{3,2,1,0:T(8,128)} fusion(f32[16,8,128,128]{3,2,1,0:T(8,128)} %fusion.48, f32[16,8,128]{2,1,0:T(8,128)S(1)} %bitcast.178), kind=kLoop, calls=%fused_computation.66.clone.1 | loop fusion | flops 6291456 | bytes 16842752 | tf_op jit(solution)/shard_map/while/body/eval_jaxpr/vmap()/div | solution.py:17
  548.1 9.6 %fusion.49 = f32[16,8,128,128]{3,2,1,0:T(8,128)} fusion(f32[16,8,128,128]{3,2,1,0:T(8,128)} %fusion.48, f32[16,8,128]{2,1,0:T(8,128)S(1)} %bitcast.178), kind=kLoop, calls=%fused_computation.66.clone.1 | loop fusion | flops 6291456 | bytes 16842752 | tf_op jit(solution)/shard_map/while/body/eval_jaxpr/vmap()/div | solution.py:17
  565.1 6.7 fusion.48
  572.5 9.6 %fusion.49 = f32[16,8,128,128]{3,2,1,0:T(8,128)} fusion(f32[16,8,128,128]{3,2,1,0:T(8,128)} %fusion.48, f32[16,8,128]{2,1,0:T(8,128)S(1)} %bitcast.178), kind=kLoop, calls=%fused_computation.66.clone.1 | loop fusion | flops 6291456 | bytes 16842752 | tf_op jit(solution)/shard_map/while/body/eval_jaxpr/vmap()/div | solution.py:17
  589.5 6.7 fusion.48
  596.8 9.6 %fusion.49 = f32[16,8,128,128]{3,2,1,0:T(8,128)} fusion(f32[16,8,128,128]{3,2,1,0:T(8,128)} %fusion.48, f32[16,8,128]{2,1,0:T(8,128)S(1)} %bitcast.178), kind=kLoop, calls=%fused_computation.66.clone.1 | loop fusion | flops 6291456 | bytes 16842752 | tf_op jit(solution)/shard_map/while/body/eval_jaxpr/vmap()/div | solution.py:17
  613.8 6.7 fusion.48
  621.2 9.6 %fusion.49 = f32[16,8,128,128]{3,2,1,0:T(8,128)} fusion(f32[16,8,128,128]{3,2,1,0:T(8,128)} %fusion.48, f32[16,8,128]{2,1,0:T(8,128)S(1)} %bitcast.178), kind=kLoop, calls=%fused_computation.66.clone.1 | loop fusion | flops 6291456 | bytes 16842752 | tf_op jit(solution)/shard_map/while/body/eval_jaxpr/vmap()/div | solution.py:17
  638.2 6.7 fusion.48
  645.6 9.6 %fusion.49 = f32[16,8,128,128]{3,2,1,0:T(8,128)} fusion(f32[16,8,128,128]{3,2,1,0:T(8,128)} %fusion.48, f32[16,8,128]{2,1,0:T(8,128)S(1)} %bitcast.178), kind=kLoop, calls=%fused_computation.66.clone.1 | loop fusion | flops 6291456 | bytes 16842752 | tf_op jit(solution)/shard_map/while/body/eval_jaxpr/vmap()/div | solution.py:17
  670.0 9.6 %fusion.49 = f32[16,8,128,128]{3,2,1,0:T(8,128)} fusion(f32[16,8,128,128]{3,2,1,0:T(8,128)} %fusion.48, f32[16,8,128]{2,1,0:T(8,128)S(1)} %bitcast.178), kind=kLoop, calls=%fused_computation.66.clone.1 | loop fusion | flops 6291456 | bytes 16842752 | tf_op jit(solution)/shard_map/while/body/eval_jaxpr/vmap()/div | solution.py:17
  687.0 8.0 all-to-all-start.2
  695.0 225.1 %while.20 = (s32[]{:T(128)}, f32[4,16,3,128]{3,1,0,2:T(8,128)}, s32[4,16,8]{1,0,2:T(4,128)}, f32[64,3,128]{2,1,0:T(4,128)S(1)}, f32[4,16,3,128]{3,1,2,0:T(8,128)...) while((s32[]{:T(128)}, f32[4,16,3,128]{3,1,0,2:T(8,128)}, ...), condition=%wide.region_4.5_spmd, body=%wide.region_0.4_spmd.sunk | while | flops 51642752 | bytes 45262552 | solution.py:113
  705.0 9.6 %fusion.42 = f32[16,8,128,128]{3,2,1,0:T(8,128)} fusion(f32[16,8,128,128]{3,2,1,0:T(8,128)} %fusion.41, f32[16,8,128]{2,1,0:T(8,128)S(1)} %bitcast.179), kind=kLoop, calls=%fused_computation.16.clone.1 | loop fusion | flops 6291456 | bytes 16842752 | tf_op jit(solution)/shard_map/while/body/eval_jaxpr/vmap()/div | solution.py:17
  721.8 8.6 gather_fusion.2
  731.1 8.6 gather_fusion.3
  761.3 9.6 %fusion.42 = f32[16,8,128,128]{3,2,1,0:T(8,128)} fusion(f32[16,8,128,128]{3,2,1,0:T(8,128)} %fusion.41, f32[16,8,128]{2,1,0:T(8,128)S(1)} %bitcast.179), kind=kLoop, calls=%fused_computation.16.clone.1 | loop fusion | flops 6291456 | bytes 16842752 | tf_op jit(solution)/shard_map/while/body/eval_jaxpr/vmap()/div | solution.py:17
  778.0 8.6 gather_fusion.2
  787.3 8.6 gather_fusion.3
  817.5 9.6 %fusion.42 = f32[16,8,128,128]{3,2,1,0:T(8,128)} fusion(f32[16,8,128,128]{3,2,1,0:T(8,128)} %fusion.41, f32[16,8,128]{2,1,0:T(8,128)S(1)} %bitcast.179), kind=kLoop, calls=%fused_computation.16.clone.1 | loop fusion | flops 6291456 | bytes 16842752 | tf_op jit(solution)/shard_map/while/body/eval_jaxpr/vmap()/div | solution.py:17
  834.2 8.6 gather_fusion.2
  843.5 8.6 gather_fusion.3
  866.3 6.7 fusion.41
  873.7 9.6 %fusion.42 = f32[16,8,128,128]{3,2,1,0:T(8,128)} fusion(f32[16,8,128,128]{3,2,1,0:T(8,128)} %fusion.41, f32[16,8,128]{2,1,0:T(8,128)S(1)} %bitcast.179), kind=kLoop, calls=%fused_computation.16.clone.1 | loop fusion | flops 6291456 | bytes 16842752 | tf_op jit(solution)/shard_map/while/body/eval_jaxpr/vmap()/div | solution.py:17
  890.5 8.6 gather_fusion.2
  899.7 8.6 gather_fusion.3
  (333 shorter events, 289.5 us)
Async XLA Ops:
  1.6 175.7 %copy-start.7 = (s32[128]{0:T(128)}, s32[128]{0:T(128)S(1)}, u32[]{:S(2)}) copy-start(s32[128]{0:T(128)S(1)} %fusion.30) | copy-start | bytes 1540
  3.8 178.8 %all-to-all-start = ((s32[128,2,8]{2,1,0:T(2,128)}), s32[128,2,8]{2,1,0:T(2,128)S(1)}, u32[]{:S(2)}, u32[]{:S(2)}) async-start(s32[128,2,8]{2,1,0:T(2,128)} %bitcast.42), calls=%async_computation | async-start | bytes 262144 | tf_op jit(solution)/shard_map/all_to_all | solution.py:76
  16.2 107.1 %copy-start.9 = (s32[128]{0:T(128)S(1)}, s32[128]{0:T(128)}, u32[]{:S(2)}) copy-start(s32[128]{0:T(128)} %param.21) | copy-start | bytes 1540
  16.2 107.1 %copy-start.8 = (f32[256]{0:T(256)S(1)}, f32[256]{0:T(256)}, u32[]{:S(2)}) copy-start(f32[256]{0:T(256)} %param.16) | copy-start | bytes 3076
  16.2 158.8 %copy-start.6 = (s32[64,8]{0,1:T(8,128)S(1)}, s32[64,8]{0,1:T(8,128)}, u32[]{:S(2)}) copy-start(s32[64,8]{0,1:T(8,128)} %param.19) | copy-start | bytes 6148
  16.2 159.5 %copy-start.1 = (f32[3,8192]{1,0:T(4,128)S(1)}, f32[3,8192]{1,0:T(4,128)}, u32[]{:S(2)}) copy-start(f32[3,8192]{1,0:T(4,128)} %param.14) | copy-start | bytes 294916
  16.2 160.1 %copy-start.5 = (f32[6,256]{1,0:T(8,128)S(1)}, f32[6,256]{1,0:T(8,128)}, u32[]{:S(2)}) copy-start(f32[6,256]{1,0:T(8,128)} %param.18) | copy-start | bytes 18436
  182.6 113.1 %all-to-all-start.1 = ((f32[128,2,3,128]{3,1,2,0:T(2,128)}), f32[128,2,3,128]{3,1,2,0:T(2,128)S(1)}, u32[]{:S(2)}, u32[]{:S(2)}) async-start(f32[128,2,3,128]{3,1,2,0:T(2,128)} %copy.137), calls=%async_computation.1 | async-start | bytes 786432 | tf_op jit(solution)/shard_map/all_to_all | solution.py:69
  188.5 107.3 %copy-start = (f32[8192]{0:T(1024)S(1)}, f32[8192]{0:T(1024)}, u32[]{:S(2)}) copy-start(f32[8192]{0:T(1024)} %param.15) | copy-start | bytes 98308
  687.0 233.9 %all-to-all-start.2 = ((f32[128,2,3,128]{3,1,2,0:T(2,128)}), f32[128,2,3,128]{3,1,2,0:T(2,128)}, u32[]{:S(2)}, u32[]{:S(2)}) async-start(f32[128,2,3,128]{3,1,2,0:T(2,128)} %copy.142), calls=%async_computation.2 | async-start | bytes 786432 | tf_op jit(solution)/shard_map/all_to_all | solution.py:94
  739.9 0.6 copy-start.2
  739.9 1.6 copy-start.3
  739.9 1.6 copy-start.4
  796.1 0.6 copy-start.2
  796.1 1.6 copy-start.3
  796.1 1.6 copy-start.4
  852.3 0.6 copy-start.2
  852.3 1.6 copy-start.3
  852.4 1.6 copy-start.4
  908.6 0.6 copy-start.2
  908.6 1.6 copy-start.3
  908.6 1.6 copy-start.4
where the time goes:
time: 928 us; the launch traced here: 925 us
  other arithmetic  475 us (51%)
  blocking collectives  266 us (29%)
  local copies, waits for them, and re-layouts  155 us (17%)
  starting transfers between devices  25.5 us (3%)
    div x20, other arithmetic, pair_pull(): factor = source_mass[:, None, :] / (spread * jnp.sqrt(spread))  192 us
    reduce_sum x20, other arithmetic, pair_pull(): spread = jnp.sum(delta * delta, axis=1) + soften_sq  135 us
    reduce_sum x20, other arithmetic, pair_pull(): return jnp.sum(delta * factor[:, None, :, :], axis=(0, 3))  128 us
    all_gather x1, blocking collectives, per_device(): lax.all_gather(node_quad, ('wide', 'narrow'), axis=1, tiled=True)  107 us
    all_gather x1, blocking collectives, per_device(): lax.all_gather(node_centre, ('wide', 'narrow'), axis=1, tiled=True)  107 us
    all_gather x1, blocking collectives, per_device(): lax.all_gather(node_mass, ('wide', 'narrow'), axis=0, tiled=True)  51.7 us
    gather x8, local copies, waits for them, and re-layouts, local_term(): all_quad[:, node_ids]  35.1 us
    gather x8, local copies, waits for them, and re-layouts, local_term(): all_centre[:, node_ids]  35.1 us
  transfers between devices with their start and end apart: 3, of which 0 were waited for; matrix products, arithmetic and copies ran while one was open for 25% of the time, Pallas kernels for 0%

commit v1 on v0

v1 whole, which is shorter than its diff:
```python
import functools

import jax
import jax.numpy as jnp
from jax import lax
from jax.experimental import pallas as pl
from jax.experimental.pallas import tpu as pltpu
from jax.sharding import PartitionSpec as P

ROWS = 128
LEAF_N = 8
LIST_N = 64
CAP = 2
BLK_DEV = 64
EXP_BLK = 128
AXES = ("wide", "narrow")
GROUP = 4
STEP = 8
NODE_FIELDS = 10
NODES_ROW = 12
SOFTEN = 0.01

f32 = jnp.float32
bf16 = jnp.bfloat16
VMEM = pl.BlockSpec(memory_space=pltpu.VMEM)
SMEM = pl.BlockSpec(memory_space=pltpu.SMEM)
ANY = pl.BlockSpec(memory_space=pl.ANY)


def params(mib):
    return pltpu.CompilerParams(vmem_limit_bytes=mib * 2**20)


def split3(value):
    high = value.astype(bf16)
    rest = value - high.astype(f32)
    middle = rest.astype(bf16)
    low = (rest - middle.astype(f32)).astype(bf16)
    return high, middle, low


def dot(left, right):
    return jnp.dot(left, right, preferred_element_type=f32)


def send_kernel(place_ref, block_ref, dest_ref, pos_ref, leaf_ref, out_ref, slot_ref, count_ref):
    devices = out_ref.shape[0]
    members = place_ref[0]
    out_ref[:, :, 3:4, :] = jnp.full((devices, CAP, 1, ROWS), -1.0, f32)

    def clear(index, carry):
        count_ref[index] = 0
        return carry

    lax.fori_loop(0, devices, clear, 0)

    def one(export, carry):
        dest = dest_ref[export]
        owner = ((dest // members) % 2) * 2 + dest % 2
        base = dest - ((dest // members) % 2) * members - dest % 2
        seen = count_ref[base]
        count_ref[base] = seen + 1
        member = (seen + place_ref[1]) % GROUP
        slot = seen // GROUP
        target = base + (member // 2) * members + member % 2
        distance = owner ^ member
        slot_ref[export] = target * CAP + slot
        start = pl.multiple_of(block_ref[export] * ROWS, ROWS)
        out_ref[target, slot, 0:3, :] = pos_ref[:, pl.ds(start, ROWS)]
        ids = leaf_ref[pl.ds(export, 1), :] + distance * BLK_DEV
        out_ref[target, slot, 3:4, 0:LEAF_N] = ids.astype(f32)
        return carry

    lax.fori_loop(0, EXP_BLK, one, 0)


def send_blocks(place, export_block, export_dest, positions, export_leaves, devices):
    return pl.pallas_call(
        send_kernel,
        out_shape=(
            jax.ShapeDtypeStruct((devices, CAP, 4, ROWS), f32),
            jax.ShapeDtypeStruct((EXP_BLK,), jnp.int32),
        ),
        in_specs=[SMEM, SMEM, SMEM, VMEM, VMEM],
        out_specs=(VMEM, SMEM),
        scratch_shapes=[pltpu.SMEM((devices,), jnp.int32)],
        compiler_params=params(16),
        name="send_blocks",
    )(place, export_block, export_dest, positions, export_leaves)


def centred_rows(position, centre):
    moved = position - centre
    square = jnp.sum(moved * moved, axis=0, keepdims=True)
    one = jnp.ones_like(square)
    return moved, square, one, jnp.zeros((3,) + square.shape[1:], f32)


def source_kernel(centre_ref, pm_ref, table_ref, weight_ref):
    count = table_ref.shape[0]
    for leaf in range(count):
        window = pm_ref[0, :, leaf * ROWS : (leaf + 1) * ROWS]
        moved, square, one, zero = centred_rows(window[0:3], centre_ref[...])
        row = jnp.concatenate([-2.0 * moved, one, square, zero], axis=0)
        high, middle, low = [part.astype(f32) for part in split3(row)]
        blank = jnp.zeros((16, ROWS), f32)
        half = [high, high, middle, middle, high, low, blank]
        table_ref[leaf] = jnp.concatenate(half + half, axis=0).T.astype(bf16)
        pulled = jnp.concatenate([moved, one, zero, zero[0:1]], axis=0) * window[3:4]
        high, middle, _ = split3(pulled)
        weight_ref[leaf] = jnp.concatenate([high, middle], axis=0)


def source_tables(centre, pm):
    groups = pm.shape[0]
    chunk = 8
    steps = BLK_DEV // chunk
    return pl.pallas_call(
        source_kernel,
        grid=(groups, steps),
        out_shape=(
            jax.ShapeDtypeStruct((groups * BLK_DEV, ROWS, 128), bf16),
            jax.ShapeDtypeStruct((groups * BLK_DEV, 16, ROWS), bf16),
        ),
        in_specs=[
            pl.BlockSpec((3, 1), lambda g, i: (0, 0)),
            pl.BlockSpec((1, 4, chunk * ROWS), lambda g, i: (g, 0, i)),
        ],
        out_specs=(
            pl.BlockSpec((chunk, ROWS, 128), lambda g, i: (g * steps + i, 0, 0)),
            pl.BlockSpec((chunk, 16, ROWS), lambda g, i: (g * steps + i, 0, 0)),
        ),
        compiler_params=params(16),
        name="source_tables",
    )(centre, pm)


def pull_block(position, centre, leaves, table_ref, weight_ref, left):
    moved, square, one, zero = centred_rows(position, centre)
    row = jnp.concatenate([moved, square + SOFTEN, one, zero], axis=0)
    high, middle, low = split3(row)
    blank = jnp.zeros((16, ROWS), bf16)
    half = jnp.concatenate([high, middle, high, middle, low, high, blank], axis=0)
    none = jnp.zeros_like(half)
    right = jnp.concatenate(
        [jnp.concatenate([half, none], axis=1), jnp.concatenate([none, half], axis=1)], axis=0
    )
    total = jnp.zeros((16, ROWS), f32)
    for pair in range(LEAF_N // 2):
        first, second = leaves[2 * pair], leaves[2 * pair + 1]
        spread = dot(jnp.where(left, table_ref[first], table_ref[second]), right)
        root = lax.rsqrt(spread)
        cubed = root * root * root
        high = cubed.astype(bf16)
        low = (cubed - high.astype(f32)).astype(bf16)
        for place, leaf in enumerate((first, second)):
            lanes = slice(place * ROWS, (place + 1) * ROWS)
            weight = weight_ref[leaf]
            total += dot(
                jnp.concatenate([weight, weight], axis=1),
                jnp.concatenate([high[:, lanes], low[:, lanes]], axis=0),
            )
    total = total[0:8] + total[8:16]
    return total[0:3] - moved * total[3:4]


def left_lanes():
    return lax.broadcasted_iota(jnp.int32, (ROWS, 128), 1) < 64


def local_kernel(leaf_ref, centre_ref, pos_ref, table_ref, weight_ref, out_ref):
    left = left_lanes()

    def step(index, carry):
        results = []
        for place in range(STEP):
            block = index * STEP + place
            start = pl.multiple_of(block * ROWS, ROWS)
            leaves = [leaf_ref[block * LEAF_N + k] for k in range(LEAF_N)]
            results.append(
                pull_block(
                    pos_ref[:, pl.ds(start, ROWS)], centre_ref[...], leaves, table_ref, weight_ref, left
                )
            )
        for place in range(STEP):
            out_ref[index * STEP + place, 0:3] = results[place]
        return carry

    lax.fori_loop(0, BLK_DEV // STEP, step, 0)


def local_pull(local_leaves, centre, positions, table, weight):
    return pl.pallas_call(
        local_kernel,
        out_shape=jax.ShapeDtypeStruct((BLK_DEV, 4, ROWS), f32),
        in_specs=[SMEM, VMEM, VMEM, VMEM, VMEM],
        out_specs=VMEM,
        compiler_params=params(24),
        cost_estimate=pl.CostEstimate(flops=16 * 10**9, bytes_accessed=10**6, transcendentals=8 * 10**6),
        name="local_pull",
    )(local_leaves, centre, positions, table, weight)


def remote_kernel(
    leaf_ref, centre_ref, pos_ref, own_ref, own_weight_ref, other_ref, other_weight_ref,
    out_ref, table_ref, weight_ref, list_ref, sems,
):
    copies = [
        pltpu.make_async_copy(own_ref, table_ref.at[pl.ds(0, BLK_DEV)], sems.at[0]),
        pltpu.make_async_copy(own_weight_ref, weight_ref.at[pl.ds(0, BLK_DEV)], sems.at[1]),
        pltpu.make_async_copy(other_ref, table_ref.at[pl.ds(BLK_DEV, (GROUP - 1) * BLK_DEV)], sems.at[2]),
        pltpu.make_async_copy(
            other_weight_ref, weight_ref.at[pl.ds(BLK_DEV, (GROUP - 1) * BLK_DEV)], sems.at[3]
        ),
    ]
    for copy in copies:
        copy.start()
    slots = pos_ref.shape[0]

    def note(slot, found):
        list_ref[found] = slot
        return found + (leaf_ref[slot * LEAF_N] >= 0).astype(jnp.int32)

    found = lax.fori_loop(0, slots, note, 0)
    last = list_ref[jnp.maximum(found - 1, 0)]
    for place in range(STEP):
        list_ref[found + place] = last
    for copy in copies:
        copy.wait()
    left = left_lanes()

    def step(index, carry):
        results = []
        for place in range(STEP):
            slot = list_ref[index * STEP + place]
            leaves = [leaf_ref[slot * LEAF_N + k] for k in range(LEAF_N)]
            results.append(
                (slot, pull_block(pos_ref[slot][0:3], centre_ref[...], leaves, table_ref, weight_ref, left))
            )
        for slot, result in results:
            out_ref[slot, 0:3] = result
        return carry

    lax.fori_loop(0, (found + STEP - 1) // STEP, step, 0)


def remote_pull(leaves, centre, visitors, own, own_weight, other, other_weight):
    slots = visitors.shape[0]
    return pl.pallas_call(
        remote_kernel,
        out_shape=jax.ShapeDtypeStruct((slots, 4, ROWS), f32),
        in_specs=[SMEM, VMEM, VMEM, ANY, ANY, ANY, ANY],
        out_specs=VMEM,
        scratch_shapes=[
            pltpu.VMEM((GROUP * BLK_DEV, ROWS, 128), bf16),
            pltpu.VMEM((GROUP * BLK_DEV, 16, ROWS), bf16),
            pltpu.SMEM((slots + STEP,), jnp.int32),
            pltpu.SemaphoreType.DMA((4,)),
        ],
        compiler_params=params(32),
        cost_estimate=pl.CostEstimate(flops=32 * 10**9, bytes_accessed=10**7, transcendentals=16 * 10**6),
        name="remote_pull",
    )(leaves, centre, visitors, own, own_weight, other, other_weight)


def node_kernel(row_ref, pos_ref, field_ref, table_ref, local_ref, out_ref, picked_ref):
    def step(block, carry):
        start = pl.multiple_of(block * ROWS, ROWS)
        place = pos_ref[:, pl.ds(start, ROWS)]
        for node in range(LIST_N):
            picked_ref[pl.ds(node, 1), :] = table_ref[pl.ds(row_ref[block * LIST_N + node], 1), :]
        column = jnp.full((LIST_N, 128), block, jnp.int32)
        base = jnp.take_along_axis(field_ref[...], column, axis=1, mode="promise_in_bounds")
        picked = picked_ref[...]

        def field(number):
            return jnp.take_along_axis(picked, base + number, axis=1, mode="promise_in_bounds")

        mass, cx, cy, cz = field(0), field(1), field(2), field(3)
        qxx, qyy, qzz, qxy, qxz, qyz = [field(number) for number in range(4, 10)]
        x, y, z = place[0:1] - cx, place[1:2] - cy, place[2:3] - cz
        spread = x * x + y * y + z * z + SOFTEN
        quad_x = qxx * x + qxy * y + qxz * z
        quad_y = qxy * x + qyy * y + qyz * z
        quad_z = qxz * x + qyz * y + qzz * z
        root = lax.rsqrt(spread)
        inverse = root * root
        cubed = inverse * root
        fifth = cubed * inverse
        scalar = x * quad_x + y * quad_y + z * quad_z
        radial = -mass * cubed - 2.5 * scalar * (fifth * inverse)
        total = [
            jnp.sum(radial * x + quad_x * fifth, axis=0, keepdims=True),
            jnp.sum(radial * y + quad_y * fifth, axis=0, keepdims=True),
            jnp.sum(radial * z + quad_z * fifth, axis=0, keepdims=True),
        ]
        out_ref[block, 0:3] = local_ref[block, 0:3] + jnp.concatenate(total, axis=0)
        return carry

    lax.fori_loop(0, BLK_DEV, step, 0)


def node_pull(rows, positions, fields, table, local):
    return pl.pallas_call(
        node_kernel,
        out_shape=jax.ShapeDtypeStruct(local.shape, f32),
        in_specs=[SMEM, VMEM, VMEM, VMEM, VMEM],
        out_specs=VMEM,
        scratch_shapes=[pltpu.VMEM((LIST_N, 128), f32)],
        compiler_params=params(24),
        cost_estimate=pl.CostEstimate(flops=4 * 10**9, bytes_accessed=2 * 10**6, transcendentals=10**6),
        name="node_pull",
    )(rows, positions, fields, table, local)


def add_kernel(slot_ref, block_ref, local_ref, back_ref, out_ref):
    for block in range(BLK_DEV):
        out_ref[:, block * ROWS : (block + 1) * ROWS] = local_ref[block, 0:3]

    def one(export, carry):
        start = pl.multiple_of(block_ref[export] * ROWS, ROWS)
        out_ref[:, pl.ds(start, ROWS)] += back_ref[slot_ref[export]][0:3]
        return carry

    lax.fori_loop(0, EXP_BLK, one, 0)


def add_returned(slots, export_block, local, back):
    return pl.pallas_call(
        add_kernel,
        out_shape=jax.ShapeDtypeStruct((3, BLK_DEV * ROWS), f32),
        in_specs=[SMEM, SMEM, VMEM, VMEM],
        out_specs=VMEM,
        compiler_params=params(16),
        name="add_returned",
    )(slots, export_block, local, back)


def swap(values):
    return lax.all_to_all(values, AXES, split_axis=0, concat_axis=0, tiled=True)


def node_table(node_mass, node_centre, node_quad, devices):
    count = node_mass.shape[0]
    rows = -(-count // NODES_ROW)
    padded = -(-rows // 8) * 8
    fields = jnp.concatenate([node_mass[None], node_centre, node_quad], axis=0).T
    fields = jnp.pad(fields, ((0, rows * NODES_ROW - count), (0, 0)))
    fields = fields.reshape(rows, NODES_ROW * NODE_FIELDS)
    fields = jnp.pad(fields, ((0, padded - rows), (0, 128 - NODES_ROW * NODE_FIELDS)))
    return swap(jnp.broadcast_to(fields[None], (devices, padded, 128))).reshape(devices * padded, 128)


def per_device(
    positions,
    masses,
    node_mass,
    node_centre,
    node_quad,
    local_leaves,
    node_lists,
    export_block,
    export_dest,
    export_leaves,
):
    groups = lax.axis_size("wide")
    members = lax.axis_size("narrow")
    devices = groups * members
    wide = lax.axis_index("wide")
    narrow = lax.axis_index("narrow")
    count = node_mass.shape[0]

    place = jnp.stack([jnp.int32(members), (wide // 2 + narrow // 2 + narrow).astype(jnp.int32)])
    outgoing, slots = send_blocks(
        place, export_block, export_dest[:, 0], positions, export_leaves, devices
    )
    arrived = swap(outgoing)

    pm = jnp.concatenate([positions, masses[None]], axis=0)
    centre = jnp.mean(positions, axis=1, keepdims=True)
    near = [(i, i ^ 1) for i in range(members)]
    pair = [(i, i ^ 1) for i in range(groups)]
    by_narrow = lax.ppermute(pm, "narrow", near)
    by_wide = lax.ppermute(pm, "wide", pair)
    by_both = lax.ppermute(by_narrow, "wide", pair)
    own, own_weight = source_tables(centre, pm[None])
    local = local_pull(local_leaves.reshape(-1), centre, positions, own, own_weight)
    other, other_weight = source_tables(centre, jnp.stack([by_narrow, by_wide, by_both]))
    table = node_table(node_mass, node_centre, node_quad, devices)

    visitors = arrived.reshape(devices * CAP, 4, ROWS)
    visitor_leaves = visitors[:, 3, 0:LEAF_N].astype(jnp.int32).reshape(-1)
    pulls = remote_pull(visitor_leaves, centre, visitors, own, own_weight, other, other_weight)
    back = swap(pulls.reshape(devices, CAP, 4, ROWS))

    inner = node_lists % count
    table_rows = table.shape[0] // devices
    rows = (node_lists // count) * table_rows + inner // NODES_ROW
    fields = jnp.pad((inner % NODES_ROW * NODE_FIELDS).T, ((0, 0), (0, 128 - BLK_DEV)))
    local = node_pull(rows.reshape(-1), positions, fields, table, local)
    return add_returned(slots, export_block, local, back.reshape(devices * CAP, 4, ROWS))


def solution(mesh):
    both = P(AXES)
    lanes = P(None, AXES)
    rows = P(AXES, None)
    return jax.shard_map(
        per_device,
        mesh=mesh,
        in_specs=(lanes, both, both, lanes, lanes, rows, rows, both, rows, rows),
        out_specs=lanes,
        check_vma=False,
    )
```

time: 928 us -> 145 us (0.16)
  other arithmetic: 475 us -> 3.83 us
  blocking collectives: 266 us -> 0 us
  local copies, waits for them, and re-layouts: 155 us -> 14.5 us
  Pallas kernels: 0 us -> 81.8 us
  starting transfers between devices: 25.5 us -> 45.2 us
    all_gather x3 -> x0, blocking collectives: 266 us -> none  [the longest x1 107 us: per_device(): lax.all_gather(node_quad, ('wide', 'narrow'), axis=1, tiled=True)]
    reduce_sum x45 -> x1, other arithmetic: 266 us -> 1.09 us  [per_device(): centre = jnp.mean(positions, axis=1, keepdims=True)]
    div x20 -> x1, other arithmetic: 192 us -> 0.01 us  [per_device(): centre = jnp.mean(positions, axis=1, keepdims=True)]
    gather x62 -> x0, local copies, waits for them, and re-layouts: 124 us -> none  [the longest x8 35.1 us: local_term(): all_quad[:, node_ids]]
    pallas_call x0 -> x7, Pallas kernels: none -> 81.8 us  [the longest x1 25.3 us: node_pull(): pl.pallas_call(node_kernel, out_shape=jax.ShapeDtypeStruct(local.shape, f...]
    all_to_all x3, starting transfers between devices: 25.5 us -> 41 us  [swap(): return lax.all_to_all(values, AXES, split_axis=0, concat_axis=0, tiled=True)]
    unnamed x18 -> x36, local copies, waits for them, and re-layouts: 2.5 us -> 12.6 us
  transfers between devices with their start and end apart: 3 -> 6, of which waited for: 0 -> 0; matrix products, arithmetic and copies ran while one was open for 25% -> 3% of each run, Pallas kernels for 0% -> 55%
where the time goes in v1:
time: 145 us; the launch traced here: 146 us
  Pallas kernels  81.8 us (56%)
  starting transfers between devices  45.2 us (31%)
  local copies, waits for them, and re-layouts  14.5 us (10%)
  other arithmetic  3.83 us (3%)
    all_to_all x3, starting transfers between devices, swap(): return lax.all_to_all(values, AXES, split_axis=0, concat_axis=0, tiled=True)  41 us
    pallas_call x1, Pallas kernels, node_pull(): pl.pallas_call(node_kernel, out_shape=jax.ShapeDtypeStruct(local.shape, f...  25.3 us
    pallas_call x1, Pallas kernels, remote_pull(): pl.pallas_call(remote_kernel, out_shape=jax.ShapeDtypeStruct((slots, 4, R...  24.5 us
    unnamed x36, local copies, waits for them, and re-layouts  12.6 us
    pallas_call x1, Pallas kernels, local_pull(): pl.pallas_call(local_kernel, out_shape=jax.ShapeDtypeStruct((BLK_DEV, 4,...  12.2 us
    pallas_call x2, Pallas kernels, source_tables(): pl.pallas_call(source_kernel, grid=(groups, steps), out_shape=(jax.ShapeD...  9.39 us
    pallas_call x1, Pallas kernels, send_blocks(): pl.pallas_call(send_kernel, out_shape=(jax.ShapeDtypeStruct((devices, CAP...  8.08 us
  transfers between devices with their start and end apart: 6, of which 0 were waited for; matrix products, arithmetic and copies ran while one was open for 3% of the time, Pallas kernels for 55%

profile of v1, /device:TPU:1, one launch (start us, length us, event | category | flops | bytes accessed | tf_op | source)
XLA Modules:
  0.0 145.6 jit_solution(5716223243692374766)
XLA Ops:
  0.0 1.0 pad_maximum_fusion.1
  1.0 2.1 %collective-permute-start = (f32[4,8192]{1,0:T(4,128)S(1)}, f32[4,8192]{1,0:T(4,128)S(1)}, u32[]{:S(2)}, u32[]{:S(2)}) collective-permute-start(f32[4,8192]{1,0:T(4,128)S(1)} %pad_maximum_fusion.1), channel_id=1, source_target_pairs={{0,1},{1,0},{2,3},{3,2},{4,5},{5,4},{6,7},{7,6},{8,9},{9,8},{10,11... | collective-permute-start | bytes 393224 | tf_op jit(solution)/shard_map/ppermute | solution.py:383
  3.2 1.0 collective-permute-start.1
  4.1 0.8 copy.20.leaf_ref
  4.9 0.1 pad_add_fusion.place_ref
  5.0 0.9 copy-done
  5.9 0.7 copy-done.2
  6.5 0.7 copy-done.4
  7.2 8.1 %send_blocks.1 = (f32[128,2,4,128]{3,2,1,0:T(4,128)}, s32[128]{0:T(128)S(1)}) custom-call(s32[2]{0:T(128)S(1)} %pad_add_fusion.place_ref, s32[128]{0:T(128)S(1)} %copy-done.2, s32[128]{0:T(128)S(1)} %bitcast.23, f32[3,8192]{1,0:T(4,128)S(1)} %copy-done, s32[128,8]{1,0:T(8,128)S(1)} %copy.20.leaf_ref), custom_call_target="tpu_custom_call" | custom-call | tf_op jit(solution)/shard_map/send_blocks/pallas_call | solution.py:78
  15.3 9.8 %all-to-all-start.1 = ((f32[128,2,4,128]{3,2,1,0:T(4,128)}), f32[128,2,4,128]{3,2,1,0:T(4,128)S(1)}, u32[]{:S(2)}, u32[]{:S(2)}) async-start(f32[128,2,4,128]{3,2,1,0:T(4,128)} %get-tuple-element.14), calls=%async_computation.1 | async-start | bytes 1048576 | tf_op jit(solution)/shard_map/all_to_all | solution.py:340
  25.1 1.0 fusion.7.pm_ref
  26.1 1.1 reduce_sum.9
  27.2 0.1 copy.29.centre_ref
  27.3 0.1 copy.27
  27.4 0.1 reshape.38.leaf_ref
  27.5 2.4 %source_tables.2 = (bf16[64,128,128]{2,1,0:T(8,128)(2,1)S(1)}, bf16[64,16,128]{2,1,0:T(8,128)(2,1)S(1)}) custom-call(f32[3,1]{1,0:T(4,128)S(1)} %copy.29.centre_ref, f32[1,4,8192]{2,1,0:T(4,128)S(1)} %fusion.7.pm_ref), custom_call_target="tpu_custom_call" | custom-call | tf_op jit(solution)/shard_map/source_tables/pallas_call | solution.py:118
  29.8 0.0 collective-permute-done
  29.9 1.1 collective-permute-start.2
  31.0 0.0 copy-start.15
  31.0 12.2 %local_pull.1.local_ref = f32[64,4,128]{2,1,0:T(4,128)S(1)} custom-call(s32[512]{0:T(512)S(1)} %reshape.38.leaf_ref, f32[3,1]{1,0:T(4,128)S(1)} %copy.29.centre_ref, f32[3,8192]{1,0:T(4,128)S(1)} %copy-done.1, bf16[64,128,128]{2,1,0:T(8,128)(2,1)S(1)} %get-tuple-element.12.table_ref.own_ref, bf16[64,16,128]{2,1,0:T(8,128)(2,1)S(1)} %get-tuple-element.13.weight_ref.own_weight_ref), custom_call_target="tpu_custom_call" | custom-call | flops 16000000000 | bytes 1000000 | tf_op jit(solution)/shard_map/local_pull/pallas_call | solution.py:193
  43.3 0.0 copy-start.7
  43.3 1.4 copy-done.7
  44.7 0.1 copy.21
  44.8 0.1 copy.32
  44.9 0.1 reshape.36
  45.0 0.0 collective-permute-done.1
  45.0 0.0 collective-permute-done.2
  45.1 0.1 pad_maximum_fusion.pm_ref
  45.2 7.0 %source_tables.3 = (bf16[192,128,128]{2,1,0:T(8,128)(2,1)S(1)}, bf16[192,16,128]{2,1,0:T(8,128)(2,1)S(1)}) custom-call(f32[3,1]{1,0:T(4,128)S(1)} %copy.29.centre_ref, f32[3,4,8192]{2,1,0:T(4,128)S(1)} %pad_maximum_fusion.pm_ref), custom_call_target="tpu_custom_call" | custom-call | tf_op jit(solution)/shard_map/source_tables/pallas_call | solution.py:118
  52.2 2.6 %copy-done.5 = bf16[192,128,128]{2,1,0:T(8,128)(2,1)} copy-done((bf16[192,128,128]{2,1,0:T(8,128)(2,1)}, bf16[192,128,128]{2,1,0:T(8,128)(2,1)S(1)}, u32[]{:S(2)}) %copy-start.5) | copy-done | bytes 6291480
  54.9 0.0 all-to-all-done.1
  54.9 1.3 broadcast_in_dim.17
  56.2 8.9 %all-to-all-start = ((f32[128,24,128]{2,1,0:T(8,128)}), f32[128,24,128]{2,1,0:T(8,128)S(1)}, u32[]{:S(2)}, u32[]{:S(2)}) async-start(f32[128,24,128]{2,1,0:T(8,128)} %broadcast_in_dim.17), calls=%async_computation | async-start | bytes 3145728 | tf_op jit(solution)/shard_map/all_to_all | solution.py:340
  65.0 0.5 fusion
  65.5 0.1 convert_element_type.12.leaf_ref
  65.6 2.8 %copy-done.6 = bf16[192,128,128]{2,1,0:T(8,128)(2,1)S(1)} copy-done((bf16[192,128,128]{2,1,0:T(8,128)(2,1)S(1)}, bf16[192,128,128]{2,1,0:T(8,128)(2,1)}, u32[]{:S(2)}) %copy-start.6) | copy-done | bytes 6291480
  68.4 1.6 %copy-done.8 = bf16[64,128,128]{2,1,0:T(8,128)(2,1)S(1)} copy-done((bf16[64,128,128]{2,1,0:T(8,128)(2,1)S(1)}, bf16[64,128,128]{2,1,0:T(8,128)(2,1)}, u32[]{:S(2)}) %copy-start.8) | copy-done | bytes 2097176
  70.0 24.5 %remote_pull.1 = f32[256,4,128]{2,1,0:T(4,128)} custom-call(s32[2048]{0:T(1024)S(1)} %convert_element_type.12.leaf_ref, f32[3,1]{1,0:T(4,128)S(1)} %copy.29.centre_ref, f32[256,4,128]{2,1,0:T(4,128)S(1)} %bitcast.22, bf16[64,128,128]{2,1,0:T(8,128)(2,1)S(1)} %copy-done.8, bf16[64,16,128]{2,1,0:T(8,128)(2,1)S(1)} %get-tuple-element.13.weight_ref.own_weight_ref, ...), custom_call_target="tpu_custom_call" | custom-call | flops 32000000000 | bytes 10000000 | tf_op jit(solution)/shard_map/remote_pull/pallas_call | solution.py:249
  94.5 0.0 all-to-all-done
  94.5 22.3 %all-to-all-start.2 = ((f32[128,2,4,128]{3,2,1,0:T(4,128)}), f32[128,2,4,128]{3,2,1,0:T(4,128)S(1)}, u32[]{:S(2)}, u32[]{:S(2)}) async-start(f32[128,2,4,128]{3,2,1,0:T(4,128)} %bitcast.13), calls=%async_computation.2 | async-start | bytes 1048576 | tf_op jit(solution)/shard_map/all_to_all | solution.py:340
  116.8 0.1 fusion.4
  116.9 0.1 copy.25
  116.9 0.1 reshape.35.row_ref
  117.0 0.0 copy-start.10
  117.0 0.9 copy-done.10
  117.9 25.3 %node_pull.1.local_ref = f32[64,4,128]{2,1,0:T(4,128)S(1)} custom-call(s32[4096]{0:T(1024)S(1)} %reshape.35.row_ref, f32[3,8192]{1,0:T(4,128)S(1)} %copy-done.1, s32[64,128]{1,0:T(8,128)S(1)} %pad.12.field_ref, f32[3072,128]{1,0:T(8,128)S(1)} %bitcast.20, f32[64,4,128]{2,1,0:T(4,128)S(1)} %copy-done.10), custom_call_target="tpu_custom_call" | custom-call | flops 4000000000 | bytes 2000000 | tf_op jit(solution)/shard_map/node_pull/pallas_call | solution.py:304
  143.3 0.0 all-to-all-done.2
  143.3 2.3 %add_returned.1 = f32[3,8192]{1,0:T(4,128)} custom-call(s32[128]{0:T(128)S(1)} %get-tuple-element.11.slot_ref, s32[128]{0:T(128)S(1)} %copy-done.3, f32[64,4,128]{2,1,0:T(4,128)S(1)} %node_pull.1.local_ref, f32[256,4,128]{2,1,0:T(4,128)S(1)} %bitcast.19), custom_call_target="tpu_custom_call" | custom-call | tf_op jit(solution)/shard_map/add_returned/pallas_call | solution.py:329
  (26 shorter events, 0.1 us)
Async XLA Ops:
  0.0 31.0 %copy-start.1 = (f32[3,8192]{1,0:T(4,128)S(1)}, f32[3,8192]{1,0:T(4,128)}, u32[]{:S(2)}) copy-start(f32[3,8192]{1,0:T(4,128)} %pos_ref.5) | copy-start | bytes 294916
  0.0 27.3 %copy-start.13 = (s32[64,8]{0,1:T(8,128)S(1)}, s32[64,8]{0,1:T(8,128)}, u32[]{:S(2)}) copy-start(s32[64,8]{0,1:T(8,128)} %param.15) | copy-start | bytes 6148
  1.0 28.8 %collective-permute-start = (f32[4,8192]{1,0:T(4,128)S(1)}, f32[4,8192]{1,0:T(4,128)S(1)}, u32[]{:S(2)}, u32[]{:S(2)}) collective-permute-start(f32[4,8192]{1,0:T(4,128)S(1)} %pad_maximum_fusion.1), channel_id=1, source_target_pairs={{0,1},{1,0},{2,3},{3,2},{4,5},{5,4},{6,7},{7,6},{8,9},{9,8},{10,11... | collective-permute-start | bytes 393224 | tf_op jit(solution)/shard_map/ppermute | solution.py:383
  3.2 41.9 %collective-permute-start.1 = (f32[4,8192]{1,0:T(4,128)S(1)}, f32[4,8192]{1,0:T(4,128)S(1)}, u32[]{:S(2)}, u32[]{:S(2)}) collective-permute-start(f32[4,8192]{1,0:T(4,128)S(1)} %pad_maximum_fusion.1), channel_id=1, source_target_pairs={{0,16},{16,0},{32,48},{48,32},{64,80},{80,64},{96,112},{112,96},{1... | collective-permute-start | bytes 393224 | tf_op jit(solution)/shard_map/ppermute | solution.py:384
  5.0 0.9 copy-start
  5.9 0.7 copy-start.2
  6.5 0.7 copy-start.4
  15.3 39.6 %all-to-all-start.1 = ((f32[128,2,4,128]{3,2,1,0:T(4,128)}), f32[128,2,4,128]{3,2,1,0:T(4,128)S(1)}, u32[]{:S(2)}, u32[]{:S(2)}) async-start(f32[128,2,4,128]{3,2,1,0:T(4,128)} %get-tuple-element.14), calls=%async_computation.1 | async-start | bytes 1048576 | tf_op jit(solution)/shard_map/all_to_all | solution.py:340
  29.9 15.2 %collective-permute-start.2 = (f32[4,8192]{1,0:T(4,128)S(1)}, f32[4,8192]{1,0:T(4,128)S(1)}, u32[]{:S(2)}, u32[]{:S(2)}) collective-permute-start(f32[4,8192]{1,0:T(4,128)S(1)} %collective-permute-done), channel_id=1, source_target_pairs={{0,16},{16,0},{32,48},{48,32},{64,80},{80,64},{96,112},{112,96},{1... | collective-permute-start | bytes 393224 | tf_op jit(solution)/shard_map/ppermute | solution.py:385
  31.0 13.7 %copy-start.11 = (s32[64,64]{1,0:T(8,128)S(1)}, s32[64,64]{1,0:T(8,128)}, u32[]{:S(2)}) copy-start(s32[64,64]{1,0:T(8,128)} %param.16) | copy-start | bytes 49156
  31.0 13.7 %copy-start.12 = (f32[6,256]{1,0:T(8,128)S(1)}, f32[6,256]{1,0:T(8,128)}, u32[]{:S(2)}) copy-start(f32[6,256]{1,0:T(8,128)} %param.14) | copy-start | bytes 18436
  31.0 13.7 %copy-start.14 = (f32[3,256]{1,0:T(4,128)S(1)}, f32[3,256]{1,0:T(4,128)}, u32[]{:S(2)}) copy-start(f32[3,256]{1,0:T(4,128)} %param.13) | copy-start | bytes 9220
  31.0 13.7 %copy-start.15 = (f32[256]{0:T(256)S(1)}, f32[256]{0:T(256)}, u32[]{:S(2)}) copy-start(f32[256]{0:T(256)} %param.12) | copy-start | bytes 3076
  43.3 1.4 copy-start.7
  44.7 11.5 %copy-start.9 = (f32[64,4,128]{2,1,0:T(4,128)}, f32[64,4,128]{2,1,0:T(4,128)S(1)}, u32[]{:S(2)}) copy-start(f32[64,4,128]{2,1,0:T(4,128)S(1)} %local_pull.1.local_ref) | copy-start | bytes 393220
  52.2 2.7 %copy-start.5 = (bf16[192,128,128]{2,1,0:T(8,128)(2,1)}, bf16[192,128,128]{2,1,0:T(8,128)(2,1)S(1)}, u32[]{:S(2)}) copy-start(bf16[192,128,128]{2,1,0:T(8,128)(2,1)S(1)} %get-tuple-element.15.other_ref) | copy-start | bytes 18874372
  56.2 38.3 %all-to-all-start = ((f32[128,24,128]{2,1,0:T(8,128)}), f32[128,24,128]{2,1,0:T(8,128)S(1)}, u32[]{:S(2)}, u32[]{:S(2)}) async-start(f32[128,24,128]{2,1,0:T(8,128)} %broadcast_in_dim.17), calls=%async_computation | async-start | bytes 3145728 | tf_op jit(solution)/shard_map/all_to_all | solution.py:340
  65.6 2.8 %copy-start.6 = (bf16[192,128,128]{2,1,0:T(8,128)(2,1)S(1)}, bf16[192,128,128]{2,1,0:T(8,128)(2,1)}, u32[]{:S(2)}) copy-start(bf16[192,128,128]{2,1,0:T(8,128)(2,1)} %copy-done.5) | copy-start | bytes 18874372
  68.4 1.6 %copy-start.8 = (bf16[64,128,128]{2,1,0:T(8,128)(2,1)S(1)}, bf16[64,128,128]{2,1,0:T(8,128)(2,1)}, u32[]{:S(2)}) copy-start(bf16[64,128,128]{2,1,0:T(8,128)(2,1)} %copy-done.7) | copy-start | bytes 6291460
  94.5 48.8 %all-to-all-start.2 = ((f32[128,2,4,128]{3,2,1,0:T(4,128)}), f32[128,2,4,128]{3,2,1,0:T(4,128)S(1)}, u32[]{:S(2)}, u32[]{:S(2)}) async-start(f32[128,2,4,128]{3,2,1,0:T(4,128)} %bitcast.13), calls=%async_computation.2 | async-start | bytes 1048576 | tf_op jit(solution)/shard_map/all_to_all | solution.py:340
  117.0 0.9 copy-start.10
  117.9 25.3 %copy-start.3 = (s32[128]{0:T(128)S(1)}, s32[128]{0:T(128)}, u32[]{:S(2)}) copy-start(s32[128]{0:T(128)} %block_ref.3) | copy-start | bytes 1540

commit v2 on v1

v2 whole, which is shorter than its diff:
```python
import functools

import jax
import jax.numpy as jnp
from jax import lax
from jax.experimental import pallas as pl
from jax.experimental.pallas import tpu as pltpu
from jax.sharding import PartitionSpec as P

ROWS = 128
LEAF_N = 8
LIST_N = 64
CAP = 2
BLK_DEV = 64
EXP_BLK = 128
AXES = ("wide", "narrow")
GROUP = 4
STEP = 8
NODE_FIELDS = 10
SOFTEN = 0.01

f32 = jnp.float32
bf16 = jnp.bfloat16
VMEM = pl.BlockSpec(memory_space=pltpu.VMEM)
SMEM = pl.BlockSpec(memory_space=pltpu.SMEM)


def params(mib):
    return pltpu.CompilerParams(vmem_limit_bytes=mib * 2**20)


def split3(value):
    high = value.astype(bf16)
    rest = value - high.astype(f32)
    middle = rest.astype(bf16)
    low = (rest - middle.astype(f32)).astype(bf16)
    return high, middle, low


def dot(left, right):
    return jnp.dot(left, right, preferred_element_type=f32)


def send_kernel(place_ref, block_ref, dest_ref, leaf_ref, pos_ref, mass_ref, out_ref, slot_ref, pm_ref, count_ref, ids_ref):
    devices = out_ref.shape[0]
    members, shift, turn = place_ref[0], place_ref[1], place_ref[2]
    pm_ref[0:3] = pos_ref[...]
    pm_ref[3:4] = mass_ref[...]
    out_ref[:, :, 3:4, :] = jnp.full((devices, CAP, 1, ROWS), -1.0, f32)
    ids_ref[...] = jnp.concatenate([leaf_ref[...].astype(f32)] * (ROWS // LEAF_N), axis=0).T

    def clear(index, carry):
        for part in range(8):
            count_ref[index * 8 + part] = 0
        return carry

    lax.fori_loop(0, devices // 8, clear, 0)

    def one(step, carry):
        for part in range(8):
            export = step * 8 + part
            dest = dest_ref[export]
            side, across = dest & 1, (dest >> shift) & 1
            base = dest - side - across * members
            seen = count_ref[base]
            count_ref[base] = seen + 1
            member = (seen + turn) & (GROUP - 1)
            slot = seen >> 2
            target = base + (member >> 1) * members + (member & 1)
            distance = (across * 2 + side) ^ member
            slot_ref[export] = target * CAP + slot
            start = pl.multiple_of(block_ref[export] * ROWS, ROWS)
            out_ref[target, slot, 0:3, :] = pos_ref[:, pl.ds(start, ROWS)]
            ids = ids_ref[pl.ds(export, 1), 0:LEAF_N]
            out_ref[target, slot, 3:4, 0:LEAF_N] = ids + (distance * BLK_DEV).astype(f32)
        return carry

    lax.fori_loop(0, EXP_BLK // 8, one, 0)


def send_blocks(place, export_block, export_dest, export_leaves, positions, masses, devices):
    return pl.pallas_call(
        send_kernel,
        out_shape=(
            jax.ShapeDtypeStruct((devices, CAP, 4, ROWS), f32),
            jax.ShapeDtypeStruct((EXP_BLK,), jnp.int32),
            jax.ShapeDtypeStruct((4, BLK_DEV * ROWS), f32),
        ),
        in_specs=[SMEM, SMEM, SMEM, VMEM, VMEM, VMEM],
        out_specs=(VMEM, SMEM, VMEM),
        scratch_shapes=[pltpu.SMEM((devices,), jnp.int32), pltpu.VMEM((EXP_BLK, 128), f32)],
        compiler_params=params(16),
        name="send_blocks",
    )(place, export_block, export_dest, export_leaves, positions, masses)


def node_rows_kernel(mass_ref, centre_ref, quad_ref, list_ref, out_ref, row_ref, lane_ref):
    devices, rows = out_ref.shape[0], out_ref.shape[1]
    count = mass_ref.shape[1]
    fields = jnp.concatenate(
        [mass_ref[...], centre_ref[...], quad_ref[...], jnp.zeros((16 - NODE_FIELDS, count), f32)], axis=0
    )
    parts = [fields[:, part * rows : (part + 1) * rows] for part in range(8)]
    table = jnp.concatenate(parts, axis=0).T
    out_ref[...] = jnp.broadcast_to(table[None], out_ref.shape)
    nodes = list_ref[...]
    bits = rows.bit_length() - 1
    row_ref[...] = ((nodes >> (bits + 3)) << bits) + (nodes & (rows - 1))
    lanes = ((nodes >> bits) & 7) * 16
    wide = jnp.concatenate([lanes, jnp.zeros_like(lanes)], axis=1)
    wide = jnp.concatenate([wide, jnp.zeros_like(wide)], axis=0)
    lane_ref[...] = wide.T[0:LIST_N]


def node_rows(node_mass, node_centre, node_quad, node_lists, devices):
    count = node_mass.shape[1]
    return pl.pallas_call(
        node_rows_kernel,
        out_shape=(
            jax.ShapeDtypeStruct((devices, count // 8, 128), f32),
            jax.ShapeDtypeStruct((BLK_DEV, LIST_N), jnp.int32),
            jax.ShapeDtypeStruct((LIST_N, 128), jnp.int32),
        ),
        in_specs=[VMEM] * 4,
        out_specs=(VMEM,) * 3,
        compiler_params=params(16),
        name="node_rows",
    )(node_mass, node_centre, node_quad, node_lists)


def centred_rows(position, centre):
    moved = position - centre
    square = jnp.sum(moved * moved, axis=0, keepdims=True)
    one = jnp.ones_like(square)
    return moved, square, one, jnp.zeros((3,) + square.shape[1:], f32)


def source_kernel(pm0_ref, pm1_ref, pm2_ref, pm3_ref, table_ref, weight_ref, centre_ref):
    size = BLK_DEV * ROWS
    centre = jnp.sum(pm0_ref[0:3], axis=1, keepdims=True) * (1.0 / size)
    centre_ref[...] = jnp.broadcast_to(centre, (3, ROWS))
    chunk = 8

    def step(index, carry):
        start = pl.multiple_of(index * (chunk * ROWS), chunk * ROWS)
        for group, pm_ref in enumerate((pm0_ref, pm1_ref, pm2_ref, pm3_ref)):
            rows = pm_ref[:, pl.ds(start, chunk * ROWS)]
            for part in range(chunk):
                window = rows[:, part * ROWS : (part + 1) * ROWS]
                leaf = group * BLK_DEV + index * chunk + part
                moved, square, one, zero = centred_rows(window[0:3], centre)
                row = jnp.concatenate([-2.0 * moved, one, square, zero], axis=0)
                high, middle, low = [piece.astype(f32) for piece in split3(row)]
                blank = jnp.zeros((16, ROWS), f32)
                half = [high, high, middle, middle, high, low, blank]
                table_ref[leaf] = jnp.concatenate(half + half, axis=0).T.astype(bf16)
                pulled = jnp.concatenate([moved, one, zero, zero[0:1]], axis=0) * window[3:4]
                high, middle, _ = split3(pulled)
                weight_ref[leaf] = jnp.concatenate([high, middle], axis=0)
        return carry

    lax.fori_loop(0, BLK_DEV // chunk, step, 0)


def source_tables(pms):
    return pl.pallas_call(
        source_kernel,
        out_shape=(
            jax.ShapeDtypeStruct((GROUP * BLK_DEV, ROWS, 128), bf16),
            jax.ShapeDtypeStruct((GROUP * BLK_DEV, 16, ROWS), bf16),
            jax.ShapeDtypeStruct((3, ROWS), f32),
        ),
        in_specs=[VMEM] * 4,
        out_specs=(VMEM,) * 3,
        compiler_params=params(32),
        name="source_tables",
    )(*pms)


def pull_block(position, centre, leaves, table_ref, weight_ref, left):
    moved, square, one, zero = centred_rows(position, centre)
    row = jnp.concatenate([moved, square + SOFTEN, one, zero], axis=0)
    high, middle, low = split3(row)
    blank = jnp.zeros((16, ROWS), bf16)
    half = jnp.concatenate([high, middle, high, middle, low, high, blank], axis=0)
    none = jnp.zeros_like(half)
    right = jnp.concatenate(
        [jnp.concatenate([half, none], axis=1), jnp.concatenate([none, half], axis=1)], axis=0
    )
    total = jnp.zeros((16, ROWS), f32)
    for pair in range(LEAF_N // 2):
        first, second = leaves[2 * pair], leaves[2 * pair + 1]
        spread = dot(jnp.where(left, table_ref[first], table_ref[second]), right)
        root = lax.rsqrt(spread)
        cubed = root * root * root
        high = cubed.astype(bf16)
        low = (cubed - high.astype(f32)).astype(bf16)
        for place, leaf in enumerate((first, second)):
            lanes = slice(place * ROWS, (place + 1) * ROWS)
            weight = weight_ref[leaf]
            total += dot(
                jnp.concatenate([weight, weight], axis=1),
                jnp.concatenate([high[:, lanes], low[:, lanes]], axis=0),
            )
    total = total[0:8] + total[8:16]
    return total[0:3] - moved * total[3:4]


def left_lanes():
    return lax.broadcasted_iota(jnp.int32, (ROWS, 128), 1) < 64


def local_kernel(leaf_ref, centre_ref, pos_ref, table_ref, weight_ref, out_ref):
    left = left_lanes()

    def step(index, carry):
        results = []
        for place in range(STEP):
            block = index * STEP + place
            start = pl.multiple_of(block * ROWS, ROWS)
            leaves = [leaf_ref[k, block] for k in range(LEAF_N)]
            results.append(
                pull_block(
                    pos_ref[:, pl.ds(start, ROWS)], centre_ref[...], leaves, table_ref, weight_ref, left
                )
            )
        for place in range(STEP):
            out_ref[index * STEP + place, 0:3] = results[place]
        return carry

    lax.fori_loop(0, BLK_DEV // STEP, step, 0)


def local_pull(local_leaves, centre, positions, table, weight):
    return pl.pallas_call(
        local_kernel,
        out_shape=jax.ShapeDtypeStruct((BLK_DEV, 4, ROWS), f32),
        in_specs=[SMEM, VMEM, VMEM, VMEM, VMEM],
        out_specs=VMEM,
        compiler_params=params(32),
        cost_estimate=pl.CostEstimate(flops=16 * 10**9, bytes_accessed=10**6, transcendentals=8 * 10**6),
        name="local_pull",
    )(local_leaves, centre, positions, table, weight)


def remote_kernel(leaf_ref, centre_ref, pos_ref, table_ref, weight_ref, out_ref, list_ref):
    slots = pos_ref.shape[0]

    def note(slot, found):
        list_ref[found] = slot
        return found + (leaf_ref[slot * LEAF_N] >= 0).astype(jnp.int32)

    found = lax.fori_loop(0, slots, note, 0)
    last = list_ref[jnp.maximum(found - 1, 0)]
    for place in range(STEP):
        list_ref[found + place] = last
    left = left_lanes()

    def step(index, carry):
        results = []
        for place in range(STEP):
            slot = list_ref[index * STEP + place]
            leaves = [leaf_ref[slot * LEAF_N + k] for k in range(LEAF_N)]
            results.append(
                (slot, pull_block(pos_ref[slot][0:3], centre_ref[...], leaves, table_ref, weight_ref, left))
            )
        for slot, result in results:
            out_ref[slot, 0:3] = result
        return carry

    lax.fori_loop(0, (found + STEP - 1) // STEP, step, 0)


def remote_pull(leaves, centre, visitors, table, weight):
    slots = visitors.shape[0]
    return pl.pallas_call(
        remote_kernel,
        out_shape=jax.ShapeDtypeStruct((slots, 4, ROWS), f32),
        in_specs=[SMEM, VMEM, VMEM, VMEM, VMEM],
        out_specs=VMEM,
        scratch_shapes=[pltpu.SMEM((slots + STEP,), jnp.int32)],
        compiler_params=params(32),
        cost_estimate=pl.CostEstimate(flops=32 * 10**9, bytes_accessed=10**7, transcendentals=16 * 10**6),
        name="remote_pull",
    )(leaves, centre, visitors, table, weight)


def pick_lanes(values, lanes):
    numbers = lax.GatherDimensionNumbers(
        offset_dims=(),
        collapsed_slice_dims=(1,),
        start_index_map=(1,),
        operand_batching_dims=(0,),
        start_indices_batching_dims=(0,),
    )
    return lax.gather(
        values, lanes[..., None], numbers, (1, 1), mode=lax.GatherScatterMode.PROMISE_IN_BOUNDS
    )


def node_sum(place, fields):
    mass, cx, cy, cz, qxx, qyy, qzz, qxy, qxz, qyz = fields
    x, y, z = place[0:1] - cx, place[1:2] - cy, place[2:3] - cz
    spread = x * x + y * y + z * z + SOFTEN
    quad_x = qxx * x + qxy * y + qxz * z
    quad_y = qxy * x + qyy * y + qyz * z
    quad_z = qxz * x + qyz * y + qzz * z
    root = lax.rsqrt(spread)
    inverse = root * root
    cubed = inverse * root
    fifth = cubed * inverse
    scalar = x * quad_x + y * quad_y + z * quad_z
    radial = -mass * cubed - 2.5 * scalar * (fifth * inverse)
    total = [
        jnp.sum(radial * along + quad * fifth, axis=0, keepdims=True)
        for along, quad in ((x, quad_x), (y, quad_y), (z, quad_z))
    ]
    return jnp.concatenate(total, axis=0)


NODE_STEP = 4


def node_kernel(row_ref, pos_ref, lane_ref, table_ref, out_ref, *picked_refs):
    shape = (LIST_N, 128)
    along = lax.broadcasted_iota(jnp.int32, shape, 1)

    def step(index, carry):
        for part in range(NODE_STEP):
            for node in range(LIST_N):
                row = row_ref[index * NODE_STEP + part, node]
                picked_refs[part][pl.ds(node, 1), :] = table_ref[pl.ds(row, 1), :]
        results = []
        for part in range(NODE_STEP):
            block = index * NODE_STEP + part
            start = pl.multiple_of(block * ROWS, ROWS)
            first = pick_lanes(lane_ref[...], jnp.full(shape, block, jnp.int32))
            picked = pick_lanes(picked_refs[part][...], (first + along) & 127)
            fields = [jnp.broadcast_to(picked[:, k : k + 1], shape) for k in range(NODE_FIELDS)]
            results.append(node_sum(pos_ref[:, pl.ds(start, ROWS)], fields))
        for part in range(NODE_STEP):
            out_ref[index * NODE_STEP + part, 0:3] = results[part]
        return carry

    lax.fori_loop(0, BLK_DEV // NODE_STEP, step, 0)


def node_pull(rows, positions, lanes, table):
    return pl.pallas_call(
        node_kernel,
        out_shape=jax.ShapeDtypeStruct((BLK_DEV, 4, ROWS), f32),
        in_specs=[SMEM, VMEM, VMEM, VMEM],
        out_specs=VMEM,
        scratch_shapes=[pltpu.VMEM((LIST_N, 128), f32)] * NODE_STEP,
        compiler_params=params(24),
        cost_estimate=pl.CostEstimate(flops=4 * 10**9, bytes_accessed=2 * 10**6, transcendentals=10**6),
        name="node_pull",
    )(rows, positions, lanes, table)


def add_kernel(slot_ref, block_ref, local_ref, node_ref, back_ref, out_ref, *sum_refs):
    parts = len(sum_refs)
    for part in range(1, parts):
        sum_refs[part][...] = jnp.zeros_like(sum_refs[part])
    sum_refs[0][...] = local_ref[...] + node_ref[...]

    def one(step, carry):
        for part in range(parts):
            export = step * parts + part
            block = block_ref[export]
            sum_refs[part][block] += back_ref[slot_ref[export]]
        return carry

    lax.fori_loop(0, EXP_BLK // parts, one, 0)
    for block in range(BLK_DEV):
        total = sum_refs[0][block]
        for part in range(1, parts):
            total = total + sum_refs[part][block]
        out_ref[:, block * ROWS : (block + 1) * ROWS] = total[0:3]


def add_returned(slots, export_block, local, node, back):
    return pl.pallas_call(
        add_kernel,
        out_shape=jax.ShapeDtypeStruct((3, BLK_DEV * ROWS), f32),
        in_specs=[SMEM, SMEM, VMEM, VMEM, VMEM],
        out_specs=VMEM,
        scratch_shapes=[pltpu.VMEM((BLK_DEV, 4, ROWS), f32)] * 4,
        compiler_params=params(16),
        name="add_returned",
    )(slots, export_block, local, node, back)


def swap(values):
    return lax.all_to_all(values, AXES, split_axis=0, concat_axis=0, tiled=True)


def per_device(
    positions,
    masses,
    node_mass,
    node_centre,
    node_quad,
    local_leaves,
    node_lists,
    export_block,
    export_dest,
    export_leaves,
):
    groups = lax.axis_size("wide")
    members = lax.axis_size("narrow")
    devices = groups * members
    wide = lax.axis_index("wide")
    narrow = lax.axis_index("narrow")

    place = jnp.stack(
        [
            jnp.int32(members),
            jnp.int32(members.bit_length() - 1),
            (wide + narrow + (narrow >> 1)).astype(jnp.int32),
        ]
    )
    outgoing, slots, pm = send_blocks(
        place, export_block, export_dest[:, 0], export_leaves.T, positions, masses[None], devices
    )
    arrived = swap(outgoing)

    near = [(i, i ^ 1) for i in range(members)]
    pair = [(i, i ^ 1) for i in range(groups)]
    by_narrow = lax.ppermute(pm, "narrow", near)
    by_wide = lax.ppermute(pm, "wide", pair)
    by_both = lax.ppermute(by_narrow, "wide", pair)
    fields, rows, lanes = node_rows(node_mass[None], node_centre, node_quad, node_lists, devices)
    table = swap(fields).reshape(-1, 128)

    sources, weights, centre = source_tables((pm, by_narrow, by_wide, by_both))
    visitors = arrived.reshape(devices * CAP, 4, ROWS)
    visitor_leaves = visitors[:, 3, 0:LEAF_N].astype(jnp.int32).reshape(-1)
    pulls = remote_pull(visitor_leaves, centre, visitors, sources, weights)
    pulls, leaves = lax.optimization_barrier((pulls, local_leaves.T))
    back = swap(pulls.reshape(devices, CAP, 4, ROWS))
    local = local_pull(leaves, centre, positions, sources, weights)
    node = node_pull(rows, positions, lanes, table)
    return add_returned(slots, export_block, local, node, back.reshape(devices * CAP, 4, ROWS))


def solution(mesh):
    both = P(AXES)
    lanes = P(None, AXES)
    rows = P(AXES, None)
    return jax.shard_map(
        per_device,
        mesh=mesh,
        in_specs=(lanes, both, both, lanes, lanes, rows, rows, both, rows, rows),
        out_specs=lanes,
        check_vma=False,
    )
```

time: 145 us -> 135 us (0.931)
  Pallas kernels: 81.8 us -> 70.9 us
  starting transfers between devices: 45.2 us -> 37.3 us
  waiting for transfers between devices: 0.02 us -> 7.82 us
  local copies, waits for them, and re-layouts: 14.5 us -> 20 us
  other arithmetic: 3.83 us -> 0.53 us
    pallas_call x3, Pallas kernels: 34.7 us -> 24.4 us  [the longest x1 19.4 us: node_pull(): pl.pallas_call(node_kernel, out_shape=jax.ShapeDtypeStruct((BLK_DEV, 4, R...]
    ppermute x1, waiting for transfers between devices: 0.01 us -> 7.81 us  [per_device(): by_narrow = lax.ppermute(pm, 'narrow', near)]
    unnamed x36, local copies, waits for them, and re-layouts: 12.6 us -> 19.9 us
    all_to_all x3, starting transfers between devices: 41 us -> 34.3 us  [swap(): return lax.all_to_all(values, AXES, split_axis=0, concat_axis=0, tiled=True)]
    pallas_call x1, Pallas kernels: 24.5 us -> 29.8 us  [remote_pull(): pl.pallas_call(remote_kernel, out_shape=jax.ShapeDtypeStruct((slots, 4, R...]
    pallas_call x1, Pallas kernels: 8.08 us -> 3.26 us  [send_blocks(): pl.pallas_call(send_kernel, out_shape=(jax.ShapeDtypeStruct((devices, CAP...]
  transfers between devices with their start and end apart: 6 -> 6, of which waited for: 0 -> 1; matrix products, arithmetic and copies ran while one was open for 3% -> 0% of each run, Pallas kernels for 55% -> 48%
where the time goes in v2:
time: 135 us; the launch traced here: 137 us
  Pallas kernels  70.9 us (53%)
  starting transfers between devices  37.3 us (28%)
  local copies, waits for them, and re-layouts  20 us (15%)
  waiting for transfers between devices  7.82 us (6%)
    all_to_all x3, starting transfers between devices, swap(): return lax.all_to_all(values, AXES, split_axis=0, concat_axis=0, tiled=True)  34.3 us
    pallas_call x1, Pallas kernels, remote_pull(): pl.pallas_call(remote_kernel, out_shape=jax.ShapeDtypeStruct((slots, 4, R...  29.8 us
    unnamed x36, local copies, waits for them, and re-layouts  19.9 us
    pallas_call x1, Pallas kernels, node_pull(): pl.pallas_call(node_kernel, out_shape=jax.ShapeDtypeStruct((BLK_DEV, 4, R...  19.4 us
    pallas_call x1, Pallas kernels, local_pull(): pl.pallas_call(local_kernel, out_shape=jax.ShapeDtypeStruct((BLK_DEV, 4,...  11.7 us
    ppermute x1, waiting for transfers between devices, per_device(): by_narrow = lax.ppermute(pm, 'narrow', near)  7.81 us
    pallas_call x1, Pallas kernels, send_blocks(): pl.pallas_call(send_kernel, out_shape=(jax.ShapeDtypeStruct((devices, CAP...  3.26 us
    pallas_call x1, Pallas kernels, source_tables(): pl.pallas_call(source_kernel, out_shape=(jax.ShapeDtypeStruct((GROUP * BL...  3.19 us
  transfers between devices with their start and end apart: 6, of which 1 were waited for; matrix products, arithmetic and copies ran while one was open for 0% of the time, Pallas kernels for 48%

profile of v2, /device:TPU:1, one launch (start us, length us, event | category | flops | bytes accessed | tf_op | source)
XLA Modules:
  0.0 136.7 jit_solution(16898882606742632222)
XLA Ops:
  0.0 0.1 pad_add_fusion.place_ref
  0.1 0.9 copy-done
  1.0 0.0 copy-start.3
  1.0 0.8 copy-done.3
  1.7 0.0 copy-start.6
  1.7 0.7 copy-done.6
  2.4 0.0 copy-start.7
  2.4 0.7 copy-done.7
  3.1 0.0 copy-start.10
  3.1 0.7 copy-done.10
  3.7 3.3 %send_blocks.1 = (f32[128,2,4,128]{3,2,1,0:T(4,128)}, s32[128]{0:T(128)S(1)}, f32[4,8192]{1,0:T(4,128)S(1)}) custom-call(s32[3]{0:T(128)S(1)} %pad_add_fusion.place_ref, s32[128]{0:T(128)S(1)} %copy-done.7, s32[128]{0:T(128)S(1)} %bitcast.17, s32[8,128]{1,0:T(8,128)S(1)} %bitcast.15, f32[3,8192]{1,0:T(4,128)S(1)} %copy-done, f32[1,8192]{1,0:T(1,128)S(1)} %bitcast.14), custom_call_target="tpu_custom_call" | custom-call | tf_op jit(solution)/shard_map/send_blocks/pallas_call | solution.py:82
  7.0 11.5 %all-to-all-start = ((f32[128,2,4,128]{3,2,1,0:T(4,128)}), f32[128,2,4,128]{3,2,1,0:T(4,128)S(1)}, u32[]{:S(2)}, u32[]{:S(2)}) async-start(f32[128,2,4,128]{3,2,1,0:T(4,128)} %get-tuple-element.17), calls=%async_computation | async-start | bytes 1048576 | tf_op jit(solution)/shard_map/all_to_all | solution.py:395
  18.5 1.5 %collective-permute-start = (f32[4,8192]{1,0:T(4,128)S(1)}, f32[4,8192]{1,0:T(4,128)S(1)}, u32[]{:S(2)}, u32[]{:S(2)}) collective-permute-start(f32[4,8192]{1,0:T(4,128)S(1)} %get-tuple-element.18.pm0_ref), channel_id=1, source_target_pairs={{0,1},{1,0},{2,3},{3,2},{4,5},{5,4},{6,7},{7,6},{8,9},{9,8},{10,11... | collective-permute-start | bytes 393224 | tf_op jit(solution)/shard_map/ppermute | solution.py:430
  20.0 0.6 collective-permute-start.1
  20.6 7.8 %collective-permute-done.pm1_ref = f32[4,8192]{1,0:T(4,128)S(1)} collective-permute-done((f32[4,8192]{1,0:T(4,128)S(1)}, f32[4,8192]{1,0:T(4,128)S(1)}, u32[]{:S(2)}, u32[]{:S(2)}) %collective-permute-start) | collective-permute-done | bytes 131104 | tf_op jit(solution)/shard_map/ppermute | solution.py:430
  28.4 0.9 collective-permute-start.2
  29.3 0.0 copy-start.2
  29.3 0.8 copy-done.2
  30.1 0.7 copy-done.4
  30.8 0.7 copy-done.5
  31.5 0.7 copy-done.9
  32.1 1.8 %node_rows.1 = (f32[128,32,128]{2,1,0:T(8,128)}, s32[64,64]{1,0:T(8,128)S(1)}, s32[64,128]{1,0:T(8,128)S(1)}) custom-call(f32[1,256]{1,0:T(1,128)S(1)} %bitcast.16, f32[3,256]{1,0:T(4,128)S(1)} %copy-done.5, f32[6,256]{1,0:T(8,128)S(1)} %copy-done.4, s32[64,64]{1,0:T(8,128)S(1)} %copy-done.2), custom_call_target="tpu_custom_call" | custom-call | tf_op jit(solution)/shard_map/node_rows/pallas_call | solution.py:117
  33.9 0.0 collective-permute-done.1.pm2_ref
  33.9 0.0 collective-permute-done.2.pm3_ref
  33.9 3.2 %source_tables.1 = (bf16[256,128,128]{2,1,0:T(8,128)(2,1)S(1)}, bf16[256,16,128]{2,1,0:T(8,128)(2,1)S(1)}, f32[3,128]{1,0:T(4,128)S(1)}) custom-call(f32[4,8192]{1,0:T(4,128)S(1)} %get-tuple-element.18.pm0_ref, f32[4,8192]{1,0:T(4,128)S(1)} %collective-permute-done.pm1_ref, f32[4,8192]{1,0:T(4,128)S(1)} %collective-permute-done.1.pm2_ref, ...), custom_call_target="tpu_custom_call" | custom-call | tf_op jit(solution)/shard_map/source_tables/pallas_call | solution.py:166
  37.1 0.0 copy-start.11
  37.1 3.3 %copy-done.11 = bf16[256,128,128]{2,1,0:T(8,128)(2,1)} copy-done((bf16[256,128,128]{2,1,0:T(8,128)(2,1)}, bf16[256,128,128]{2,1,0:T(8,128)(2,1)S(1)}, u32[]{:S(2)}) %copy-start.11) | copy-done | bytes 8388632
  40.4 1.0 copy-done.14
  41.4 0.0 all-to-all-done
  41.4 9.0 %all-to-all-start.1 = ((f32[128,32,128]{2,1,0:T(8,128)}), f32[128,32,128]{2,1,0:T(8,128)S(1)}, u32[]{:S(2)}, u32[]{:S(2)}) async-start(f32[128,32,128]{2,1,0:T(8,128)} %get-tuple-element.25), calls=%async_computation.1 | async-start | bytes 4194304 | tf_op jit(solution)/shard_map/all_to_all | solution.py:395
  50.4 0.5 fusion
  50.9 0.1 convert_element_type.8.leaf_ref
  51.0 3.4 %copy-done.12 = bf16[256,128,128]{2,1,0:T(8,128)(2,1)S(1)} copy-done((bf16[256,128,128]{2,1,0:T(8,128)(2,1)S(1)}, bf16[256,128,128]{2,1,0:T(8,128)(2,1)}, u32[]{:S(2)}) %copy-start.12) | copy-done | bytes 8388632
  54.4 1.2 copy-done.15
  55.6 29.8 %remote_pull.1 = f32[256,4,128]{2,1,0:T(4,128)} custom-call(s32[2048]{0:T(1024)S(1)} %convert_element_type.8.leaf_ref, f32[3,128]{1,0:T(4,128)S(1)} %get-tuple-element.19.centre_ref, f32[256,4,128]{2,1,0:T(4,128)S(1)} %bitcast.13, bf16[256,128,128]{2,1,0:T(8,128)(2,1)S(1)} %copy-done.12, bf16[256,16,128]{2,1,0:T(8,128)(2,1)S(1)} %copy-done.15), custom_call_target="tpu_custom_call" | custom-call | flops 32000000000 | bytes 10000000 | tf_op jit(solution)/shard_map/remote_pull/pallas_call | solution.py:276
  85.4 0.0 all-to-all-done.1
  85.4 13.8 %all-to-all-start.2 = ((f32[128,2,4,128]{3,2,1,0:T(4,128)}), f32[128,2,4,128]{3,2,1,0:T(4,128)S(1)}, u32[]{:S(2)}, u32[]{:S(2)}) async-start(f32[128,2,4,128]{3,2,1,0:T(4,128)} %bitcast.8), calls=%async_computation.2 | async-start | bytes 1048576 | tf_op jit(solution)/shard_map/all_to_all | solution.py:395
  99.2 0.0 copy-done.1
  99.2 0.0 copy-done.17
  99.2 0.0 copy-start.13
  99.2 3.4 %copy-done.13 = bf16[256,128,128]{2,1,0:T(8,128)(2,1)S(1)} copy-done((bf16[256,128,128]{2,1,0:T(8,128)(2,1)S(1)}, bf16[256,128,128]{2,1,0:T(8,128)(2,1)}, u32[]{:S(2)}) %copy-start.13) | copy-done | bytes 8388632
  102.6 1.2 copy-done.16
  103.8 11.7 %local_pull.1.local_ref = f32[64,4,128]{2,1,0:T(4,128)S(1)} custom-call(s32[8,64]{1,0:T(8,128)S(1)} %bitcast.18, f32[3,128]{1,0:T(4,128)S(1)} %get-tuple-element.19.centre_ref, f32[3,8192]{1,0:T(4,128)S(1)} %copy-done.1, bf16[256,128,128]{2,1,0:T(8,128)(2,1)S(1)} %copy-done.13, bf16[256,16,128]{2,1,0:T(8,128)(2,1)S(1)} %copy-done.16), custom_call_target="tpu_custom_call" | custom-call | flops 16000000000 | bytes 1000000 | tf_op jit(solution)/shard_map/local_pull/pallas_call | solution.py:235
  115.5 0.0 copy-start.8
  115.6 19.4 %node_pull.1.node_ref = f32[64,4,128]{2,1,0:T(4,128)S(1)} custom-call(s32[64,64]{1,0:T(8,128)S(1)} %get-tuple-element.23.row_ref, f32[3,8192]{1,0:T(4,128)S(1)} %copy-done.1, s32[64,128]{1,0:T(8,128)S(1)} %get-tuple-element.24.lane_ref, f32[4096,128]{1,0:T(8,128)S(1)} %bitcast.10), custom_call_target="tpu_custom_call" | custom-call | flops 4000000000 | bytes 2000000 | tf_op jit(solution)/shard_map/node_pull/pallas_call | solution.py:349
  135.0 0.0 all-to-all-done.2
  135.0 0.0 copy-done.8
  135.0 1.7 %add_returned.1 = f32[3,8192]{1,0:T(4,128)} custom-call(s32[128]{0:T(128)S(1)} %get-tuple-element.16.slot_ref, s32[128]{0:T(128)S(1)} %copy-done.8, f32[64,4,128]{2,1,0:T(4,128)S(1)} %local_pull.1.local_ref, f32[64,4,128]{2,1,0:T(4,128)S(1)} %node_pull.1.node_ref, f32[256,4,128]{2,1,0:T(4,128)S(1)} %bitcast.11), custom_call_target="tpu_custom_call" | custom-call | tf_op jit(solution)/shard_map/add_returned/pallas_call | solution.py:383
  (10 shorter events, 0.0 us)
Async XLA Ops:
  0.1 0.9 copy-start
  1.0 0.8 copy-start.3
  1.7 0.7 copy-start.6
  2.4 0.7 copy-start.7
  3.1 0.7 copy-start.10
  7.0 34.4 %all-to-all-start = ((f32[128,2,4,128]{3,2,1,0:T(4,128)}), f32[128,2,4,128]{3,2,1,0:T(4,128)S(1)}, u32[]{:S(2)}, u32[]{:S(2)}) async-start(f32[128,2,4,128]{3,2,1,0:T(4,128)} %get-tuple-element.17), calls=%async_computation | async-start | bytes 1048576 | tf_op jit(solution)/shard_map/all_to_all | solution.py:395
  18.5 9.9 %collective-permute-start = (f32[4,8192]{1,0:T(4,128)S(1)}, f32[4,8192]{1,0:T(4,128)S(1)}, u32[]{:S(2)}, u32[]{:S(2)}) collective-permute-start(f32[4,8192]{1,0:T(4,128)S(1)} %get-tuple-element.18.pm0_ref), channel_id=1, source_target_pairs={{0,1},{1,0},{2,3},{3,2},{4,5},{5,4},{6,7},{7,6},{8,9},{9,8},{10,11... | collective-permute-start | bytes 393224 | tf_op jit(solution)/shard_map/ppermute | solution.py:430
  20.0 13.9 %collective-permute-start.1 = (f32[4,8192]{1,0:T(4,128)S(1)}, f32[4,8192]{1,0:T(4,128)S(1)}, u32[]{:S(2)}, u32[]{:S(2)}) collective-permute-start(f32[4,8192]{1,0:T(4,128)S(1)} %get-tuple-element.18.pm0_ref), channel_id=1, source_target_pairs={{0,16},{16,0},{32,48},{48,32},{64,80},{80,64},{96,112},{112,96},{1... | collective-permute-start | bytes 393224 | tf_op jit(solution)/shard_map/ppermute | solution.py:431
  28.4 5.5 %collective-permute-start.2 = (f32[4,8192]{1,0:T(4,128)S(1)}, f32[4,8192]{1,0:T(4,128)S(1)}, u32[]{:S(2)}, u32[]{:S(2)}) collective-permute-start(f32[4,8192]{1,0:T(4,128)S(1)} %collective-permute-done.pm1_ref), channel_id=1, source_target_pairs={{0,16},{16,0},{32,48},{48,32},{64,80},{80,64},{96,112},{112,96},{1... | collective-permute-start | bytes 393224 | tf_op jit(solution)/shard_map/ppermute | solution.py:432
  29.3 0.8 copy-start.2
  30.1 0.7 copy-start.4
  30.8 0.7 copy-start.5
  31.5 0.7 copy-start.9
  37.1 3.3 %copy-start.11 = (bf16[256,128,128]{2,1,0:T(8,128)(2,1)}, bf16[256,128,128]{2,1,0:T(8,128)(2,1)S(1)}, u32[]{:S(2)}) copy-start(bf16[256,128,128]{2,1,0:T(8,128)(2,1)S(1)} %get-tuple-element.20.table_ref) | copy-start | bytes 25165828
  40.4 1.0 copy-start.14
  41.4 44.0 %all-to-all-start.1 = ((f32[128,32,128]{2,1,0:T(8,128)}), f32[128,32,128]{2,1,0:T(8,128)S(1)}, u32[]{:S(2)}, u32[]{:S(2)}) async-start(f32[128,32,128]{2,1,0:T(8,128)} %get-tuple-element.25), calls=%async_computation.1 | async-start | bytes 4194304 | tf_op jit(solution)/shard_map/all_to_all | solution.py:395
  51.0 3.4 %copy-start.12 = (bf16[256,128,128]{2,1,0:T(8,128)(2,1)S(1)}, bf16[256,128,128]{2,1,0:T(8,128)(2,1)}, u32[]{:S(2)}) copy-start(bf16[256,128,128]{2,1,0:T(8,128)(2,1)} %copy-done.11) | copy-start | bytes 25165828
  54.4 1.2 copy-start.15
  55.6 43.6 %copy-start.1 = (f32[3,8192]{1,0:T(4,128)S(1)}, f32[3,8192]{1,0:T(4,128)}, u32[]{:S(2)}) copy-start(f32[3,8192]{1,0:T(4,128)} %pos_ref.5) | copy-start | bytes 294916
  55.6 43.6 %copy-start.17 = (s32[64,8]{0,1:T(8,128)S(1)}, s32[64,8]{0,1:T(8,128)}, u32[]{:S(2)}) copy-start(s32[64,8]{0,1:T(8,128)} %param.15) | copy-start | bytes 6148
  85.4 49.5 %all-to-all-start.2 = ((f32[128,2,4,128]{3,2,1,0:T(4,128)}), f32[128,2,4,128]{3,2,1,0:T(4,128)S(1)}, u32[]{:S(2)}, u32[]{:S(2)}) async-start(f32[128,2,4,128]{3,2,1,0:T(4,128)} %bitcast.8), calls=%async_computation.2 | async-start | bytes 1048576 | tf_op jit(solution)/shard_map/all_to_all | solution.py:395
  99.2 3.4 %copy-start.13 = (bf16[256,128,128]{2,1,0:T(8,128)(2,1)S(1)}, bf16[256,128,128]{2,1,0:T(8,128)(2,1)}, u32[]{:S(2)}) copy-start(bf16[256,128,128]{2,1,0:T(8,128)(2,1)} %copy-done.11) | copy-start | bytes 25165828
  102.6 1.2 copy-start.16
  115.5 19.4 %copy-start.8 = (s32[128]{0:T(128)S(1)}, s32[128]{0:T(128)}, u32[]{:S(2)}) copy-start(s32[128]{0:T(128)} %block_ref.3) | copy-start | bytes 1540

commit v3 on v2

v3 whole, which is shorter than its diff:
```python
import functools

import jax
import jax.numpy as jnp
from jax import lax
from jax.experimental import pallas as pl
from jax.experimental.pallas import tpu as pltpu
from jax.sharding import PartitionSpec as P

ROWS = 128
LEAF_N = 8
LIST_N = 64
CAP = 2
BLK_DEV = 64
EXP_BLK = 128
AXES = ("wide", "narrow")
GROUP = 4
STEP = 8
NODE_FIELDS = 10
SOFTEN = 0.01

f32 = jnp.float32
bf16 = jnp.bfloat16
VMEM = pl.BlockSpec(memory_space=pltpu.VMEM)
SMEM = pl.BlockSpec(memory_space=pltpu.SMEM)
HBM = pl.BlockSpec(memory_space=pltpu.HBM)


def params(mib):
    return pltpu.CompilerParams(vmem_limit_bytes=mib * 2**20)


def split3(value):
    high = value.astype(bf16)
    rest = value - high.astype(f32)
    middle = rest.astype(bf16)
    low = (rest - middle.astype(f32)).astype(bf16)
    return high, middle, low


def dot(left, right):
    return jnp.dot(left, right, preferred_element_type=f32)


def fetch(sources, targets, sems):
    copies = [
        pltpu.make_async_copy(source, target, sems.at[number])
        for number, (source, target) in enumerate(zip(sources, targets))
    ]
    for copy in copies:
        copy.start()
    return copies


def send_kernel(
    place_ref, block_in, dest_in, leaf_in, pos_in, mass_in, out_ref, slot_ref, pm_ref,
    block_ref, dest_ref, leaf_ref, pos_ref, mass_ref, count_ref, ids_ref, sems,
):
    copies = fetch(
        (block_in, dest_in, leaf_in, pos_in, mass_in),
        (block_ref, dest_ref, leaf_ref, pos_ref, mass_ref),
        sems,
    )
    devices = out_ref.shape[0]
    members, shift, turn = place_ref[0], place_ref[1], place_ref[2]
    out_ref[:, :, 3:4, :] = jnp.full((devices, CAP, 1, ROWS), -1.0, f32)

    def clear(index, carry):
        for part in range(8):
            count_ref[index * 8 + part] = 0
        return carry

    lax.fori_loop(0, devices // 8, clear, 0)
    for copy in copies:
        copy.wait()
    pm_ref[0:3] = pos_ref[...]
    pm_ref[3:4] = mass_ref[...]
    ids_ref[...] = jnp.concatenate([leaf_ref[...].astype(f32)] * (ROWS // LEAF_N), axis=0).T

    def one(step, carry):
        for part in range(8):
            export = step * 8 + part
            dest = dest_ref[export]
            side, across = dest & 1, (dest >> shift) & 1
            base = dest - side - across * members
            seen = count_ref[base]
            count_ref[base] = seen + 1
            member = (seen + turn) & (GROUP - 1)
            slot = seen >> 2
            target = base + (member >> 1) * members + (member & 1)
            distance = (across * 2 + side) ^ member
            slot_ref[export] = target * CAP + slot
            start = pl.multiple_of(block_ref[export] * ROWS, ROWS)
            out_ref[target, slot, 0:3, :] = pos_ref[:, pl.ds(start, ROWS)]
            ids = ids_ref[pl.ds(export, 1), 0:LEAF_N]
            out_ref[target, slot, 3:4, 0:LEAF_N] = ids + (distance * BLK_DEV).astype(f32)
        return carry

    lax.fori_loop(0, EXP_BLK // 8, one, 0)


def send_blocks(place, export_block, export_dest, export_leaves, positions, masses, devices):
    return pl.pallas_call(
        send_kernel,
        out_shape=(
            jax.ShapeDtypeStruct((devices, CAP, 4, ROWS), f32),
            jax.ShapeDtypeStruct((EXP_BLK,), jnp.int32),
            jax.ShapeDtypeStruct((4, BLK_DEV * ROWS), f32),
        ),
        in_specs=[SMEM] + [HBM] * 5,
        out_specs=(VMEM, SMEM, VMEM),
        scratch_shapes=[
            pltpu.SMEM((EXP_BLK,), jnp.int32),
            pltpu.SMEM((EXP_BLK,), jnp.int32),
            pltpu.VMEM((LEAF_N, EXP_BLK), jnp.int32),
            pltpu.VMEM(positions.shape, f32),
            pltpu.VMEM(masses.shape, f32),
            pltpu.SMEM((devices,), jnp.int32),
            pltpu.VMEM((EXP_BLK, 128), f32),
            pltpu.SemaphoreType.DMA((5,)),
        ],
        compiler_params=params(16),
        name="send_blocks",
    )(place, export_block, export_dest, export_leaves, positions, masses)


def node_rows_kernel(
    mass_in, centre_in, quad_in, list_in, out_ref, row_ref, part_ref, mass_ref, centre_ref, quad_ref, list_ref, sems
):
    copies = fetch(
        (mass_in, centre_in, quad_in, list_in), (mass_ref, centre_ref, quad_ref, list_ref), sems
    )
    for copy in copies:
        copy.wait()
    rows = out_ref.shape[1]
    count = mass_ref.shape[1]
    fields = jnp.concatenate(
        [mass_ref[...], centre_ref[...], quad_ref[...], jnp.zeros((16 - NODE_FIELDS, count), f32)], axis=0
    )
    parts = [fields[:, part * rows : (part + 1) * rows] for part in range(8)]
    table = jnp.concatenate(parts, axis=0).T
    out_ref[...] = jnp.broadcast_to(table[None], out_ref.shape)
    half = BLK_DEV // 2
    nodes = list_ref[...]
    nodes = jnp.concatenate([nodes[0:half], nodes[half:]], axis=1)
    bits = rows.bit_length() - 1
    row_ref[...] = ((nodes >> (bits + 3)) << bits) + (nodes & (rows - 1))
    part_ref[...] = (nodes >> bits) & 7


def node_rows(node_mass, node_centre, node_quad, node_lists, devices):
    count = node_mass.shape[1]
    arguments = (node_mass, node_centre, node_quad, node_lists)
    return pl.pallas_call(
        node_rows_kernel,
        out_shape=(
            jax.ShapeDtypeStruct((devices, count // 8, 128), f32),
            jax.ShapeDtypeStruct((BLK_DEV // 2, 2 * LIST_N), jnp.int32),
            jax.ShapeDtypeStruct((BLK_DEV // 2, 2 * LIST_N), jnp.int32),
        ),
        in_specs=[HBM] * 4,
        out_specs=(VMEM,) * 3,
        scratch_shapes=[pltpu.VMEM(value.shape, value.dtype) for value in arguments]
        + [pltpu.SemaphoreType.DMA((4,))],
        compiler_params=params(16),
        name="node_rows",
    )(*arguments)


def centred_rows(position, centre):
    moved = position - centre
    square = jnp.sum(moved * moved, axis=0, keepdims=True)
    one = jnp.ones_like(square)
    return moved, square, one, jnp.zeros((3,) + square.shape[1:], f32)


def mean_position(pm_ref):
    return jnp.sum(pm_ref[0:3], axis=1, keepdims=True) * (1.0 / pm_ref.shape[1])


def fill_tables(pm_refs, centre, table_ref, weight_ref):
    chunk = 8

    def step(index, carry):
        start = pl.multiple_of(index * (chunk * ROWS), chunk * ROWS)
        for group, pm_ref in enumerate(pm_refs):
            rows = pm_ref[:, pl.ds(start, chunk * ROWS)]
            for part in range(chunk):
                window = rows[:, part * ROWS : (part + 1) * ROWS]
                leaf = group * BLK_DEV + index * chunk + part
                moved, square, one, zero = centred_rows(window[0:3], centre)
                row = jnp.concatenate([-2.0 * moved, one, square, zero], axis=0)
                high, middle, low = [piece.astype(f32) for piece in split3(row)]
                blank = jnp.zeros((16, ROWS), f32)
                half = [high, high, middle, middle, high, low, blank]
                table_ref[leaf] = jnp.concatenate(half + half, axis=0).T.astype(bf16)
                pulled = jnp.concatenate([moved, one, zero, zero[0:1]], axis=0) * window[3:4]
                high, middle, _ = split3(pulled)
                weight_ref[leaf] = jnp.concatenate([high, middle], axis=0)
        return carry

    lax.fori_loop(0, BLK_DEV // chunk, step, 0)


def pull_block(position, centre, leaves, table_ref, weight_ref, left):
    moved, square, one, zero = centred_rows(position, centre)
    row = jnp.concatenate([moved, square + SOFTEN, one, zero], axis=0)
    high, middle, low = split3(row)
    blank = jnp.zeros((16, ROWS), bf16)
    half = jnp.concatenate([high, middle, high, middle, low, high, blank], axis=0)
    none = jnp.zeros_like(half)
    right = jnp.concatenate(
        [jnp.concatenate([half, none], axis=1), jnp.concatenate([none, half], axis=1)], axis=0
    )
    total = jnp.zeros((16, ROWS), f32)
    for pair in range(LEAF_N // 2):
        first, second = leaves[2 * pair], leaves[2 * pair + 1]
        spread = dot(jnp.where(left, table_ref[first], table_ref[second]), right)
        root = lax.rsqrt(spread)
        cubed = root * root * root
        high = cubed.astype(bf16)
        low = (cubed - high.astype(f32)).astype(bf16)
        for place, leaf in enumerate((first, second)):
            lanes = slice(place * ROWS, (place + 1) * ROWS)
            weight = weight_ref[leaf]
            total += dot(
                jnp.concatenate([weight, weight], axis=1),
                jnp.concatenate([high[:, lanes], low[:, lanes]], axis=0),
            )
    total = total[0:8] + total[8:16]
    return total[0:3] - moved * total[3:4]


def left_lanes():
    return lax.broadcasted_iota(jnp.int32, (ROWS, 128), 1) < 64


def remote_kernel(
    leaf_ref, pos_ref, pm0_ref, pm1_ref, pm2_ref, pm3_ref, out_ref, list_ref, table_ref, weight_ref
):
    slots = pos_ref.shape[0]

    def note(slot, found):
        list_ref[found] = slot
        return found + (leaf_ref[slot * LEAF_N] >= 0).astype(jnp.int32)

    found = lax.fori_loop(0, slots, note, 0)
    last = list_ref[jnp.maximum(found - 1, 0)]
    for place in range(STEP):
        list_ref[found + place] = last
    centre = mean_position(pm0_ref)
    fill_tables((pm0_ref, pm1_ref, pm2_ref, pm3_ref), centre, table_ref, weight_ref)
    left = left_lanes()

    def step(index, carry):
        results = []
        for place in range(STEP):
            slot = list_ref[index * STEP + place]
            leaves = [leaf_ref[slot * LEAF_N + k] for k in range(LEAF_N)]
            results.append((slot, pull_block(pos_ref[slot][0:3], centre, leaves, table_ref, weight_ref, left)))
        for slot, result in results:
            out_ref[slot, 0:3] = result
        return carry

    lax.fori_loop(0, (found + STEP - 1) // STEP, step, 0)


def remote_pull(leaves, visitors, pms):
    slots = visitors.shape[0]
    return pl.pallas_call(
        remote_kernel,
        out_shape=jax.ShapeDtypeStruct((slots, 4, ROWS), f32),
        in_specs=[SMEM] + [VMEM] * 5,
        out_specs=VMEM,
        scratch_shapes=[
            pltpu.SMEM((slots + STEP,), jnp.int32),
            pltpu.VMEM((GROUP * BLK_DEV, ROWS, 128), bf16),
            pltpu.VMEM((GROUP * BLK_DEV, 16, ROWS), bf16),
        ],
        compiler_params=params(32),
        cost_estimate=pl.CostEstimate(flops=32 * 10**9, bytes_accessed=10**7, transcendentals=16 * 10**6),
        name="remote_pull",
    )(leaves, visitors, *pms)


def node_sum(place, fields):
    mass, cx, cy, cz, qxx, qyy, qzz, qxy, qxz, qyz = fields
    x, y, z = place[0] - cx, place[1] - cy, place[2] - cz
    spread = x * x + y * y + z * z + SOFTEN
    quad_x = qxx * x + qxy * y + qxz * z
    quad_y = qxy * x + qyy * y + qyz * z
    quad_z = qxz * x + qyz * y + qzz * z
    root = lax.rsqrt(spread)
    inverse = root * root
    cubed = inverse * root
    fifth = cubed * inverse
    scalar = x * quad_x + y * quad_y + z * quad_z
    radial = -mass * cubed - 2.5 * scalar * (fifth * inverse)
    return radial * x + quad_x * fifth, radial * y + quad_y * fifth, radial * z + quad_z * fifth


def node_pair(block, centre, table_ref, part_ref, picked, left, spread_ref, gather_ref):
    turned = picked.T
    part = part_ref[pl.ds(block, 1), :]
    fields = turned[0:16]
    for number in range(1, 8):
        fields = jnp.where(part == number, turned[16 * number : 16 * number + 16], fields)
    rows = [fields[0:1]] + [fields[k + 1 : k + 2] - centre[k : k + 1] for k in range(3)]
    rows += [fields[k : k + 1] for k in range(4, NODE_FIELDS)]
    both = jnp.where(left, table_ref[block], table_ref[block + BLK_DEV // 2])
    place = dot(both, spread_ref[...])
    pulls = node_sum([place[:, 128 * k : 128 * k + 128] for k in range(3)], rows)
    total = jnp.zeros((16, ROWS), f32)
    for number, pull in enumerate(pulls):
        high = pull.astype(bf16)
        low = (pull - high.astype(f32)).astype(bf16)
        total += lax.dot_general(
            gather_ref[number],
            jnp.concatenate([high, low], axis=1),
            (((1,), (1,)), ((), ())),
            preferred_element_type=f32,
        )
    return total


NODE_STEP = 2


def own_kernel(
    leaf_ref, row_ref, part_ref, pm_ref, nodes_ref, out_ref, table_ref, weight_ref, spread_ref, gather_ref, *picked_refs
):
    half = BLK_DEV // 2
    centre = mean_position(pm_ref)
    fill_tables((pm_ref,), centre, table_ref, weight_ref)
    left = left_lanes()

    def step(index, carry):
        results = []
        for place in range(STEP):
            block = index * STEP + place
            start = pl.multiple_of(block * ROWS, ROWS)
            leaves = [leaf_ref[k, block] for k in range(LEAF_N)]
            results.append(
                pull_block(pm_ref[0:3, pl.ds(start, ROWS)], centre, leaves, table_ref, weight_ref, left)
            )
        for place in range(STEP):
            out_ref[index * STEP + place, 0:3] = results[place]
        return carry

    lax.fori_loop(0, BLK_DEV // STEP, step, 0)

    row = lax.broadcasted_iota(jnp.int32, (ROWS, 128), 0)
    lane = lax.broadcasted_iota(jnp.int32, (ROWS, 128), 1)
    for along in range(3):
        inner = row & 63
        hit = (inner == along) | (inner == 16 + along) | (inner == 40 + along)
        hit = hit & ((row >> 6) == (lane >> 6))
        spread_ref[:, 128 * along : 128 * along + 128] = jnp.where(hit, -0.5, 0.0).astype(bf16)
        row16 = lax.broadcasted_iota(jnp.int32, (16, 256), 0)
        lane16 = lax.broadcasted_iota(jnp.int32, (16, 256), 1) & 127
        mine = row16 == along + 4 * (lane16 >> 6)
        gather_ref[along] = jnp.where(mine, 1.0, 0.0).astype(bf16)

    def gather(refs, first):
        for number, ref in enumerate(refs):
            for node in range(2 * LIST_N):
                ref[pl.ds(node, 1), :] = nodes_ref[pl.ds(row_ref[first + number, node], 1), :]

    def compute(refs, first):
        results = [
            node_pair(first + number, centre, table_ref, part_ref, ref[...], left, spread_ref, gather_ref)
            for number, ref in enumerate(refs)
        ]
        for number, result in enumerate(results):
            out_ref[first + number, 0:3] += result[0:3]
            out_ref[first + number + half, 0:3] += result[4:7]

    before, after = picked_refs[:NODE_STEP], picked_refs[NODE_STEP:]
    gather(before, 0)

    def node_step(index, carry):
        first = index * (2 * NODE_STEP)
        gather(after, first + NODE_STEP)
        compute(before, first)
        gather(before, jnp.minimum(first + 2 * NODE_STEP, half - NODE_STEP))
        compute(after, first + NODE_STEP)
        return carry

    lax.fori_loop(0, half // (2 * NODE_STEP), node_step, 0)


def own_pull(local_leaves, rows, parts, pm, nodes):
    return pl.pallas_call(
        own_kernel,
        out_shape=jax.ShapeDtypeStruct((BLK_DEV, 4, ROWS), f32),
        in_specs=[SMEM, SMEM, VMEM, VMEM, VMEM],
        out_specs=VMEM,
        scratch_shapes=[
            pltpu.VMEM((BLK_DEV, ROWS, 128), bf16),
            pltpu.VMEM((BLK_DEV, 16, ROWS), bf16),
            pltpu.VMEM((ROWS, 3 * 128), bf16),
            pltpu.VMEM((3, 16, 256), bf16),
        ]
        + [pltpu.VMEM((2 * LIST_N, 128), f32)] * (2 * NODE_STEP),
        compiler_params=params(32),
        cost_estimate=pl.CostEstimate(flops=20 * 10**9, bytes_accessed=4 * 10**6, transcendentals=9 * 10**6),
        name="own_pull",
    )(local_leaves, rows, parts, pm, nodes)


def add_kernel(slot_ref, block_ref, own_ref, back_ref, out_ref, *sum_refs):
    parts = len(sum_refs)
    for part in range(1, parts):
        sum_refs[part][...] = jnp.zeros_like(sum_refs[part])
    sum_refs[0][...] = own_ref[...]

    def one(step, carry):
        for part in range(parts):
            export = step * parts + part
            block = block_ref[export]
            sum_refs[part][block] += back_ref[slot_ref[export]]
        return carry

    lax.fori_loop(0, EXP_BLK // parts, one, 0)
    for block in range(BLK_DEV):
        total = sum_refs[0][block]
        for part in range(1, parts):
            total = total + sum_refs[part][block]
        out_ref[:, block * ROWS : (block + 1) * ROWS] = total[0:3]


def add_returned(slots, export_block, own, back):
    return pl.pallas_call(
        add_kernel,
        out_shape=jax.ShapeDtypeStruct((3, BLK_DEV * ROWS), f32),
        in_specs=[SMEM, SMEM, VMEM, VMEM],
        out_specs=VMEM,
        scratch_shapes=[pltpu.VMEM((BLK_DEV, 4, ROWS), f32)] * 4,
        compiler_params=params(16),
        name="add_returned",
    )(slots, export_block, own, back)


def swap(values):
    return lax.all_to_all(values, AXES, split_axis=0, concat_axis=0, tiled=True)


def per_device(
    positions,
    masses,
    node_mass,
    node_centre,
    node_quad,
    local_leaves,
    node_lists,
    export_block,
    export_dest,
    export_leaves,
):
    groups = lax.axis_size("wide")
    members = lax.axis_size("narrow")
    devices = groups * members
    wide = lax.axis_index("wide")
    narrow = lax.axis_index("narrow")

    place = jnp.stack(
        [
            jnp.int32(members),
            jnp.int32(members.bit_length() - 1),
            (wide + narrow + (narrow >> 1)).astype(jnp.int32),
        ]
    )
    outgoing, slots, pm = send_blocks(
        place, export_block, export_dest[:, 0], export_leaves.T, positions, masses[None], devices
    )
    arrived = swap(outgoing)

    pms = [pm] + [
        lax.ppermute(pm, AXES, [(i, i ^ flip) for i in range(devices)])
        for flip in (1, members, members + 1)
    ]
    fields, rows, parts = node_rows(node_mass[None], node_centre, node_quad, node_lists, devices)
    nodes = swap(fields).reshape(-1, 128)

    visitors = arrived.reshape(devices * CAP, 4, ROWS)
    visitor_leaves = visitors[:, 3, 0:LEAF_N].astype(jnp.int32).reshape(-1)
    pulls = remote_pull(visitor_leaves, visitors, pms)
    pulls, leaves = lax.optimization_barrier((pulls, local_leaves.T))
    back = swap(pulls.reshape(devices, CAP, 4, ROWS))
    own = own_pull(leaves, rows, parts, pm, nodes)
    return add_returned(slots, export_block, own, back.reshape(devices * CAP, 4, ROWS))


def solution(mesh):
    both = P(AXES)
    lanes = P(None, AXES)
    rows = P(AXES, None)
    return jax.shard_map(
        per_device,
        mesh=mesh,
        in_specs=(lanes, both, both, lanes, lanes, rows, rows, both, rows, rows),
        out_specs=lanes,
        check_vma=False,
    )
```

time: 135 us -> 110 us (0.81); the launches traced: 137 us -> 110 us
  Pallas kernels: 70.9 us -> 56.3 us
  local copies, waits for them, and re-layouts: 20 us -> 7.93 us
    unnamed x36 -> x24, local copies, waits for them, and re-layouts: 19.9 us -> 7.82 us
    pallas_call x3 -> x1, Pallas kernels: 34.3 us -> 22.8 us  [own_pull(): pl.pallas_call(own_kernel, out_shape=jax.ShapeDtypeStruct((BLK_DEV, 4, RO...]
    all_to_all x3, waiting for transfers between devices: 0.01 us -> 8.52 us  [swap(): return lax.all_to_all(values, AXES, split_axis=0, concat_axis=0, tiled=True)]
    ppermute x3, waiting for transfers between devices: 7.81 us -> 0.01 us  [per_device(): lax.ppermute(pm, AXES, [(i, i ^ flip) for i in range(devices)])]
    pallas_call x1, Pallas kernels: 29.8 us -> 27.6 us  [remote_pull(): pl.pallas_call(remote_kernel, out_shape=jax.ShapeDtypeStruct((slots, 4, R...]
  transfers between devices with their start and end apart: 6 -> 6, of which waited for: 1 -> 2; matrix products, arithmetic and copies ran while one was open for 0% -> 1% of each run, Pallas kernels for 48% -> 46%
where the time goes in v3:
time: 110 us
  Pallas kernels  56.3 us (51%)
  starting transfers between devices  36.3 us (33%)
  waiting for transfers between devices  8.53 us (8%)
  local copies, waits for them, and re-layouts  7.93 us (7%)
    all_to_all x3, starting transfers between devices, swap(): return lax.all_to_all(values, AXES, split_axis=0, concat_axis=0, tiled=True)  33.8 us
    pallas_call x1, Pallas kernels, remote_pull(): pl.pallas_call(remote_kernel, out_shape=jax.ShapeDtypeStruct((slots, 4, R...  27.6 us
    pallas_call x1, Pallas kernels, own_pull(): pl.pallas_call(own_kernel, out_shape=jax.ShapeDtypeStruct((BLK_DEV, 4, RO...  22.8 us
    all_to_all x3, waiting for transfers between devices, swap(): return lax.all_to_all(values, AXES, split_axis=0, concat_axis=0, tiled=True)  8.52 us
    unnamed x24, local copies, waits for them, and re-layouts  7.82 us
    pallas_call x1, Pallas kernels, send_blocks(): pl.pallas_call(send_kernel, out_shape=(jax.ShapeDtypeStruct((devices, CAP...  3.69 us
    ppermute x3, starting transfers between devices, per_device(): lax.ppermute(pm, AXES, [(i, i ^ flip) for i in range(devices)])  2.5 us
  transfers between devices with their start and end apart: 6, of which 2 were waited for; matrix products, arithmetic and copies ran while one was open for 1% of the time, Pallas kernels for 46%

profile of v3, /device:TPU:1, one launch (start us, length us, event | category | flops | bytes accessed | tf_op | source)
XLA Modules:
  0.0 109.8 jit_solution(11235728208324360365)
XLA Ops:
  0.0 0.1 pad_add_fusion.place_ref
  0.1 0.0 copy-start.1
  0.1 0.9 copy-done.1
  1.0 0.0 copy-start.3
  1.0 0.8 copy-done.3
  1.7 0.0 copy-start.6
  1.7 0.7 copy-done.6
  2.4 0.0 copy-start.7
  2.4 0.7 copy-done.7
  3.1 0.0 copy-start.10
  3.1 0.7 copy-done.10
  3.7 3.7 %send_blocks.1 = (f32[128,2,4,128]{3,2,1,0:T(4,128)}, s32[128]{0:T(128)S(1)}, f32[4,8192]{1,0:T(4,128)S(1)}) custom-call(s32[3]{0:T(128)S(1)} %pad_add_fusion.place_ref, s32[128]{0:T(128)S(1)} %copy-done.7, s32[128]{0:T(128)S(1)} %bitcast.17, s32[8,128]{1,0:T(8,128)S(1)} %bitcast.15, f32[3,8192]{1,0:T(4,128)S(1)} %copy-done.1, f32[1,8192]{1,0:T(1,128)S(1)} %bitcast.14), custom_call_target="tpu_custom_call" | custom-call | tf_op jit(solution)/shard_map/send_blocks/pallas_call | solution.py:103
  7.4 11.5 %all-to-all-start = ((f32[128,2,4,128]{3,2,1,0:T(4,128)}), f32[128,2,4,128]{3,2,1,0:T(4,128)S(1)}, u32[]{:S(2)}, u32[]{:S(2)}) async-start(f32[128,2,4,128]{3,2,1,0:T(4,128)} %get-tuple-element.14), calls=%async_computation | async-start | bytes 1048576 | tf_op jit(solution)/shard_map/all_to_all | solution.py:445
  19.0 1.7 %collective-permute-start.2 = (f32[4,8192]{1,0:T(4,128)S(1)}, f32[4,8192]{1,0:T(4,128)S(1)}, u32[]{:S(2)}, u32[]{:S(2)}) collective-permute-start(f32[4,8192]{1,0:T(4,128)S(1)} %get-tuple-element.15.pm0_ref.pm_ref), channel_id=1, source_target_pairs={{0,17},{1,16},{2,19},{3,18},{4,21},{5,20},{6,23},{7,22},{8,25},{9,... | collective-permute-start | bytes 393224 | tf_op jit(solution)/shard_map/ppermute | solution.py:479
  20.7 0.1 collective-permute-start.1
  20.8 0.6 collective-permute-start
  21.5 0.0 copy-start.2
  21.5 0.8 copy-done.2
  22.2 0.0 copy-start.4
  22.2 0.7 copy-done.4
  22.9 0.0 copy-start.5
  22.9 0.7 copy-done.5
  23.6 0.0 copy-start.9
  23.6 0.7 copy-done.9
  24.3 0.5 node_rows.1
  24.8 0.0 copy-start
  24.8 1.3 %copy-done = f32[128,32,128]{2,1,0:T(8,128)} copy-done((f32[128,32,128]{2,1,0:T(8,128)}, f32[128,32,128]{2,1,0:T(8,128)S(1)}, u32[]{:S(2)}) %copy-start) | copy-done | bytes 2097176
  26.1 7.1 %all-to-all-done = f32[128,2,4,128]{3,2,1,0:T(4,128)S(1)} async-done(((f32[128,2,4,128]{3,2,1,0:T(4,128)}), f32[128,2,4,128]{3,2,1,0:T(4,128)S(1)}, u32[]{:S(2)}, u32[]{:S(2)}) %all-to-all-start) | async-done | bytes 524320 | tf_op jit(solution)/shard_map/all_to_all | solution.py:445
  33.2 4.1 %all-to-all-start.1 = ((f32[128,32,128]{2,1,0:T(8,128)}), f32[128,32,128]{2,1,0:T(8,128)S(1)}, u32[]{:S(2)}, u32[]{:S(2)}) async-start(f32[128,32,128]{2,1,0:T(8,128)} %copy-done), calls=%async_computation.1 | async-start | bytes 4194304 | tf_op jit(solution)/shard_map/all_to_all | solution.py:445
  37.4 0.5 fusion
  37.8 0.1 convert_element_type.8.leaf_ref
  38.0 0.0 copy-start.11
  38.0 0.0 collective-permute-done.2.pm3_ref
  38.0 0.0 collective-permute-done.1.pm2_ref
  38.0 0.0 collective-permute-done.pm1_ref
  38.0 27.6 %remote_pull.1 = f32[256,4,128]{2,1,0:T(4,128)} custom-call(s32[2048]{0:T(1024)S(1)} %convert_element_type.8.leaf_ref, f32[256,4,128]{2,1,0:T(4,128)S(1)} %bitcast.13, f32[4,8192]{1,0:T(4,128)S(1)} %get-tuple-element.15.pm0_ref.pm_ref, f32[4,8192]{1,0:T(4,128)S(1)} %collective-permute-done.pm1_ref, f32[4,8192]{1,0:T(4,128)S(1)} %collective-permute-done.1.pm2_ref, ...), custom_call_target="tpu_custom_call" | custom-call | flops 32000000000 | bytes 10000000 | tf_op jit(solution)/shard_map/remote_pull/pallas_call | solution.py:270
  65.6 1.4 %all-to-all-done.1 = f32[128,32,128]{2,1,0:T(8,128)S(1)} async-done(((f32[128,32,128]{2,1,0:T(8,128)}), f32[128,32,128]{2,1,0:T(8,128)S(1)}, u32[]{:S(2)}, u32[]{:S(2)}) %all-to-all-start.1) | async-done | bytes 2097184 | tf_op jit(solution)/shard_map/all_to_all | solution.py:445
  67.0 18.2 %all-to-all-start.2 = ((f32[128,2,4,128]{3,2,1,0:T(4,128)}), f32[128,2,4,128]{3,2,1,0:T(4,128)S(1)}, u32[]{:S(2)}, u32[]{:S(2)}) async-start(f32[128,2,4,128]{3,2,1,0:T(4,128)} %bitcast.8), calls=%async_computation.2 | async-start | bytes 1048576 | tf_op jit(solution)/shard_map/all_to_all | solution.py:445
  85.2 0.0 copy-done.11
  85.2 0.0 copy-start.8
  85.2 22.8 %own_pull.1.own_ref = f32[64,4,128]{2,1,0:T(4,128)S(1)} custom-call(s32[8,64]{1,0:T(8,128)S(1)} %bitcast.18, s32[32,128]{1,0:T(8,128)S(1)} %get-tuple-element.17.row_ref, s32[32,128]{1,0:T(8,128)S(1)} %get-tuple-element.18.part_ref, f32[4,8192]{1,0:T(4,128)S(1)} %get-tuple-element.15.pm0_ref.pm_ref, f32[4096,128]{1,0:T(8,128)S(1)} %bitcast.10), custom_call_target="tpu_custom_call" | custom-call | flops 20000000000 | bytes 4000000 | tf_op jit(solution)/shard_map/own_pull/pallas_call | solution.py:393
  108.0 0.0 all-to-all-done.2
  108.0 0.0 copy-done.8
  108.0 1.7 %add_returned.1 = f32[3,8192]{1,0:T(4,128)} custom-call(s32[128]{0:T(128)S(1)} %get-tuple-element.13.slot_ref, s32[128]{0:T(128)S(1)} %copy-done.8, f32[64,4,128]{2,1,0:T(4,128)S(1)} %own_pull.1.own_ref, f32[256,4,128]{2,1,0:T(4,128)S(1)} %bitcast.11), custom_call_target="tpu_custom_call" | custom-call | tf_op jit(solution)/shard_map/add_returned/pallas_call | solution.py:433
Async XLA Ops:
  0.1 0.9 copy-start.1
  1.0 0.8 copy-start.3
  1.7 0.7 copy-start.6
  2.4 0.7 copy-start.7
  3.1 0.7 copy-start.10
  7.4 25.8 %all-to-all-start = ((f32[128,2,4,128]{3,2,1,0:T(4,128)}), f32[128,2,4,128]{3,2,1,0:T(4,128)S(1)}, u32[]{:S(2)}, u32[]{:S(2)}) async-start(f32[128,2,4,128]{3,2,1,0:T(4,128)} %get-tuple-element.14), calls=%async_computation | async-start | bytes 1048576 | tf_op jit(solution)/shard_map/all_to_all | solution.py:445
  19.0 19.0 %collective-permute-start.2 = (f32[4,8192]{1,0:T(4,128)S(1)}, f32[4,8192]{1,0:T(4,128)S(1)}, u32[]{:S(2)}, u32[]{:S(2)}) collective-permute-start(f32[4,8192]{1,0:T(4,128)S(1)} %get-tuple-element.15.pm0_ref.pm_ref), channel_id=1, source_target_pairs={{0,17},{1,16},{2,19},{3,18},{4,21},{5,20},{6,23},{7,22},{8,25},{9,... | collective-permute-start | bytes 393224 | tf_op jit(solution)/shard_map/ppermute | solution.py:479
  20.7 17.3 %collective-permute-start.1 = (f32[4,8192]{1,0:T(4,128)S(1)}, f32[4,8192]{1,0:T(4,128)S(1)}, u32[]{:S(2)}, u32[]{:S(2)}) collective-permute-start(f32[4,8192]{1,0:T(4,128)S(1)} %get-tuple-element.15.pm0_ref.pm_ref), channel_id=1, source_target_pairs={{0,16},{1,17},{2,18},{3,19},{4,20},{5,21},{6,22},{7,23},{8,24},{9,... | collective-permute-start | bytes 393224 | tf_op jit(solution)/shard_map/ppermute | solution.py:479
  20.8 17.2 %collective-permute-start = (f32[4,8192]{1,0:T(4,128)S(1)}, f32[4,8192]{1,0:T(4,128)S(1)}, u32[]{:S(2)}, u32[]{:S(2)}) collective-permute-start(f32[4,8192]{1,0:T(4,128)S(1)} %get-tuple-element.15.pm0_ref.pm_ref), channel_id=1, source_target_pairs={{0,1},{1,0},{2,3},{3,2},{4,5},{5,4},{6,7},{7,6},{8,9},{9,8},{10,11... | collective-permute-start | bytes 393224 | tf_op jit(solution)/shard_map/ppermute | solution.py:479
  21.5 0.8 copy-start.2
  22.2 0.7 copy-start.4
  22.9 0.7 copy-start.5
  23.6 0.7 copy-start.9
  24.8 1.3 %copy-start = (f32[128,32,128]{2,1,0:T(8,128)}, f32[128,32,128]{2,1,0:T(8,128)S(1)}, u32[]{:S(2)}) copy-start(f32[128,32,128]{2,1,0:T(8,128)S(1)} %get-tuple-element.19) | copy-start | bytes 6291460
  33.2 33.8 %all-to-all-start.1 = ((f32[128,32,128]{2,1,0:T(8,128)}), f32[128,32,128]{2,1,0:T(8,128)S(1)}, u32[]{:S(2)}, u32[]{:S(2)}) async-start(f32[128,32,128]{2,1,0:T(8,128)} %copy-done), calls=%async_computation.1 | async-start | bytes 4194304 | tf_op jit(solution)/shard_map/all_to_all | solution.py:445
  38.0 47.2 %copy-start.11 = (s32[64,8]{0,1:T(8,128)S(1)}, s32[64,8]{0,1:T(8,128)}, u32[]{:S(2)}) copy-start(s32[64,8]{0,1:T(8,128)} %param.15) | copy-start | bytes 6148
  67.0 41.0 %all-to-all-start.2 = ((f32[128,2,4,128]{3,2,1,0:T(4,128)}), f32[128,2,4,128]{3,2,1,0:T(4,128)S(1)}, u32[]{:S(2)}, u32[]{:S(2)}) async-start(f32[128,2,4,128]{3,2,1,0:T(4,128)} %bitcast.8), calls=%async_computation.2 | async-start | bytes 1048576 | tf_op jit(solution)/shard_map/all_to_all | solution.py:445
  85.2 22.8 %copy-start.8 = (s32[128]{0:T(128)S(1)}, s32[128]{0:T(128)}, u32[]{:S(2)}) copy-start(s32[128]{0:T(128)} %block_ref.1) | copy-start | bytes 1540

commit v4 on v3

--- a/solution.py
+++ b/solution.py
@@ -14,7 +14,7 @@
 BLK_DEV = 64
 EXP_BLK = 128
 AXES = ("wide", "narrow")
-GROUP = 4
+GROUP = 8
 STEP = 8
 NODE_FIELDS = 10
 SOFTEN = 0.01
@@ -52,17 +52,34 @@
     return copies
 
 
+def node_rows(mass, centre, quad, nodes):
+    count = mass.shape[1]
+    rows = count // 8
+    fields = jnp.concatenate([mass, centre, quad, jnp.zeros((16 - NODE_FIELDS, count), f32)], axis=0)
+    parts = [fields[:, part * rows : (part + 1) * rows] for part in range(8)]
+    half = BLK_DEV // 2
+    nodes = jnp.concatenate([nodes[0:half], nodes[half:]], axis=1)
+    bits = rows.bit_length() - 1
+    row = ((nodes >> (bits + 3)) << bits) + (nodes & (rows - 1))
+    return jnp.concatenate(parts, axis=0).T, row, (nodes >> bits) & 7
+
+
 def send_kernel(
-    place_ref, block_in, dest_in, leaf_in, pos_in, mass_in, out_ref, slot_ref, pm_ref,
-    block_ref, dest_ref, leaf_ref, pos_ref, mass_ref, count_ref, ids_ref, sems,
+    place_ref, block_in, dest_in, leaf_in, pos_in, mass_in, node_mass_in, node_centre_in, node_quad_in, list_in,
+    out_ref, slot_ref, pm_ref, table_ref, row_ref, part_ref,
+    block_ref, dest_ref, leaf_ref, pos_ref, mass_ref, node_mass_ref, node_centre_ref, node_quad_ref, list_ref,
+    count_ref, ids_ref, sems,
 ):
     copies = fetch(
-        (block_in, dest_in, leaf_in, pos_in, mass_in),
-        (block_ref, dest_ref, leaf_ref, pos_ref, mass_ref),
+        (block_in, dest_in, leaf_in, pos_in, mass_in, node_mass_in, node_centre_in, node_quad_in, list_in),
+        (
+            block_ref, dest_ref, leaf_ref, pos_ref, mass_ref,
+            node_mass_ref, node_centre_ref, node_quad_ref, list_ref,
+        ),
         sems,
     )
     devices = out_ref.shape[0]
-    members, shift, turn = place_ref[0], place_ref[1], place_ref[2]
+    shift, turn = place_ref[0], place_ref[1]
     out_ref[:, :, 3:4, :] = jnp.full((devices, CAP, 1, ROWS), -1.0, f32)
 
     def clear(index, carry):
@@ -73,6 +90,9 @@
     lax.fori_loop(0, devices // 8, clear, 0)
     for copy in copies:
         copy.wait()
+    table_ref[...], row_ref[...], part_ref[...] = node_rows(
+        node_mass_ref[...], node_centre_ref[...], node_quad_ref[...], list_ref[...]
+    )
     pm_ref[0:3] = pos_ref[...]
     pm_ref[3:4] = mass_ref[...]
     ids_ref[...] = jnp.concatenate([leaf_ref[...].astype(f32)] * (ROWS // LEAF_N), axis=0).T
@@ -81,14 +101,14 @@
         for part in range(8):
             export = step * 8 + part
             dest = dest_ref[export]
-            side, across = dest & 1, (dest >> shift) & 1
-            base = dest - side - across * members
+            side, up, core = dest & 1, (dest >> 2) & 1, (dest >> shift) & 1
+            base = dest - side - up * 4 - (core << shift)
             seen = count_ref[base]
             count_ref[base] = seen + 1
             member = (seen + turn) & (GROUP - 1)
-            slot = seen >> 2
-            target = base + (member >> 1) * members + (member & 1)
-            distance = (across * 2 + side) ^ member
+            slot = seen >> 3
+            target = base + (member & 1) + (member & 2) * 2 + ((member >> 2) << shift)
+            distance = (side + up * 2 + core * 4) ^ member
             slot_ref[export] = target * CAP + slot
             start = pl.multiple_of(block_ref[export] * ROWS, ROWS)
             out_ref[target, slot, 0:3, :] = pos_ref[:, pl.ds(start, ROWS)]
@@ -99,72 +119,35 @@
     lax.fori_loop(0, EXP_BLK // 8, one, 0)
 
 
-def send_blocks(place, export_block, export_dest, export_leaves, positions, masses, devices):
+def send_blocks(place, devices, *arguments):
+    lists = arguments[-1]
+    count = arguments[-4].shape[1]
+    half = (lists.shape[0] // 2, lists.shape[1] * 2)
     return pl.pallas_call(
         send_kernel,
         out_shape=(
             jax.ShapeDtypeStruct((devices, CAP, 4, ROWS), f32),
             jax.ShapeDtypeStruct((EXP_BLK,), jnp.int32),
             jax.ShapeDtypeStruct((4, BLK_DEV * ROWS), f32),
+            jax.ShapeDtypeStruct((count // 8, 128), f32),
+            jax.ShapeDtypeStruct(half, jnp.int32),
+            jax.ShapeDtypeStruct(half, jnp.int32),
         ),
-        in_specs=[SMEM] + [HBM] * 5,
-        out_specs=(VMEM, SMEM, VMEM),
+        in_specs=[SMEM] + [HBM] * len(arguments),
+        out_specs=(VMEM, SMEM, VMEM, VMEM, VMEM, VMEM),
         scratch_shapes=[
             pltpu.SMEM((EXP_BLK,), jnp.int32),
             pltpu.SMEM((EXP_BLK,), jnp.int32),
-            pltpu.VMEM((LEAF_N, EXP_BLK), jnp.int32),
-            pltpu.VMEM(positions.shape, f32),
-            pltpu.VMEM(masses.shape, f32),
+        ]
+        + [pltpu.VMEM(value.shape, value.dtype) for value in arguments[2:]]
+        + [
             pltpu.SMEM((devices,), jnp.int32),
             pltpu.VMEM((EXP_BLK, 128), f32),
-            pltpu.SemaphoreType.DMA((5,)),
+            pltpu.SemaphoreType.DMA((len(arguments),)),
         ],
-        compiler_params=params(16),
+        compiler_params=params(56),
         name="send_blocks",
-    )(place, export_block, export_dest, export_leaves, positions, masses)
-
-
-def node_rows_kernel(
-    mass_in, centre_in, quad_in, list_in, out_ref, row_ref, part_ref, mass_ref, centre_ref, quad_ref, list_ref, sems
-):
-    copies = fetch(
-        (mass_in, centre_in, quad_in, list_in), (mass_ref, centre_ref, quad_ref, list_ref), sems
-    )
-    for copy in copies:
-        copy.wait()
-    rows = out_ref.shape[1]
-    count = mass_ref.shape[1]
-    fields = jnp.concatenate(
-        [mass_ref[...], centre_ref[...], quad_ref[...], jnp.zeros((16 - NODE_FIELDS, count), f32)], axis=0
-    )
-    parts = [fields[:, part * rows : (part + 1) * rows] for part in range(8)]
-    table = jnp.concatenate(parts, axis=0).T
-    out_ref[...] = jnp.broadcast_to(table[None], out_ref.shape)
-    half = BLK_DEV // 2
-    nodes = list_ref[...]
-    nodes = jnp.concatenate([nodes[0:half], nodes[half:]], axis=1)
-    bits = rows.bit_length() - 1
-    row_ref[...] = ((nodes >> (bits + 3)) << bits) + (nodes & (rows - 1))
-    part_ref[...] = (nodes >> bits) & 7
-
-
-def node_rows(node_mass, node_centre, node_quad, node_lists, devices):
-    count = node_mass.shape[1]
-    arguments = (node_mass, node_centre, node_quad, node_lists)
-    return pl.pallas_call(
-        node_rows_kernel,
-        out_shape=(
-            jax.ShapeDtypeStruct((devices, count // 8, 128), f32),
-            jax.ShapeDtypeStruct((BLK_DEV // 2, 2 * LIST_N), jnp.int32),
-            jax.ShapeDtypeStruct((BLK_DEV // 2, 2 * LIST_N), jnp.int32),
-        ),
-        in_specs=[HBM] * 4,
-        out_specs=(VMEM,) * 3,
-        scratch_shapes=[pltpu.VMEM(value.shape, value.dtype) for value in arguments]
-        + [pltpu.SemaphoreType.DMA((4,))],
-        compiler_params=params(16),
-        name="node_rows",
-    )(*arguments)
+    )(place, *arguments)
 
 
 def centred_rows(position, centre):
@@ -179,7 +162,7 @@
 
 
 def fill_tables(pm_refs, centre, table_ref, weight_ref):
-    chunk = 8
+    chunk = 4
 
     def step(index, carry):
         start = pl.multiple_of(index * (chunk * ROWS), chunk * ROWS)
@@ -235,9 +218,9 @@
     return lax.broadcasted_iota(jnp.int32, (ROWS, 128), 1) < 64
 
 
-def remote_kernel(
-    leaf_ref, pos_ref, pm0_ref, pm1_ref, pm2_ref, pm3_ref, out_ref, list_ref, table_ref, weight_ref
-):
+def remote_kernel(leaf_ref, pos_ref, *refs):
+    pm_refs = refs[:GROUP]
+    out_ref, list_ref, table_ref, weight_ref = refs[GROUP:]
     slots = pos_ref.shape[0]
 
     def note(slot, found):
@@ -248,8 +231,8 @@
     last = list_ref[jnp.maximum(found - 1, 0)]
     for place in range(STEP):
         list_ref[found + place] = last
-    centre = mean_position(pm0_ref)
-    fill_tables((pm0_ref, pm1_ref, pm2_ref, pm3_ref), centre, table_ref, weight_ref)
+    centre = mean_position(pm_refs[0])
+    fill_tables(pm_refs, centre, table_ref, weight_ref)
     left = left_lanes()
 
     def step(index, carry):
@@ -270,14 +253,14 @@
     return pl.pallas_call(
         remote_kernel,
         out_shape=jax.ShapeDtypeStruct((slots, 4, ROWS), f32),
-        in_specs=[SMEM] + [VMEM] * 5,
+        in_specs=[SMEM] + [VMEM] * (1 + GROUP),
         out_specs=VMEM,
         scratch_shapes=[
             pltpu.SMEM((slots + STEP,), jnp.int32),
             pltpu.VMEM((GROUP * BLK_DEV, ROWS, 128), bf16),
             pltpu.VMEM((GROUP * BLK_DEV, 16, ROWS), bf16),
         ],
-        compiler_params=params(32),
+        compiler_params=params(40),
         cost_estimate=pl.CostEstimate(flops=32 * 10**9, bytes_accessed=10**7, transcendentals=16 * 10**6),
         name="remote_pull",
     )(leaves, visitors, *pms)
@@ -326,10 +309,7 @@
 NODE_STEP = 2
 
 
-def own_kernel(
-    leaf_ref, row_ref, part_ref, pm_ref, nodes_ref, out_ref, table_ref, weight_ref, spread_ref, gather_ref, *picked_refs
-):
-    half = BLK_DEV // 2
+def local_kernel(leaf_ref, pm_ref, out_ref, table_ref, weight_ref):
     centre = mean_position(pm_ref)
     fill_tables((pm_ref,), centre, table_ref, weight_ref)
     left = left_lanes()
@@ -349,6 +329,31 @@
 
     lax.fori_loop(0, BLK_DEV // STEP, step, 0)
 
+
+def local_pull(local_leaves, pm):
+    return pl.pallas_call(
+        local_kernel,
+        out_shape=jax.ShapeDtypeStruct((BLK_DEV, 4, ROWS), f32),
+        in_specs=[SMEM, VMEM],
+        out_specs=VMEM,
+        scratch_shapes=[
+            pltpu.VMEM((BLK_DEV, ROWS, 128), bf16),
+            pltpu.VMEM((BLK_DEV, 16, ROWS), bf16),
+        ],
+        compiler_params=params(24),
+        cost_estimate=pl.CostEstimate(flops=16 * 10**9, bytes_accessed=10**6, transcendentals=8 * 10**6),
+        name="local_pull",
+    )(local_leaves, pm)
+
+
+def node_kernel(
+    row_ref, part_ref, pm_ref, nodes_ref, local_ref, out_ref, table_ref, weight_ref, spread_ref, gather_ref, *picked_refs
+):
+    half = BLK_DEV // 2
+    centre = mean_position(pm_ref)
+    fill_tables((pm_ref,), centre, table_ref, weight_ref)
+    left = left_lanes()
+
     row = lax.broadcasted_iota(jnp.int32, (ROWS, 128), 0)
     lane = lax.broadcasted_iota(jnp.int32, (ROWS, 128), 1)
     for along in range(3):
@@ -372,8 +377,8 @@
             for number, ref in enumerate(refs)
         ]
         for number, result in enumerate(results):
-            out_ref[first + number, 0:3] += result[0:3]
-            out_ref[first + number + half, 0:3] += result[4:7]
+            out_ref[first + number, 0:3] = local_ref[first + number, 0:3] + result[0:3]
+            out_ref[first + number + half, 0:3] = local_ref[first + number + half, 0:3] + result[4:7]
 
     before, after = picked_refs[:NODE_STEP], picked_refs[NODE_STEP:]
     gather(before, 0)
@@ -389,11 +394,11 @@
     lax.fori_loop(0, half // (2 * NODE_STEP), node_step, 0)
 
 
-def own_pull(local_leaves, rows, parts, pm, nodes):
+def node_pull(rows, parts, pm, nodes, local):
     return pl.pallas_call(
-        own_kernel,
+        node_kernel,
         out_shape=jax.ShapeDtypeStruct((BLK_DEV, 4, ROWS), f32),
-        in_specs=[SMEM, SMEM, VMEM, VMEM, VMEM],
+        in_specs=[SMEM, VMEM, VMEM, VMEM, VMEM],
         out_specs=VMEM,
         scratch_shapes=[
             pltpu.VMEM((BLK_DEV, ROWS, 128), bf16),
@@ -402,10 +407,10 @@
             pltpu.VMEM((3, 16, 256), bf16),
         ]
         + [pltpu.VMEM((2 * LIST_N, 128), f32)] * (2 * NODE_STEP),
-        compiler_params=params(32),
-        cost_estimate=pl.CostEstimate(flops=20 * 10**9, bytes_accessed=4 * 10**6, transcendentals=9 * 10**6),
-        name="own_pull",
-    )(local_leaves, rows, parts, pm, nodes)
+        compiler_params=params(24),
+        cost_estimate=pl.CostEstimate(flops=12 * 10**9, bytes_accessed=4 * 10**6, transcendentals=10**6),
+        name="node_pull",
+    )(rows, parts, pm, nodes, local)
 
 
 def add_kernel(slot_ref, block_ref, own_ref, back_ref, out_ref, *sum_refs):
@@ -460,34 +465,38 @@
     groups = lax.axis_size("wide")
     members = lax.axis_size("narrow")
     devices = groups * members
-    wide = lax.axis_index("wide")
     narrow = lax.axis_index("narrow")
 
-    place = jnp.stack(
-        [
-            jnp.int32(members),
-            jnp.int32(members.bit_length() - 1),
-            (wide + narrow + (narrow >> 1)).astype(jnp.int32),
-        ]
-    )
-    outgoing, slots, pm = send_blocks(
-        place, export_block, export_dest[:, 0], export_leaves.T, positions, masses[None], devices
+    place = jnp.stack([jnp.int32(members.bit_length() - 1), narrow.astype(jnp.int32)])
+    outgoing, slots, pm, fields, rows, parts = send_blocks(
+        place,
+        devices,
+        export_block,
+        export_dest[:, 0],
+        export_leaves.T,
+        positions,
+        masses[None],
+        node_mass[None],
+        node_centre,
+        node_quad,
+        node_lists,
     )
     arrived = swap(outgoing)
+    nodes = lax.all_gather(fields, AXES, axis=0, tiled=True)
 
     pms = [pm] + [
-        lax.ppermute(pm, AXES, [(i, i ^ flip) for i in range(devices)])
-        for flip in (1, members, members + 1)
+        lax.ppermute(pm, "narrow", [(i, i ^ flip) for i in range(members)]) for flip in (1, 4, 5)
     ]
-    fields, rows, parts = node_rows(node_mass[None], node_centre, node_quad, node_lists, devices)
-    nodes = swap(fields).reshape(-1, 128)
+    pms += [lax.ppermute(other, "wide", [(i, i ^ 1) for i in range(groups)]) for other in pms]
+    local = local_pull(local_leaves.T, pm)
+    arrived, local = lax.optimization_barrier((arrived, local))
 
     visitors = arrived.reshape(devices * CAP, 4, ROWS)
     visitor_leaves = visitors[:, 3, 0:LEAF_N].astype(jnp.int32).reshape(-1)
     pulls = remote_pull(visitor_leaves, visitors, pms)
-    pulls, leaves = lax.optimization_barrier((pulls, local_leaves.T))
+    pulls, local = lax.optimization_barrier((pulls, local))
     back = swap(pulls.reshape(devices, CAP, 4, ROWS))
-    own = own_pull(leaves, rows, parts, pm, nodes)
+    own = node_pull(rows, parts, pm, nodes, local)
     return add_returned(slots, export_block, own, back.reshape(devices * CAP, 4, ROWS))
 
 

time: 110 us -> 121 us (1.10)
  between operations: 0.13 us -> 13.5 us
  Pallas kernels: 56.3 us -> 61.5 us
  local copies, waits for them, and re-layouts: 7.93 us -> 3.33 us
  starting transfers between devices: 36.3 us -> 32.9 us
    all_to_all x3 -> x2, waiting for transfers between devices: 8.52 us -> 0.01 us  [swap(): return lax.all_to_all(values, AXES, split_axis=0, concat_axis=0, tiled=True)]
    all_to_all x3 -> x2, starting transfers between devices: 33.8 us -> 26.2 us  [swap(): return lax.all_to_all(values, AXES, split_axis=0, concat_axis=0, tiled=True)]
    all_gather x0 -> x1, waiting for transfers between devices: none -> 7.6 us  [per_device(): nodes = lax.all_gather(fields, AXES, axis=0, tiled=True)]
    unnamed x24 -> x16, local copies, waits for them, and re-layouts: 7.82 us -> 3.22 us
    ppermute x3 -> x7, starting transfers between devices: 2.5 us -> 6.65 us  [the longest x3 3.76 us: per_device(): lax.ppermute(pm, 'narrow', [(i, i ^ flip) for i in range(members)])]
    pallas_call x2, Pallas kernels: 23.3 us -> 26.1 us  [the longest x1 13.8 us: local_pull(): pl.pallas_call(local_kernel, out_shape=jax.ShapeDtypeStruct((BLK_DEV, 4,...]
    pallas_call x1, Pallas kernels: 27.6 us -> 29.1 us  [remote_pull(): pl.pallas_call(remote_kernel, out_shape=jax.ShapeDtypeStruct((slots, 4, R...]
  transfers between devices with their start and end apart: 6 -> 10, of which waited for: 2 -> 3; matrix products, arithmetic and copies ran while one was open for 1% -> 0% of each run, Pallas kernels for 46% -> 46%
where the time goes in v4:
time: 121 us
  Pallas kernels  61.5 us (51%)
  starting transfers between devices  32.9 us (27%)
  between operations  13.5 us (11%)
  waiting for transfers between devices  8.69 us (7%)
  local copies, waits for them, and re-layouts  3.33 us (3%)
    pallas_call x1, Pallas kernels, remote_pull(): pl.pallas_call(remote_kernel, out_shape=jax.ShapeDtypeStruct((slots, 4, R...  29.1 us
    all_to_all x2, starting transfers between devices, swap(): return lax.all_to_all(values, AXES, split_axis=0, concat_axis=0, tiled=True)  26.2 us
    pallas_call x1, Pallas kernels, local_pull(): pl.pallas_call(local_kernel, out_shape=jax.ShapeDtypeStruct((BLK_DEV, 4,...  13.8 us
    pallas_call x1, Pallas kernels, node_pull(): pl.pallas_call(node_kernel, out_shape=jax.ShapeDtypeStruct((BLK_DEV, 4, R...  12.2 us
    all_gather x1, waiting for transfers between devices, per_device(): nodes = lax.all_gather(fields, AXES, axis=0, tiled=True)  7.6 us
    pallas_call x1, Pallas kernels, send_blocks(): pl.pallas_call(send_kernel, out_shape=(jax.ShapeDtypeStruct((devices, CAP...  4.59 us
    ppermute x3, starting transfers between devices, per_device(): lax.ppermute(pm, 'narrow', [(i, i ^ flip) for i in range(members)])  3.76 us
    unnamed x16, local copies, waits for them, and re-layouts  3.22 us
  transfers between devices with their start and end apart: 10, of which 3 were waited for; matrix products, arithmetic and copies ran while one was open for 0% of the time, Pallas kernels for 46%

profile of v4, /device:TPU:1, one launch (start us, length us, event | category | flops | bytes accessed | tf_op | source)
XLA Modules:
  0.0 121.0 jit_solution(7501934873782311259)
XLA Ops:
  6.5 0.6 pad_add_fusion.place_ref
  7.1 4.6 %send_blocks.1 = (f32[128,2,4,128]{3,2,1,0:T(4,128)}, s32[128]{0:T(128)}, f32[4,8192]{1,0:T(4,128)}, f32[32,128]{1,0:T(8,128)}, s32[32,128]{1,0:T(8,128)}, /*index=5*/s32[32,128]{1,0:T(8,128)}) custom-call(s32[2]{0:T(128)} %pad_add_fusion.place_ref, s32[128]{0:T(128)} %block_ref.1, s32[128]{0:T(128)} %bitcast.16, s32[8,128]{1,0:T(8,128)} %bitcast.14, ...), custom_call_target="tpu_custom_call" | custom-call | tf_op jit(solution)/shard_map/send_blocks/pallas_call | solution.py:126
  11.7 2.1 %collective-permute-start = (f32[4,8192]{1,0:T(4,128)}, f32[4,8192]{1,0:T(4,128)S(1)}, u32[]{:S(2)}, u32[]{:S(2)}) collective-permute-start(f32[4,8192]{1,0:T(4,128)} %get-tuple-element.18.pm_ref.refs_0_), channel_id=1, source_target_pairs={{0,1},{1,0},{2,3},{3,2},{4,5},{5,4},{6,7},{7,6},{8,9},{9,8},{10,11... | collective-permute-start | bytes 393224 | tf_op jit(solution)/shard_map/ppermute | solution.py:488
  13.8 1.6 %collective-permute-start.1 = (f32[4,8192]{1,0:T(4,128)}, f32[4,8192]{1,0:T(4,128)S(1)}, u32[]{:S(2)}, u32[]{:S(2)}) collective-permute-start(f32[4,8192]{1,0:T(4,128)} %get-tuple-element.18.pm_ref.refs_0_), channel_id=1, source_target_pairs={{0,4},{1,5},{2,6},{3,7},{4,0},{5,1},{6,2},{7,3},{8,12},{9,13},{10,... | collective-permute-start | bytes 393224 | tf_op jit(solution)/shard_map/ppermute | solution.py:488
  15.5 0.0 collective-permute-start.2
  15.5 1.2 %collective-permute-start.3 = (f32[4,8192]{1,0:T(4,128)}, f32[4,8192]{1,0:T(4,128)S(1)}, u32[]{:S(2)}, u32[]{:S(2)}) collective-permute-start(f32[4,8192]{1,0:T(4,128)} %get-tuple-element.18.pm_ref.refs_0_), channel_id=1, source_target_pairs={{0,16},{16,0},{32,48},{48,32},{64,80},{80,64},{96,112},{112,96},{1... | collective-permute-start | bytes 393224 | tf_op jit(solution)/shard_map/ppermute | solution.py:490
  16.7 10.2 %all-to-all-start = ((f32[128,2,4,128]{3,2,1,0:T(4,128)}), f32[128,2,4,128]{3,2,1,0:T(4,128)S(1)}, u32[]{:S(2)}, u32[]{:S(2)}) async-start(f32[128,2,4,128]{3,2,1,0:T(4,128)} %get-tuple-element.20), calls=%async_computation | async-start | bytes 1048576 | tf_op jit(solution)/shard_map/all_to_all | solution.py:450
  26.9 0.0 all-gather.2.cloned.1.call-start
  27.0 0.7 all-gather.2.cloned.1.call-update
  27.6 0.0 copy-start.3
  27.7 0.9 copy-done.3
  28.6 0.0 copy-start.7
  28.6 0.7 copy-done.7
  29.2 0.0 copy-start.4
  29.2 13.8 %local_pull.1.local_ref = f32[64,4,128]{2,1,0:T(4,128)S(1)} custom-call(s32[8,64]{1,0:T(8,128)S(1)} %bitcast.12, f32[4,8192]{1,0:T(4,128)S(1)} %copy-done.3), custom_call_target="tpu_custom_call" | custom-call | flops 16000000000 | bytes 1000000 | tf_op jit(solution)/shard_map/local_pull/pallas_call | solution.py:334
  43.1 0.0 collective-permute-done.refs_1_
  43.1 1.1 collective-permute-start.4
  44.2 0.0 collective-permute-done.1.refs_2_
  44.2 0.1 collective-permute-start.5
  44.4 0.0 collective-permute-done.2.refs_3_
  44.4 0.4 collective-permute-start.6
  44.8 0.0 all-to-all-done
  44.8 0.5 fusion
  45.2 0.1 convert_element_type.8.leaf_ref
  45.4 0.0 copy-start.5
  45.4 0.0 copy-start.6
  45.4 0.0 collective-permute-done.3.refs_4_
  45.4 0.0 collective-permute-done.4.refs_5_
  45.4 0.2 collective-permute-done.5.refs_6_
  45.6 0.2 collective-permute-done.6.refs_7_
  45.8 0.0 copy-done.4
  45.8 29.1 %remote_pull.1 = f32[256,4,128]{2,1,0:T(4,128)} custom-call(s32[2048]{0:T(1024)S(1)} %convert_element_type.8.leaf_ref, f32[256,4,128]{2,1,0:T(4,128)S(1)} %bitcast.11, f32[4,8192]{1,0:T(4,128)S(1)} %copy-done.4, f32[4,8192]{1,0:T(4,128)S(1)} %collective-permute-done.refs_1_, f32[4,8192]{1,0:T(4,128)S(1)} %collective-permute-done.1.refs_2_, ...), custom_call_target="tpu_custom_call" | custom-call | flops 32000000000 | bytes 10000000 | tf_op jit(solution)/shard_map/remote_pull/pallas_call | solution.py:253
  74.9 16.0 %all-to-all-start.1 = ((f32[128,2,4,128]{3,2,1,0:T(4,128)}), f32[128,2,4,128]{3,2,1,0:T(4,128)S(1)}, u32[]{:S(2)}, u32[]{:S(2)}) async-start(f32[128,2,4,128]{3,2,1,0:T(4,128)} %bitcast.7), calls=%async_computation.1 | async-start | bytes 1048576 | tf_op jit(solution)/shard_map/all_to_all | solution.py:450
  90.9 7.6 %all-gather.2.cloned.1.call-done.nodes_ref = f32[4096,128]{1,0:T(8,128)} async-done(((f32[32,128]{1,0:T(8,128)}), f32[4096,128]{1,0:T(8,128)}) %all-gather.2.cloned.1.call-update) | async-done | bytes 2097168 | tf_op jit(solution)/shard_map/all_gather | solution.py:485
  98.5 0.0 copy-done.5
  98.5 0.0 copy-done.6
  98.5 0.0 copy-start.2
  98.5 1.6 %copy-done.2 = f32[4096,128]{1,0:T(8,128)S(1)} copy-done((f32[4096,128]{1,0:T(8,128)S(1)}, f32[4096,128]{1,0:T(8,128)}, u32[]{:S(2)}) %copy-start.2) | copy-done | bytes 2097176
  100.1 0.0 copy-start
  100.1 0.0 copy-start.1
  100.1 12.2 %node_pull.1.own_ref = f32[64,4,128]{2,1,0:T(4,128)S(1)} custom-call(s32[32,128]{1,0:T(8,128)S(1)} %copy-done.5, s32[32,128]{1,0:T(8,128)S(1)} %copy-done.6, f32[4,8192]{1,0:T(4,128)S(1)} %copy-done.4, f32[4096,128]{1,0:T(8,128)S(1)} %copy-done.2, f32[64,4,128]{2,1,0:T(4,128)S(1)} %local_pull.1.local_ref), custom_call_target="tpu_custom_call" | custom-call | flops 12000000000 | bytes 4000000 | tf_op jit(solution)/shard_map/node_pull/pallas_call | solution.py:398
  112.4 0.0 all-to-all-done.1
  112.4 0.0 copy-done
  112.4 0.0 copy-done.1
  112.4 1.7 %add_returned.1 = f32[3,8192]{1,0:T(4,128)} custom-call(s32[128]{0:T(128)S(1)} %copy-done.1, s32[128]{0:T(128)S(1)} %copy-done, f32[64,4,128]{2,1,0:T(4,128)S(1)} %node_pull.1.own_ref, f32[256,4,128]{2,1,0:T(4,128)S(1)} %bitcast.9), custom_call_target="tpu_custom_call" | custom-call | tf_op jit(solution)/shard_map/add_returned/pallas_call | solution.py:438
Async XLA Ops:
  11.7 31.4 %collective-permute-start = (f32[4,8192]{1,0:T(4,128)}, f32[4,8192]{1,0:T(4,128)S(1)}, u32[]{:S(2)}, u32[]{:S(2)}) collective-permute-start(f32[4,8192]{1,0:T(4,128)} %get-tuple-element.18.pm_ref.refs_0_), channel_id=1, source_target_pairs={{0,1},{1,0},{2,3},{3,2},{4,5},{5,4},{6,7},{7,6},{8,9},{9,8},{10,11... | collective-permute-start | bytes 393224 | tf_op jit(solution)/shard_map/ppermute | solution.py:488
  13.8 30.4 %collective-permute-start.1 = (f32[4,8192]{1,0:T(4,128)}, f32[4,8192]{1,0:T(4,128)S(1)}, u32[]{:S(2)}, u32[]{:S(2)}) collective-permute-start(f32[4,8192]{1,0:T(4,128)} %get-tuple-element.18.pm_ref.refs_0_), channel_id=1, source_target_pairs={{0,4},{1,5},{2,6},{3,7},{4,0},{5,1},{6,2},{7,3},{8,12},{9,13},{10,... | collective-permute-start | bytes 393224 | tf_op jit(solution)/shard_map/ppermute | solution.py:488
  15.5 28.9 %collective-permute-start.2 = (f32[4,8192]{1,0:T(4,128)}, f32[4,8192]{1,0:T(4,128)S(1)}, u32[]{:S(2)}, u32[]{:S(2)}) collective-permute-start(f32[4,8192]{1,0:T(4,128)} %get-tuple-element.18.pm_ref.refs_0_), channel_id=1, source_target_pairs={{0,5},{1,4},{2,7},{3,6},{4,1},{5,0},{6,3},{7,2},{8,13},{9,12},{10,... | collective-permute-start | bytes 393224 | tf_op jit(solution)/shard_map/ppermute | solution.py:488
  15.5 29.9 %collective-permute-start.3 = (f32[4,8192]{1,0:T(4,128)}, f32[4,8192]{1,0:T(4,128)S(1)}, u32[]{:S(2)}, u32[]{:S(2)}) collective-permute-start(f32[4,8192]{1,0:T(4,128)} %get-tuple-element.18.pm_ref.refs_0_), channel_id=1, source_target_pairs={{0,16},{16,0},{32,48},{48,32},{64,80},{80,64},{96,112},{112,96},{1... | collective-permute-start | bytes 393224 | tf_op jit(solution)/shard_map/ppermute | solution.py:490
  16.7 28.1 %all-to-all-start = ((f32[128,2,4,128]{3,2,1,0:T(4,128)}), f32[128,2,4,128]{3,2,1,0:T(4,128)S(1)}, u32[]{:S(2)}, u32[]{:S(2)}) async-start(f32[128,2,4,128]{3,2,1,0:T(4,128)} %get-tuple-element.20), calls=%async_computation | async-start | bytes 1048576 | tf_op jit(solution)/shard_map/all_to_all | solution.py:450
  26.9 71.6 %all-gather.2.cloned.1.call-start = ((), (), s32[]{:S(2)}) async-start(), calls=%async_computation.2 | async-start | bytes 2113536 | tf_op jit(solution)/shard_map/all_gather | solution.py:485
  27.6 0.9 copy-start.3
  28.6 0.7 copy-start.7
  29.2 16.5 %copy-start.4 = (f32[4,8192]{1,0:T(4,128)S(1)}, f32[4,8192]{1,0:T(4,128)}, u32[]{:S(2)}) copy-start(f32[4,8192]{1,0:T(4,128)} %get-tuple-element.18.pm_ref.refs_0_) | copy-start | bytes 393220
  43.1 2.3 %collective-permute-start.4 = (f32[4,8192]{1,0:T(4,128)S(1)}, f32[4,8192]{1,0:T(4,128)S(1)}, u32[]{:S(2)}, u32[]{:S(2)}) collective-permute-start(f32[4,8192]{1,0:T(4,128)S(1)} %collective-permute-done.refs_1_), channel_id=1, source_target_pairs={{0,16},{16,0},{32,48},{48,32},{64,80},{80,64},{96,112},{112,96},{1... | collective-permute-start | bytes 393224 | tf_op jit(solution)/shard_map/ppermute | solution.py:490
  44.2 1.3 %collective-permute-start.5 = (f32[4,8192]{1,0:T(4,128)S(1)}, f32[4,8192]{1,0:T(4,128)S(1)}, u32[]{:S(2)}, u32[]{:S(2)}) collective-permute-start(f32[4,8192]{1,0:T(4,128)S(1)} %collective-permute-done.1.refs_2_), channel_id=1, source_target_pairs={{0,16},{16,0},{32,48},{48,32},{64,80},{80,64},{96,112},{112,96},{1... | collective-permute-start | bytes 393224 | tf_op jit(solution)/shard_map/ppermute | solution.py:490
  44.4 1.4 %collective-permute-start.6 = (f32[4,8192]{1,0:T(4,128)S(1)}, f32[4,8192]{1,0:T(4,128)S(1)}, u32[]{:S(2)}, u32[]{:S(2)}) collective-permute-start(f32[4,8192]{1,0:T(4,128)S(1)} %collective-permute-done.2.refs_3_), channel_id=1, source_target_pairs={{0,16},{16,0},{32,48},{48,32},{64,80},{80,64},{96,112},{112,96},{1... | collective-permute-start | bytes 393224 | tf_op jit(solution)/shard_map/ppermute | solution.py:490
  45.4 53.2 %copy-start.5 = (s32[32,128]{1,0:T(8,128)S(1)}, s32[32,128]{1,0:T(8,128)}, u32[]{:S(2)}) copy-start(s32[32,128]{1,0:T(8,128)} %get-tuple-element.16.row_ref) | copy-start | bytes 49156
  45.4 53.2 %copy-start.6 = (s32[32,128]{1,0:T(8,128)S(1)}, s32[32,128]{1,0:T(8,128)}, u32[]{:S(2)}) copy-start(s32[32,128]{1,0:T(8,128)} %get-tuple-element.17.part_ref) | copy-start | bytes 49156
  74.9 37.4 %all-to-all-start.1 = ((f32[128,2,4,128]{3,2,1,0:T(4,128)}), f32[128,2,4,128]{3,2,1,0:T(4,128)S(1)}, u32[]{:S(2)}, u32[]{:S(2)}) async-start(f32[128,2,4,128]{3,2,1,0:T(4,128)} %bitcast.7), calls=%async_computation.1 | async-start | bytes 1048576 | tf_op jit(solution)/shard_map/all_to_all | solution.py:450
  98.5 1.6 %copy-start.2 = (f32[4096,128]{1,0:T(8,128)S(1)}, f32[4096,128]{1,0:T(8,128)}, u32[]{:S(2)}) copy-start(f32[4096,128]{1,0:T(8,128)} %all-gather.2.cloned.1.call-done.nodes_ref) | copy-start | bytes 6291460
  100.1 12.2 %copy-start = (s32[128]{0:T(128)S(1)}, s32[128]{0:T(128)}, u32[]{:S(2)}) copy-start(s32[128]{0:T(128)} %block_ref.1) | copy-start | bytes 1540
  100.1 12.3 %copy-start.1 = (s32[128]{0:T(128)S(1)}, s32[128]{0:T(128)}, u32[]{:S(2)}) copy-start(s32[128]{0:T(128)} %get-tuple-element.15.slot_ref) | copy-start | bytes 1540
Sparse Core Ops, SparseCore 0:
  30.7 67.7 all-gather.1

commit v5 on v4

--- a/solution.py
+++ b/solution.py
@@ -52,7 +52,7 @@
     return copies
 
 
-def node_rows(mass, centre, quad, nodes):
+def node_rows(mass, centre, quad, nodes, devices):
     count = mass.shape[1]
     rows = count // 8
     fields = jnp.concatenate([mass, centre, quad, jnp.zeros((16 - NODE_FIELDS, count), f32)], axis=0)
@@ -60,13 +60,15 @@
     half = BLK_DEV // 2
     nodes = jnp.concatenate([nodes[0:half], nodes[half:]], axis=1)
     bits = rows.bit_length() - 1
-    row = ((nodes >> (bits + 3)) << bits) + (nodes & (rows - 1))
+    each = rows // GROUP
+    share = (nodes & (rows - 1)) // each
+    row = (share * devices + (nodes >> (bits + 3))) * each + (nodes & (each - 1))
     return jnp.concatenate(parts, axis=0).T, row, (nodes >> bits) & 7
 
 
 def send_kernel(
-    place_ref, block_in, dest_in, leaf_in, pos_in, mass_in, node_mass_in, node_centre_in, node_quad_in, list_in,
-    out_ref, slot_ref, pm_ref, table_ref, row_ref, part_ref,
+    block_in, dest_in, leaf_in, pos_in, mass_in, node_mass_in, node_centre_in, node_quad_in, list_in,
+    out_ref, slot_ref, pm_ref, row_ref, part_ref,
     block_ref, dest_ref, leaf_ref, pos_ref, mass_ref, node_mass_ref, node_centre_ref, node_quad_ref, list_ref,
     count_ref, ids_ref, sems,
 ):
@@ -79,8 +81,9 @@
         sems,
     )
     devices = out_ref.shape[0]
-    shift, turn = place_ref[0], place_ref[1]
-    out_ref[:, :, 3:4, :] = jnp.full((devices, CAP, 1, ROWS), -1.0, f32)
+    shift = lax.axis_size("narrow").bit_length() - 1
+    turn = lax.axis_index("narrow")
+    out_ref[:, 0:CAP, 3:4, :] = jnp.full((devices, CAP, 1, ROWS), -1.0, f32)
 
     def clear(index, carry):
         for part in range(8):
@@ -90,9 +93,13 @@
     lax.fori_loop(0, devices // 8, clear, 0)
     for copy in copies:
         copy.wait()
-    table_ref[...], row_ref[...], part_ref[...] = node_rows(
-        node_mass_ref[...], node_centre_ref[...], node_quad_ref[...], list_ref[...]
+    table, row_ref[...], part_ref[...] = node_rows(
+        node_mass_ref[...], node_centre_ref[...], node_quad_ref[...], list_ref[...], devices
     )
+    each = table.shape[0] // GROUP
+    for device in range(devices):
+        member = (device & 1) + ((device >> 2) & 1) * 2 + ((device >> shift) & 1) * 4
+        out_ref[device, CAP] = table[member * each : (member + 1) * each]
     pm_ref[0:3] = pos_ref[...]
     pm_ref[3:4] = mass_ref[...]
     ids_ref[...] = jnp.concatenate([leaf_ref[...].astype(f32)] * (ROWS // LEAF_N), axis=0).T
@@ -119,22 +126,20 @@
     lax.fori_loop(0, EXP_BLK // 8, one, 0)
 
 
-def send_blocks(place, devices, *arguments):
+def send_blocks(devices, *arguments):
     lists = arguments[-1]
-    count = arguments[-4].shape[1]
     half = (lists.shape[0] // 2, lists.shape[1] * 2)
     return pl.pallas_call(
         send_kernel,
         out_shape=(
-            jax.ShapeDtypeStruct((devices, CAP, 4, ROWS), f32),
+            jax.ShapeDtypeStruct((devices, CAP + 1, 4, ROWS), f32),
             jax.ShapeDtypeStruct((EXP_BLK,), jnp.int32),
             jax.ShapeDtypeStruct((4, BLK_DEV * ROWS), f32),
-            jax.ShapeDtypeStruct((count // 8, 128), f32),
             jax.ShapeDtypeStruct(half, jnp.int32),
             jax.ShapeDtypeStruct(half, jnp.int32),
         ),
-        in_specs=[SMEM] + [HBM] * len(arguments),
-        out_specs=(VMEM, SMEM, VMEM, VMEM, VMEM, VMEM),
+        in_specs=[HBM] * len(arguments),
+        out_specs=(VMEM, SMEM, VMEM, VMEM, VMEM),
         scratch_shapes=[
             pltpu.SMEM((EXP_BLK,), jnp.int32),
             pltpu.SMEM((EXP_BLK,), jnp.int32),
@@ -147,7 +152,7 @@
         ],
         compiler_params=params(56),
         name="send_blocks",
-    )(place, *arguments)
+    )(*arguments)
 
 
 def centred_rows(position, centre):
@@ -221,13 +226,17 @@
 def remote_kernel(leaf_ref, pos_ref, *refs):
     pm_refs = refs[:GROUP]
     out_ref, list_ref, table_ref, weight_ref = refs[GROUP:]
-    slots = pos_ref.shape[0]
-
-    def note(slot, found):
-        list_ref[found] = slot
-        return found + (leaf_ref[slot * LEAF_N] >= 0).astype(jnp.int32)
-
-    found = lax.fori_loop(0, slots, note, 0)
+    devices = pos_ref.shape[0] // (CAP + 1)
+
+    def note(index, found):
+        for part in range(8):
+            for slot in range(CAP):
+                slot = (index * 8 + part) * (CAP + 1) + slot
+                list_ref[found] = slot
+                found = found + jnp.where(leaf_ref[slot * LEAF_N] >= 0, 1, 0)
+        return found
+
+    found = lax.fori_loop(0, devices // 8, note, 0)
     last = list_ref[jnp.maximum(found - 1, 0)]
     for place in range(STEP):
         list_ref[found + place] = last
@@ -242,21 +251,21 @@
             leaves = [leaf_ref[slot * LEAF_N + k] for k in range(LEAF_N)]
             results.append((slot, pull_block(pos_ref[slot][0:3], centre, leaves, table_ref, weight_ref, left)))
         for slot, result in results:
-            out_ref[slot, 0:3] = result
+            out_ref[slot // (CAP + 1), slot % (CAP + 1), 0:3] = result
         return carry
 
     lax.fori_loop(0, (found + STEP - 1) // STEP, step, 0)
 
 
 def remote_pull(leaves, visitors, pms):
-    slots = visitors.shape[0]
+    devices = visitors.shape[0] // (CAP + 1)
     return pl.pallas_call(
         remote_kernel,
-        out_shape=jax.ShapeDtypeStruct((slots, 4, ROWS), f32),
+        out_shape=jax.ShapeDtypeStruct((devices, CAP, 4, ROWS), f32),
         in_specs=[SMEM] + [VMEM] * (1 + GROUP),
         out_specs=VMEM,
         scratch_shapes=[
-            pltpu.SMEM((slots + STEP,), jnp.int32),
+            pltpu.SMEM((devices * CAP + STEP,), jnp.int32),
             pltpu.VMEM((GROUP * BLK_DEV, ROWS, 128), bf16),
             pltpu.VMEM((GROUP * BLK_DEV, 16, ROWS), bf16),
         ],
@@ -269,7 +278,7 @@
 def node_sum(place, fields):
     mass, cx, cy, cz, qxx, qyy, qzz, qxy, qxz, qyz = fields
     x, y, z = place[0] - cx, place[1] - cy, place[2] - cz
-    spread = x * x + y * y + z * z + SOFTEN
+    spread = x * x + y * y + (z * z + SOFTEN)
     quad_x = qxx * x + qxy * y + qxz * z
     quad_y = qxy * x + qyy * y + qyz * z
     quad_z = qxz * x + qyz * y + qzz * z
@@ -278,35 +287,128 @@
     cubed = inverse * root
     fifth = cubed * inverse
     scalar = x * quad_x + y * quad_y + z * quad_z
-    radial = -mass * cubed - 2.5 * scalar * (fifth * inverse)
+    radial = mass * cubed + scalar * (fifth * (-2.5 * inverse))
     return radial * x + quad_x * fifth, radial * y + quad_y * fifth, radial * z + quad_z * fifth
 
 
-def node_pair(block, centre, table_ref, part_ref, picked, left, spread_ref, gather_ref):
-    turned = picked.T
-    part = part_ref[pl.ds(block, 1), :]
-    fields = turned[0:16]
-    for number in range(1, 8):
-        fields = jnp.where(part == number, turned[16 * number : 16 * number + 16], fields)
-    rows = [fields[0:1]] + [fields[k + 1 : k + 2] - centre[k : k + 1] for k in range(3)]
-    rows += [fields[k : k + 1] for k in range(4, NODE_FIELDS)]
-    both = jnp.where(left, table_ref[block], table_ref[block + BLK_DEV // 2])
-    place = dot(both, spread_ref[...])
-    pulls = node_sum([place[:, 128 * k : 128 * k + 128] for k in range(3)], rows)
-    total = jnp.zeros((16, ROWS), f32)
-    for number, pull in enumerate(pulls):
-        high = pull.astype(bf16)
-        low = (pull - high.astype(f32)).astype(bf16)
-        total += lax.dot_general(
-            gather_ref[number],
-            jnp.concatenate([high, low], axis=1),
-            (((1,), (1,)), ((), ())),
-            preferred_element_type=f32,
-        )
-    return total
-
-
-NODE_STEP = 2
+NODE_PART = 16
+
+
+def node_kernel(
+    row_ref, part_ref, pm_ref, local_ref, *refs,
+):
+    half = BLK_DEV // 2
+    share_refs, (out_ref, table_ref, weight_ref, spread_ref, gather_ref, nodes_ref) = refs[:GROUP], refs[GROUP : GROUP + 6]
+    refs = refs[GROUP + 6 :]
+    picked_refs, field_refs, place_refs, pull_refs = refs[0:2], refs[2:4], refs[4:6], refs[6:8]
+    narrow = lax.axis_index("narrow")
+    here = (narrow & 1) + ((narrow >> 2) & 1) * 2 + (lax.axis_index("wide") & 1) * 4
+    devices, each = share_refs[0].shape[0], share_refs[0].shape[1]
+    for distance, share_ref in enumerate(share_refs):
+        first = pl.multiple_of((here ^ distance) * (devices * each), devices * each)
+        for device in range(0, devices, 2):
+            nodes_ref[pl.ds(first + device * each, 2 * each), :] = jnp.concatenate(
+                [share_ref[device], share_ref[device + 1]], axis=0
+            )
+    centre = mean_position(pm_ref)
+    fill_tables((pm_ref,), centre, table_ref, weight_ref)
+    left = left_lanes()
+
+    row = lax.broadcasted_iota(jnp.int32, (ROWS, 128), 0)
+    lane = lax.broadcasted_iota(jnp.int32, (ROWS, 128), 1)
+    for along in range(3):
+        inner = row & 63
+        hit = (inner == along) | (inner == 16 + along) | (inner == 40 + along)
+        hit = hit & ((row >> 6) == (lane >> 6))
+        spread_ref[:, 128 * along : 128 * along + 128] = jnp.where(hit, -0.5, 0.0).astype(bf16)
+        row16 = lax.broadcasted_iota(jnp.int32, (16, 256), 0)
+        lane16 = lax.broadcasted_iota(jnp.int32, (16, 256), 1) & 127
+        mine = row16 == along + 4 * (lane16 >> 6)
+        gather_ref[along] = jnp.where(mine, 1.0, 0.0).astype(bf16)
+
+    def pick(block, target, first, last):
+        for node in range(first, last):
+            target[pl.ds(node, 1), :] = nodes_ref[pl.ds(row_ref[block, node], 1), :]
+
+    def lay_out(block, side):
+        turned = picked_refs[side][...].T
+        part = part_ref[pl.ds(block, 1), :]
+        fields = turned[0:16]
+        for number in range(1, 8):
+            fields = jnp.where(part == number, turned[16 * number : 16 * number + 16], fields)
+        rows = [-fields[0:1]] + [fields[k + 1 : k + 2] - centre[k : k + 1] for k in range(3)]
+        rows += [fields[k : k + 1] for k in range(4, NODE_FIELDS)]
+        for number, value in enumerate(rows):
+            field_refs[side][number] = jnp.broadcast_to(value, (8, 128))
+        both = jnp.where(left, table_ref[block], table_ref[block + half])
+        place_refs[side][...] = dot(both, spread_ref[...])
+
+    def compute(side, start):
+        rows = [field_refs[side][number] for number in range(NODE_FIELDS)]
+        halves = [
+            node_sum([place_refs[side][at : at + 8, 128 * k : 128 * k + 128] for k in range(3)], rows)
+            for at in range(start, start + NODE_PART, 8)
+        ]
+        for number in range(3):
+            pull = jnp.concatenate([half_[number] for half_ in halves], axis=0)
+            high = pull.astype(bf16)
+            pull_refs[side][number, start : start + NODE_PART, 0:128] = high
+            pull_refs[side][number, start : start + NODE_PART, 128:256] = (pull - high.astype(f32)).astype(bf16)
+
+    def add_up(block, side):
+        total = jnp.zeros((16, ROWS), f32)
+        for number in range(3):
+            total += lax.dot_general(
+                gather_ref[number],
+                pull_refs[side][number],
+                (((1,), (1,)), ((), ())),
+                preferred_element_type=f32,
+            )
+        out_ref[block, 0:3] = local_ref[block, 0:3] + total[0:3]
+        out_ref[block + half, 0:3] = local_ref[block + half, 0:3] + total[4:7]
+
+    pick(0, picked_refs[0], 0, 2 * LIST_N)
+    pick(1, picked_refs[1], 0, 2 * LIST_N)
+    lay_out(0, 0)
+
+    def step(index, carry):
+        for side in range(2):
+            block = index * 2 + side
+            other = 1 - side
+            lay_out(jnp.minimum(block + 1, half - 1), other)
+            add_up(jnp.maximum(block - 1, 0), other)
+            ahead = jnp.minimum(block + 2, half - 1)
+            for start in range(0, ROWS, NODE_PART):
+                compute(side, start)
+                pick(ahead, picked_refs[side], start, start + NODE_PART)
+        return carry
+
+    lax.fori_loop(0, half // 2, step, 0)
+    add_up(half - 1, 1)
+
+
+def node_pull(rows, parts, pm, local, shares):
+    devices, each = shares[0].shape[0:2]
+    return pl.pallas_call(
+        node_kernel,
+        out_shape=jax.ShapeDtypeStruct((BLK_DEV, 4, ROWS), f32),
+        in_specs=[SMEM] + [VMEM] * (3 + GROUP),
+        out_specs=VMEM,
+        scratch_shapes=[
+            pltpu.VMEM((BLK_DEV, ROWS, 128), bf16),
+            pltpu.VMEM((BLK_DEV, 16, ROWS), bf16),
+            pltpu.VMEM((ROWS, 3 * 128), bf16),
+            pltpu.VMEM((3, 16, 256), bf16),
+            pltpu.VMEM((GROUP * devices * each, 128), f32),
+        ]
+        + [pltpu.VMEM((2 * LIST_N, 128), f32)] * 2
+        + [pltpu.VMEM((NODE_FIELDS, 8, 128), f32)] * 2
+        + [pltpu.VMEM((ROWS, 3 * 128), f32)] * 2
+        + [pltpu.VMEM((3, ROWS, 256), bf16)] * 2,
+        compiler_params=params(24),
+        cost_estimate=pl.CostEstimate(flops=12 * 10**9, bytes_accessed=4 * 10**6, transcendentals=10**6),
+        name="node_pull",
+    )(rows, parts, pm, local, *shares)
 
 
 def local_kernel(leaf_ref, pm_ref, out_ref, table_ref, weight_ref):
@@ -344,73 +446,6 @@
         cost_estimate=pl.CostEstimate(flops=16 * 10**9, bytes_accessed=10**6, transcendentals=8 * 10**6),
         name="local_pull",
     )(local_leaves, pm)
-
-
-def node_kernel(
-    row_ref, part_ref, pm_ref, nodes_ref, local_ref, out_ref, table_ref, weight_ref, spread_ref, gather_ref, *picked_refs
-):
-    half = BLK_DEV // 2
-    centre = mean_position(pm_ref)
-    fill_tables((pm_ref,), centre, table_ref, weight_ref)
-    left = left_lanes()
-
-    row = lax.broadcasted_iota(jnp.int32, (ROWS, 128), 0)
-    lane = lax.broadcasted_iota(jnp.int32, (ROWS, 128), 1)
-    for along in range(3):
-        inner = row & 63
-        hit = (inner == along) | (inner == 16 + along) | (inner == 40 + along)
-        hit = hit & ((row >> 6) == (lane >> 6))
-        spread_ref[:, 128 * along : 128 * along + 128] = jnp.where(hit, -0.5, 0.0).astype(bf16)
-        row16 = lax.broadcasted_iota(jnp.int32, (16, 256), 0)
-        lane16 = lax.broadcasted_iota(jnp.int32, (16, 256), 1) & 127
-        mine = row16 == along + 4 * (lane16 >> 6)
-        gather_ref[along] = jnp.where(mine, 1.0, 0.0).astype(bf16)
-
-    def gather(refs, first):
-        for number, ref in enumerate(refs):
-            for node in range(2 * LIST_N):
-                ref[pl.ds(node, 1), :] = nodes_ref[pl.ds(row_ref[first + number, node], 1), :]
-
-    def compute(refs, first):
-        results = [
-            node_pair(first + number, centre, table_ref, part_ref, ref[...], left, spread_ref, gather_ref)
-            for number, ref in enumerate(refs)
-        ]
-        for number, result in enumerate(results):
-            out_ref[first + number, 0:3] = local_ref[first + number, 0:3] + result[0:3]
-            out_ref[first + number + half, 0:3] = local_ref[first + number + half, 0:3] + result[4:7]
-
-    before, after = picked_refs[:NODE_STEP], picked_refs[NODE_STEP:]
-    gather(before, 0)
-
-    def node_step(index, carry):
-        first = index * (2 * NODE_STEP)
-        gather(after, first + NODE_STEP)
-        compute(before, first)
-        gather(before, jnp.minimum(first + 2 * NODE_STEP, half - NODE_STEP))
-        compute(after, first + NODE_STEP)
-        return carry
-
-    lax.fori_loop(0, half // (2 * NODE_STEP), node_step, 0)
-
-
-def node_pull(rows, parts, pm, nodes, local):
-    return pl.pallas_call(
-        node_kernel,
-        out_shape=jax.ShapeDtypeStruct((BLK_DEV, 4, ROWS), f32),
-        in_specs=[SMEM, VMEM, VMEM, VMEM, VMEM],
-        out_specs=VMEM,
-        scratch_shapes=[
-            pltpu.VMEM((BLK_DEV, ROWS, 128), bf16),
-            pltpu.VMEM((BLK_DEV, 16, ROWS), bf16),
-            pltpu.VMEM((ROWS, 3 * 128), bf16),
-            pltpu.VMEM((3, 16, 256), bf16),
-        ]
-        + [pltpu.VMEM((2 * LIST_N, 128), f32)] * (2 * NODE_STEP),
-        compiler_params=params(24),
-        cost_estimate=pl.CostEstimate(flops=12 * 10**9, bytes_accessed=4 * 10**6, transcendentals=10**6),
-        name="node_pull",
-    )(rows, parts, pm, nodes, local)
 
 
 def add_kernel(slot_ref, block_ref, own_ref, back_ref, out_ref, *sum_refs):
@@ -465,11 +500,14 @@
     groups = lax.axis_size("wide")
     members = lax.axis_size("narrow")
     devices = groups * members
-    narrow = lax.axis_index("narrow")
-
-    place = jnp.stack([jnp.int32(members.bit_length() - 1), narrow.astype(jnp.int32)])
-    outgoing, slots, pm, fields, rows, parts = send_blocks(
-        place,
+
+    def group_of(value):
+        found = [value] + [
+            lax.ppermute(value, "narrow", [(i, i ^ flip) for i in range(members)]) for flip in (1, 4, 5)
+        ]
+        return found + [lax.ppermute(other, "wide", [(i, i ^ 1) for i in range(groups)]) for other in found]
+
+    outgoing, slots, pm, rows, parts = send_blocks(
         devices,
         export_block,
         export_dest[:, 0],
@@ -482,21 +520,17 @@
         node_lists,
     )
     arrived = swap(outgoing)
-    nodes = lax.all_gather(fields, AXES, axis=0, tiled=True)
-
-    pms = [pm] + [
-        lax.ppermute(pm, "narrow", [(i, i ^ flip) for i in range(members)]) for flip in (1, 4, 5)
-    ]
-    pms += [lax.ppermute(other, "wide", [(i, i ^ 1) for i in range(groups)]) for other in pms]
+    pms = group_of(pm)
     local = local_pull(local_leaves.T, pm)
     arrived, local = lax.optimization_barrier((arrived, local))
 
-    visitors = arrived.reshape(devices * CAP, 4, ROWS)
+    shares = group_of(arrived[:, CAP])
+    visitors = arrived.reshape(devices * (CAP + 1), 4, ROWS)
     visitor_leaves = visitors[:, 3, 0:LEAF_N].astype(jnp.int32).reshape(-1)
     pulls = remote_pull(visitor_leaves, visitors, pms)
     pulls, local = lax.optimization_barrier((pulls, local))
-    back = swap(pulls.reshape(devices, CAP, 4, ROWS))
-    own = node_pull(rows, parts, pm, nodes, local)
+    back = swap(pulls)
+    own = node_pull(rows, parts, pm, local, shares)
     return add_returned(slots, export_block, own, back.reshape(devices * CAP, 4, ROWS))
 
 

time: 121 us -> 111 us (0.917)
  between operations: 13.5 us -> 0.15 us
  waiting for transfers between devices: 8.69 us -> 10.3 us
    all_gather x1 -> x0, waiting for transfers between devices: 7.6 us -> none  [per_device(): nodes = lax.all_gather(fields, AXES, axis=0, tiled=True)]
    all_to_all x2, starting transfers between devices: 26.2 us -> 18.8 us  [swap(): return lax.all_to_all(values, AXES, split_axis=0, concat_axis=0, tiled=True)]
    ppermute x7 -> x14, starting transfers between devices: 6.65 us -> 13.6 us  [the longest x8 7.96 us: group_of(): lax.ppermute(other, 'wide', [(i, i ^ 1) for i in range(groups)])]
    ppermute x7 -> x14, waiting for transfers between devices: 0.41 us -> 5.38 us  [the longest x6 5.3 us: group_of(): lax.ppermute(value, 'narrow', [(i, i ^ flip) for i in range(members)])]
    all_to_all x2, waiting for transfers between devices: 0.01 us -> 4.95 us  [swap(): return lax.all_to_all(values, AXES, split_axis=0, concat_axis=0, tiled=True)]
    pallas_call x1, Pallas kernels: 29.1 us -> 32.4 us  [remote_pull(): pl.pallas_call(remote_kernel, out_shape=jax.ShapeDtypeStruct((devices, CA...]
    pallas_call x1, Pallas kernels: 12.2 us -> 10.3 us  [node_pull(): pl.pallas_call(node_kernel, out_shape=jax.ShapeDtypeStruct((BLK_DEV, 4, R...]
    unnamed x16 -> x24, local copies, waits for them, and re-layouts: 3.22 us -> 3.81 us
  transfers between devices with their start and end apart: 10 -> 16, of which waited for: 3 -> 5; matrix products, arithmetic and copies ran while one was open for 0% -> 1% of each run, Pallas kernels for 46% -> 51%
where the time goes in v5:
time: 111 us; the launch traced here: 110 us
  Pallas kernels  62.3 us (56%)
  starting transfers between devices  32.4 us (29%)
  waiting for transfers between devices  10.3 us (9%)
  local copies, waits for them, and re-layouts  3.99 us (4%)
    pallas_call x1, Pallas kernels, remote_pull(): pl.pallas_call(remote_kernel, out_shape=jax.ShapeDtypeStruct((devices, CA...  32.4 us
    all_to_all x2, starting transfers between devices, swap(): return lax.all_to_all(values, AXES, split_axis=0, concat_axis=0, tiled=True)  18.8 us
    pallas_call x1, Pallas kernels, local_pull(): pl.pallas_call(local_kernel, out_shape=jax.ShapeDtypeStruct((BLK_DEV, 4,...  13.8 us
    pallas_call x1, Pallas kernels, node_pull(): pl.pallas_call(node_kernel, out_shape=jax.ShapeDtypeStruct((BLK_DEV, 4, R...  10.3 us
    ppermute x8, starting transfers between devices, group_of(): lax.ppermute(other, 'wide', [(i, i ^ 1) for i in range(groups)])  7.96 us
    ppermute x6, starting transfers between devices, group_of(): lax.ppermute(value, 'narrow', [(i, i ^ flip) for i in range(members)])  5.66 us
    ppermute x6, waiting for transfers between devices, group_of(): lax.ppermute(value, 'narrow', [(i, i ^ flip) for i in range(members)])  5.3 us
    all_to_all x2, waiting for transfers between devices, swap(): return lax.all_to_all(values, AXES, split_axis=0, concat_axis=0, tiled=True)  4.95 us
  transfers between devices with their start and end apart: 16, of which 5 were waited for; matrix products, arithmetic and copies ran while one was open for 1% of the time, Pallas kernels for 51%

profile of v5, /device:TPU:1, one launch (start us, length us, event | category | flops | bytes accessed | tf_op | source)
XLA Modules:
  0.0 109.9 jit_solution(15562909937298615274)
XLA Ops:
  0.0 4.1 %send_blocks.1 = (f32[128,3,4,128]{3,2,1,0:T(4,128)}, s32[128]{0:T(128)}, f32[4,8192]{1,0:T(4,128)}, s32[32,128]{1,0:T(8,128)}, s32[32,128]{1,0:T(8,128)}) custom-call(s32[128]{0:T(128)} %block_ref.1, s32[128]{0:T(128)} %bitcast.16, s32[8,128]{1,0:T(8,128)} %bitcast.14, f32[3,8192]{1,0:T(4,128)} %pos_in.1, f32[1,8192]{1,0:T(1,128)} %bitcast.13, ...), custom_call_target="tpu_custom_call" | custom-call | tf_op jit(solution)/shard_map/send_blocks/pallas_call | solution.py:132
  4.1 1.5 %collective-permute-start.3 = (f32[4,8192]{1,0:T(4,128)}, f32[4,8192]{1,0:T(4,128)S(1)}, u32[]{:S(2)}, u32[]{:S(2)}) collective-permute-start(f32[4,8192]{1,0:T(4,128)} %get-tuple-element.17.pm_ref.refs_0_), channel_id=1, source_target_pairs={{0,16},{16,0},{32,48},{48,32},{64,80},{80,64},{96,112},{112,96},{1... | collective-permute-start | bytes 393224 | tf_op jit(solution)/shard_map/ppermute | solution.py:508
  5.6 2.7 %collective-permute-start.2 = (f32[4,8192]{1,0:T(4,128)}, f32[4,8192]{1,0:T(4,128)S(1)}, u32[]{:S(2)}, u32[]{:S(2)}) collective-permute-start(f32[4,8192]{1,0:T(4,128)} %get-tuple-element.17.pm_ref.refs_0_), channel_id=1, source_target_pairs={{0,5},{1,4},{2,7},{3,6},{4,1},{5,0},{6,3},{7,2},{8,13},{9,12},{10,... | collective-permute-start | bytes 393224 | tf_op jit(solution)/shard_map/ppermute | solution.py:506
  8.2 0.0 collective-permute-start.1
  8.2 0.3 collective-permute-start
  8.5 10.7 %all-to-all-start = ((f32[128,3,4,128]{3,2,1,0:T(4,128)}), f32[128,3,4,128]{3,2,1,0:T(4,128)S(1)}, u32[]{:S(2)}, u32[]{:S(2)}) async-start(f32[128,3,4,128]{3,2,1,0:T(4,128)} %get-tuple-element.18), calls=%async_computation | async-start | bytes 1572864 | tf_op jit(solution)/shard_map/all_to_all | solution.py:485
  19.2 0.0 copy-done.2
  19.2 0.0 copy-done.9
  19.2 13.8 %local_pull.1.local_ref = f32[64,4,128]{2,1,0:T(4,128)S(1)} custom-call(s32[8,64]{1,0:T(8,128)S(1)} %bitcast.12, f32[4,8192]{1,0:T(4,128)S(1)} %copy-done.2), custom_call_target="tpu_custom_call" | custom-call | flops 16000000000 | bytes 1000000 | tf_op jit(solution)/shard_map/local_pull/pallas_call | solution.py:436
  33.1 0.0 copy-start.10
  33.1 0.7 copy-done.10
  33.8 0.0 collective-permute-done.2.refs_3_
  33.8 1.1 collective-permute-start.6
  34.8 1.2 %all-to-all-done = f32[128,3,4,128]{3,2,1,0:T(4,128)S(1)} async-done(((f32[128,3,4,128]{3,2,1,0:T(4,128)}), f32[128,3,4,128]{3,2,1,0:T(4,128)S(1)}, u32[]{:S(2)}, u32[]{:S(2)}) %all-to-all-start) | async-done | bytes 786464 | tf_op jit(solution)/shard_map/all_to_all | solution.py:485
  36.1 0.6 collective-permute-start.9
  36.7 0.0 collective-permute-done.3.refs_4_
  36.7 1.0 collective-permute-start.8
  37.7 0.0 collective-permute-done.1.refs_2_
  37.7 1.1 %collective-permute-start.7 = (f32[128,4,128]{2,1,0:T(4,128)S(1)}, f32[128,4,128]{2,1,0:T(4,128)S(1)}, u32[]{:S(2)}, u32[]{:S(2)}) collective-permute-start(f32[128,4,128]{2,1,0:T(4,128)S(1)} %slice_bitcast_fusion.refs_0_), channel_id=1, source_target_pairs={{0,1},{1,0},{2,3},{3,2},{4,5},{5,4},{6,7},{7,6},{8,9},{9,8},{10,11... | collective-permute-start | bytes 786440 | tf_op jit(solution)/shard_map/ppermute | solution.py:506
  38.8 0.0 collective-permute-done.refs_1_
  38.8 1.5 %collective-permute-start.5 = (f32[4,8192]{1,0:T(4,128)S(1)}, f32[4,8192]{1,0:T(4,128)S(1)}, u32[]{:S(2)}, u32[]{:S(2)}) collective-permute-start(f32[4,8192]{1,0:T(4,128)S(1)} %collective-permute-done.1.refs_2_), channel_id=1, source_target_pairs={{0,16},{16,0},{32,48},{48,32},{64,80},{80,64},{96,112},{112,96},{1... | collective-permute-start | bytes 393224 | tf_op jit(solution)/shard_map/ppermute | solution.py:508
  40.3 0.0 collective-permute-done.6.refs_7_
  40.3 0.1 collective-permute-start.4
  40.4 0.7 fusion
  41.1 0.1 convert_element_type.8.leaf_ref
  41.2 0.1 collective-permute-done.5.refs_6_
  41.3 0.7 copy-done.5
  41.9 0.4 collective-permute-start.10
  42.3 2.0 %collective-permute-done.9.refs_3_ = f32[128,4,128]{2,1,0:T(4,128)S(1)} collective-permute-done((f32[128,4,128]{2,1,0:T(4,128)S(1)}, f32[128,4,128]{2,1,0:T(4,128)S(1)}, u32[]{:S(2)}, u32[]{:S(2)}) %collective-permute-start.9) | collective-permute-done | bytes 262176 | tf_op jit(solution)/shard_map/ppermute | solution.py:506
  44.3 2.5 %collective-permute-start.13 = (f32[128,4,128]{2,1,0:T(4,128)S(1)}, f32[128,4,128]{2,1,0:T(4,128)S(1)}, u32[]{:S(2)}, u32[]{:S(2)}) collective-permute-start(f32[128,4,128]{2,1,0:T(4,128)S(1)} %collective-permute-done.9.refs_3_), channel_id=1, source_target_pairs={{0,16},{16,0},{32,48},{48,32},{64,80},{80,64},{96,112},{112,96},{1... | collective-permute-start | bytes 786440 | tf_op jit(solution)/shard_map/ppermute | solution.py:508
  46.9 3.2 %collective-permute-done.8.refs_2_ = f32[128,4,128]{2,1,0:T(4,128)S(1)} collective-permute-done((f32[128,4,128]{2,1,0:T(4,128)S(1)}, f32[128,4,128]{2,1,0:T(4,128)S(1)}, u32[]{:S(2)}, u32[]{:S(2)}) %collective-permute-start.8) | collective-permute-done | bytes 262176 | tf_op jit(solution)/shard_map/ppermute | solution.py:506
  50.1 0.9 collective-permute-start.12
  51.0 0.0 collective-permute-done.7.refs_1_
  51.0 0.0 collective-permute-start.11
  51.0 0.0 collective-permute-done.4.refs_5_
  51.1 0.9 copy-done.4
  51.9 0.9 copy-done.6
  52.9 32.4 %remote_pull.1 = f32[128,2,4,128]{3,2,1,0:T(4,128)} custom-call(s32[3072]{0:T(1024)S(1)} %convert_element_type.8.leaf_ref, f32[384,4,128]{2,1,0:T(4,128)S(1)} %bitcast.11, f32[4,8192]{1,0:T(4,128)S(1)} %copy-done.2, f32[4,8192]{1,0:T(4,128)S(1)} %collective-permute-done.refs_1_, f32[4,8192]{1,0:T(4,128)S(1)} %collective-permute-done.1.refs_2_, ...), custom_call_target="tpu_custom_call" | custom-call | flops 32000000000 | bytes 10000000 | tf_op jit(solution)/shard_map/remote_pull/pallas_call | solution.py:262
  85.3 8.1 %all-to-all-start.1 = ((f32[128,2,4,128]{3,2,1,0:T(4,128)}), f32[128,2,4,128]{3,2,1,0:T(4,128)S(1)}, u32[]{:S(2)}, u32[]{:S(2)}) async-start(f32[128,2,4,128]{3,2,1,0:T(4,128)} %remote_pull.1), calls=%async_computation.1 | async-start | bytes 1048576 | tf_op jit(solution)/shard_map/all_to_all | solution.py:485
  93.4 0.0 collective-permute-done.10.refs_4_
  93.4 0.0 collective-permute-done.13.refs_7_
  93.4 0.0 collective-permute-done.12.refs_6_
  93.4 0.0 collective-permute-done.11.refs_5_
  93.4 10.3 %node_pull.1.own_ref = f32[64,4,128]{2,1,0:T(4,128)S(1)} custom-call(s32[32,128]{1,0:T(8,128)S(1)} %copy-done.7, s32[32,128]{1,0:T(8,128)S(1)} %copy-done.8, f32[4,8192]{1,0:T(4,128)S(1)} %copy-done.2, f32[64,4,128]{2,1,0:T(4,128)S(1)} %copy-done.11, f32[128,4,128]{2,1,0:T(4,128)S(1)} %slice_bitcast_fusion.refs_0_, ...), custom_call_target="tpu_custom_call" | custom-call | flops 12000000000 | bytes 4000000 | tf_op jit(solution)/shard_map/node_pull/pallas_call | solution.py:392
  103.7 3.8 %all-to-all-done.1 = f32[128,2,4,128]{3,2,1,0:T(4,128)S(1)} async-done(((f32[128,2,4,128]{3,2,1,0:T(4,128)}), f32[128,2,4,128]{3,2,1,0:T(4,128)S(1)}, u32[]{:S(2)}, u32[]{:S(2)}) %all-to-all-start.1) | async-done | bytes 524320 | tf_op jit(solution)/shard_map/all_to_all | solution.py:485
  107.5 0.7 copy-done
  108.1 0.0 copy-done.1
  108.2 1.7 %add_returned.1 = f32[3,8192]{1,0:T(4,128)} custom-call(s32[128]{0:T(128)S(1)} %copy-done.1, s32[128]{0:T(128)S(1)} %copy-done, f32[64,4,128]{2,1,0:T(4,128)S(1)} %node_pull.1.own_ref, f32[256,4,128]{2,1,0:T(4,128)S(1)} %bitcast.9), custom_call_target="tpu_custom_call" | custom-call | tf_op jit(solution)/shard_map/add_returned/pallas_call | solution.py:473
  (16 shorter events, 0.1 us)
Async XLA Ops:
  4.1 32.6 %collective-permute-start.3 = (f32[4,8192]{1,0:T(4,128)}, f32[4,8192]{1,0:T(4,128)S(1)}, u32[]{:S(2)}, u32[]{:S(2)}) collective-permute-start(f32[4,8192]{1,0:T(4,128)} %get-tuple-element.17.pm_ref.refs_0_), channel_id=1, source_target_pairs={{0,16},{16,0},{32,48},{48,32},{64,80},{80,64},{96,112},{112,96},{1... | collective-permute-start | bytes 393224 | tf_op jit(solution)/shard_map/ppermute | solution.py:508
  5.6 28.2 %collective-permute-start.2 = (f32[4,8192]{1,0:T(4,128)}, f32[4,8192]{1,0:T(4,128)S(1)}, u32[]{:S(2)}, u32[]{:S(2)}) collective-permute-start(f32[4,8192]{1,0:T(4,128)} %get-tuple-element.17.pm_ref.refs_0_), channel_id=1, source_target_pairs={{0,5},{1,4},{2,7},{3,6},{4,1},{5,0},{6,3},{7,2},{8,13},{9,12},{10,... | collective-permute-start | bytes 393224 | tf_op jit(solution)/shard_map/ppermute | solution.py:506
  8.2 29.5 %collective-permute-start.1 = (f32[4,8192]{1,0:T(4,128)}, f32[4,8192]{1,0:T(4,128)S(1)}, u32[]{:S(2)}, u32[]{:S(2)}) collective-permute-start(f32[4,8192]{1,0:T(4,128)} %get-tuple-element.17.pm_ref.refs_0_), channel_id=1, source_target_pairs={{0,4},{1,5},{2,6},{3,7},{4,0},{5,1},{6,2},{7,3},{8,12},{9,13},{10,... | collective-permute-start | bytes 393224 | tf_op jit(solution)/shard_map/ppermute | solution.py:506
  8.2 30.6 %collective-permute-start = (f32[4,8192]{1,0:T(4,128)}, f32[4,8192]{1,0:T(4,128)S(1)}, u32[]{:S(2)}, u32[]{:S(2)}) collective-permute-start(f32[4,8192]{1,0:T(4,128)} %get-tuple-element.17.pm_ref.refs_0_), channel_id=1, source_target_pairs={{0,1},{1,0},{2,3},{3,2},{4,5},{5,4},{6,7},{7,6},{8,9},{9,8},{10,11... | collective-permute-start | bytes 393224 | tf_op jit(solution)/shard_map/ppermute | solution.py:506
  8.5 10.7 %copy-start.2 = (f32[4,8192]{1,0:T(4,128)S(1)}, f32[4,8192]{1,0:T(4,128)}, u32[]{:S(2)}) copy-start(f32[4,8192]{1,0:T(4,128)} %get-tuple-element.17.pm_ref.refs_0_) | copy-start | bytes 393220
  8.5 10.7 %copy-start.9 = (s32[64,8]{0,1:T(8,128)S(1)}, s32[64,8]{0,1:T(8,128)}, u32[]{:S(2)}) copy-start(s32[64,8]{0,1:T(8,128)} %param.15) | copy-start | bytes 6148
  8.5 27.5 %all-to-all-start = ((f32[128,3,4,128]{3,2,1,0:T(4,128)}), f32[128,3,4,128]{3,2,1,0:T(4,128)S(1)}, u32[]{:S(2)}, u32[]{:S(2)}) async-start(f32[128,3,4,128]{3,2,1,0:T(4,128)} %get-tuple-element.18), calls=%async_computation | async-start | bytes 1572864 | tf_op jit(solution)/shard_map/all_to_all | solution.py:485
  33.1 0.7 copy-start.10
  33.8 6.5 %collective-permute-start.6 = (f32[4,8192]{1,0:T(4,128)S(1)}, f32[4,8192]{1,0:T(4,128)S(1)}, u32[]{:S(2)}, u32[]{:S(2)}) collective-permute-start(f32[4,8192]{1,0:T(4,128)S(1)} %collective-permute-done.2.refs_3_), channel_id=1, source_target_pairs={{0,16},{16,0},{32,48},{48,32},{64,80},{80,64},{96,112},{112,96},{1... | collective-permute-start | bytes 393224 | tf_op jit(solution)/shard_map/ppermute | solution.py:508
  36.1 8.3 %collective-permute-start.9 = (f32[128,4,128]{2,1,0:T(4,128)S(1)}, f32[128,4,128]{2,1,0:T(4,128)S(1)}, u32[]{:S(2)}, u32[]{:S(2)}) collective-permute-start(f32[128,4,128]{2,1,0:T(4,128)S(1)} %slice_bitcast_fusion.refs_0_), channel_id=1, source_target_pairs={{0,5},{1,4},{2,7},{3,6},{4,1},{5,0},{6,3},{7,2},{8,13},{9,12},{10,... | collective-permute-start | bytes 786440 | tf_op jit(solution)/shard_map/ppermute | solution.py:506
  36.7 13.4 %collective-permute-start.8 = (f32[128,4,128]{2,1,0:T(4,128)S(1)}, f32[128,4,128]{2,1,0:T(4,128)S(1)}, u32[]{:S(2)}, u32[]{:S(2)}) collective-permute-start(f32[128,4,128]{2,1,0:T(4,128)S(1)} %slice_bitcast_fusion.refs_0_), channel_id=1, source_target_pairs={{0,4},{1,5},{2,6},{3,7},{4,0},{5,1},{6,2},{7,3},{8,12},{9,13},{10,... | collective-permute-start | bytes 786440 | tf_op jit(solution)/shard_map/ppermute | solution.py:506
  37.7 13.3 %collective-permute-start.7 = (f32[128,4,128]{2,1,0:T(4,128)S(1)}, f32[128,4,128]{2,1,0:T(4,128)S(1)}, u32[]{:S(2)}, u32[]{:S(2)}) collective-permute-start(f32[128,4,128]{2,1,0:T(4,128)S(1)} %slice_bitcast_fusion.refs_0_), channel_id=1, source_target_pairs={{0,1},{1,0},{2,3},{3,2},{4,5},{5,4},{6,7},{7,6},{8,9},{9,8},{10,11... | collective-permute-start | bytes 786440 | tf_op jit(solution)/shard_map/ppermute | solution.py:506
  38.8 2.5 %collective-permute-start.5 = (f32[4,8192]{1,0:T(4,128)S(1)}, f32[4,8192]{1,0:T(4,128)S(1)}, u32[]{:S(2)}, u32[]{:S(2)}) collective-permute-start(f32[4,8192]{1,0:T(4,128)S(1)} %collective-permute-done.1.refs_2_), channel_id=1, source_target_pairs={{0,16},{16,0},{32,48},{48,32},{64,80},{80,64},{96,112},{112,96},{1... | collective-permute-start | bytes 393224 | tf_op jit(solution)/shard_map/ppermute | solution.py:508
  40.3 0.8 copy-start.3
  40.3 10.8 %collective-permute-start.4 = (f32[4,8192]{1,0:T(4,128)S(1)}, f32[4,8192]{1,0:T(4,128)}, u32[]{:S(2)}, u32[]{:S(2)}) collective-permute-start(f32[4,8192]{1,0:T(4,128)S(1)} %collective-permute-done.refs_1_), channel_id=1, source_target_pairs={{0,16},{16,0},{32,48},{48,32},{64,80},{80,64},{96,112},{112,96},{1... | collective-permute-start | bytes 393224 | tf_op jit(solution)/shard_map/ppermute | solution.py:508
  41.3 0.7 copy-start.5
  41.9 51.4 %collective-permute-start.10 = (f32[128,4,128]{2,1,0:T(4,128)S(1)}, f32[128,4,128]{2,1,0:T(4,128)S(1)}, u32[]{:S(2)}, u32[]{:S(2)}) collective-permute-start(f32[128,4,128]{2,1,0:T(4,128)S(1)} %slice_bitcast_fusion.refs_0_), channel_id=1, source_target_pairs={{0,16},{16,0},{32,48},{48,32},{64,80},{80,64},{96,112},{112,96},{1... | collective-permute-start | bytes 786440 | tf_op jit(solution)/shard_map/ppermute | solution.py:508
  44.3 49.0 %collective-permute-start.13 = (f32[128,4,128]{2,1,0:T(4,128)S(1)}, f32[128,4,128]{2,1,0:T(4,128)S(1)}, u32[]{:S(2)}, u32[]{:S(2)}) collective-permute-start(f32[128,4,128]{2,1,0:T(4,128)S(1)} %collective-permute-done.9.refs_3_), channel_id=1, source_target_pairs={{0,16},{16,0},{32,48},{48,32},{64,80},{80,64},{96,112},{112,96},{1... | collective-permute-start | bytes 786440 | tf_op jit(solution)/shard_map/ppermute | solution.py:508
  50.1 43.3 %collective-permute-start.12 = (f32[128,4,128]{2,1,0:T(4,128)S(1)}, f32[128,4,128]{2,1,0:T(4,128)S(1)}, u32[]{:S(2)}, u32[]{:S(2)}) collective-permute-start(f32[128,4,128]{2,1,0:T(4,128)S(1)} %collective-permute-done.8.refs_2_), channel_id=1, source_target_pairs={{0,16},{16,0},{32,48},{48,32},{64,80},{80,64},{96,112},{112,96},{1... | collective-permute-start | bytes 786440 | tf_op jit(solution)/shard_map/ppermute | solution.py:508
  51.0 42.4 %collective-permute-start.11 = (f32[128,4,128]{2,1,0:T(4,128)S(1)}, f32[128,4,128]{2,1,0:T(4,128)S(1)}, u32[]{:S(2)}, u32[]{:S(2)}) collective-permute-start(f32[128,4,128]{2,1,0:T(4,128)S(1)} %collective-permute-done.7.refs_1_), channel_id=1, source_target_pairs={{0,16},{16,0},{32,48},{48,32},{64,80},{80,64},{96,112},{112,96},{1... | collective-permute-start | bytes 786440 | tf_op jit(solution)/shard_map/ppermute | solution.py:508
  51.0 0.9 copy-start.4
  51.9 0.9 copy-start.6
  85.3 8.2 %copy-start.7 = (s32[32,128]{1,0:T(8,128)S(1)}, s32[32,128]{1,0:T(8,128)}, u32[]{:S(2)}) copy-start(s32[32,128]{1,0:T(8,128)} %get-tuple-element.15.row_ref) | copy-start | bytes 49156
  85.3 8.2 %copy-start.8 = (s32[32,128]{1,0:T(8,128)S(1)}, s32[32,128]{1,0:T(8,128)}, u32[]{:S(2)}) copy-start(s32[32,128]{1,0:T(8,128)} %get-tuple-element.16.part_ref) | copy-start | bytes 49156
  85.3 8.2 %copy-start.11 = (f32[64,4,128]{2,1,0:T(4,128)S(1)}, f32[64,4,128]{2,1,0:T(4,128)}, u32[]{:S(2)}) copy-start(f32[64,4,128]{2,1,0:T(4,128)} %copy-done.10) | copy-start | bytes 393220
  85.3 22.2 %all-to-all-start.1 = ((f32[128,2,4,128]{3,2,1,0:T(4,128)}), f32[128,2,4,128]{3,2,1,0:T(4,128)S(1)}, u32[]{:S(2)}, u32[]{:S(2)}) async-start(f32[128,2,4,128]{3,2,1,0:T(4,128)} %remote_pull.1), calls=%async_computation.1 | async-start | bytes 1048576 | tf_op jit(solution)/shard_map/all_to_all | solution.py:485
  107.5 0.7 copy-start
  107.5 0.7 copy-start.1

commit v6 on v5

--- a/solution.py
+++ b/solution.py
@@ -100,8 +100,15 @@
     for device in range(devices):
         member = (device & 1) + ((device >> 2) & 1) * 2 + ((device >> shift) & 1) * 4
         out_ref[device, CAP] = table[member * each : (member + 1) * each]
-    pm_ref[0:3] = pos_ref[...]
-    pm_ref[3:4] = mass_ref[...]
+    size = pos_ref.shape[1]
+    centre = jnp.sum(pos_ref[...], axis=1, keepdims=True) * (1.0 / size)
+    moved = pos_ref[...] - centre
+    square = jnp.sum(moved * moved, axis=0, keepdims=True)
+    mass = mass_ref[...]
+    pm_ref[:, 0:size] = jnp.concatenate([-2.0 * moved, square, mass * moved, mass], axis=0)
+    pm_ref[:, size : size + ROWS] = jnp.broadcast_to(
+        jnp.concatenate([centre, jnp.zeros((5, 1), f32)], axis=0), (8, ROWS)
+    )
     ids_ref[...] = jnp.concatenate([leaf_ref[...].astype(f32)] * (ROWS // LEAF_N), axis=0).T
 
     def one(step, carry):
@@ -134,7 +141,7 @@
         out_shape=(
             jax.ShapeDtypeStruct((devices, CAP + 1, 4, ROWS), f32),
             jax.ShapeDtypeStruct((EXP_BLK,), jnp.int32),
-            jax.ShapeDtypeStruct((4, BLK_DEV * ROWS), f32),
+            jax.ShapeDtypeStruct((8, BLK_DEV * ROWS + ROWS), f32),
             jax.ShapeDtypeStruct(half, jnp.int32),
             jax.ShapeDtypeStruct(half, jnp.int32),
         ),
@@ -155,47 +162,34 @@
     )(*arguments)
 
 
-def centred_rows(position, centre):
-    moved = position - centre
-    square = jnp.sum(moved * moved, axis=0, keepdims=True)
-    one = jnp.ones_like(square)
-    return moved, square, one, jnp.zeros((3,) + square.shape[1:], f32)
-
-
-def mean_position(pm_ref):
-    return jnp.sum(pm_ref[0:3], axis=1, keepdims=True) * (1.0 / pm_ref.shape[1])
-
-
-def fill_tables(pm_refs, centre, table_ref, weight_ref):
-    chunk = 4
+def fill_tables(source_refs, table_ref, weight_ref):
+    chunk = 32 if len(source_refs) == 1 else 8
+    row = lax.broadcasted_iota(jnp.int32, (16, ROWS), 0)
+    ones = jnp.where(row < 3, 1.0, 0.0).astype(bf16)
 
     def step(index, carry):
         start = pl.multiple_of(index * (chunk * ROWS), chunk * ROWS)
-        for group, pm_ref in enumerate(pm_refs):
-            rows = pm_ref[:, pl.ds(start, chunk * ROWS)]
+        for group, source_ref in enumerate(source_refs):
+            rows = source_ref[:, pl.ds(start, chunk * ROWS)]
             for part in range(chunk):
-                window = rows[:, part * ROWS : (part + 1) * ROWS]
                 leaf = group * BLK_DEV + index * chunk + part
-                moved, square, one, zero = centred_rows(window[0:3], centre)
-                row = jnp.concatenate([-2.0 * moved, one, square, zero], axis=0)
-                high, middle, low = [piece.astype(f32) for piece in split3(row)]
-                blank = jnp.zeros((16, ROWS), f32)
-                half = [high, high, middle, middle, high, low, blank]
-                table_ref[leaf] = jnp.concatenate(half + half, axis=0).T.astype(bf16)
-                pulled = jnp.concatenate([moved, one, zero, zero[0:1]], axis=0) * window[3:4]
-                high, middle, _ = split3(pulled)
+                high, middle, low = split3(rows[:, part * ROWS : (part + 1) * ROWS])
+                half = [high, high, middle, middle, high, low, ones]
+                table_ref[leaf] = jnp.concatenate(half + half, axis=0).T
                 weight_ref[leaf] = jnp.concatenate([high, middle], axis=0)
         return carry
 
     lax.fori_loop(0, BLK_DEV // chunk, step, 0)
 
 
-def pull_block(position, centre, leaves, table_ref, weight_ref, left):
-    moved, square, one, zero = centred_rows(position, centre)
-    row = jnp.concatenate([moved, square + SOFTEN, one, zero], axis=0)
-    high, middle, low = split3(row)
-    blank = jnp.zeros((16, ROWS), bf16)
-    half = jnp.concatenate([high, middle, high, middle, low, high, blank], axis=0)
+def pull_block(moved, leaves, table_ref, weight_ref, left):
+    square = jnp.sum(moved * moved, axis=0, keepdims=True) + SOFTEN
+    one = jnp.ones_like(square)
+    none = jnp.zeros((4, ROWS), f32)
+    high, middle, low = split3(jnp.concatenate([moved, one, none], axis=0))
+    pieces = [piece.astype(f32) for piece in split3(square)]
+    ends = jnp.concatenate(pieces + [none, none, none, one - one], axis=0).astype(bf16)
+    half = jnp.concatenate([high, middle, high, middle, low, high, ends], axis=0)
     none = jnp.zeros_like(half)
     right = jnp.concatenate(
         [jnp.concatenate([half, none], axis=1), jnp.concatenate([none, half], axis=1)], axis=0
@@ -215,7 +209,7 @@
                 jnp.concatenate([weight, weight], axis=1),
                 jnp.concatenate([high[:, lanes], low[:, lanes]], axis=0),
             )
-    total = total[0:8] + total[8:16]
+    total = total[4:8] + total[12:16]
     return total[0:3] - moved * total[3:4]
 
 
@@ -225,7 +219,7 @@
 
 def remote_kernel(leaf_ref, pos_ref, *refs):
     pm_refs = refs[:GROUP]
-    out_ref, list_ref, table_ref, weight_ref = refs[GROUP:]
+    out_ref, list_ref, centre_ref, table_ref, weight_ref = refs[GROUP:]
     devices = pos_ref.shape[0] // (CAP + 1)
 
     def note(index, found):
@@ -240,8 +234,10 @@
     last = list_ref[jnp.maximum(found - 1, 0)]
     for place in range(STEP):
         list_ref[found + place] = last
-    centre = mean_position(pm_refs[0])
-    fill_tables(pm_refs, centre, table_ref, weight_ref)
+    size = BLK_DEV * ROWS
+    for group, pm_ref in enumerate(pm_refs):
+        centre_ref[group] = pm_ref[:, size : size + ROWS]
+    fill_tables(pm_refs, table_ref, weight_ref)
     left = left_lanes()
 
     def step(index, carry):
@@ -249,7 +245,8 @@
         for place in range(STEP):
             slot = list_ref[index * STEP + place]
             leaves = [leaf_ref[slot * LEAF_N + k] for k in range(LEAF_N)]
-            results.append((slot, pull_block(pos_ref[slot][0:3], centre, leaves, table_ref, weight_ref, left)))
+            moved = pos_ref[slot][0:3] - centre_ref[leaves[0] // BLK_DEV][0:3]
+            results.append((slot, pull_block(moved, leaves, table_ref, weight_ref, left)))
         for slot, result in results:
             out_ref[slot // (CAP + 1), slot % (CAP + 1), 0:3] = result
         return carry
@@ -266,10 +263,11 @@
         out_specs=VMEM,
         scratch_shapes=[
             pltpu.SMEM((devices * CAP + STEP,), jnp.int32),
+            pltpu.VMEM((GROUP, 8, ROWS), f32),
             pltpu.VMEM((GROUP * BLK_DEV, ROWS, 128), bf16),
             pltpu.VMEM((GROUP * BLK_DEV, 16, ROWS), bf16),
         ],
-        compiler_params=params(40),
+        compiler_params=params(28),
         cost_estimate=pl.CostEstimate(flops=32 * 10**9, bytes_accessed=10**7, transcendentals=16 * 10**6),
         name="remote_pull",
     )(leaves, visitors, *pms)
@@ -310,8 +308,7 @@
             nodes_ref[pl.ds(first + device * each, 2 * each), :] = jnp.concatenate(
                 [share_ref[device], share_ref[device + 1]], axis=0
             )
-    centre = mean_position(pm_ref)
-    fill_tables((pm_ref,), centre, table_ref, weight_ref)
+    fill_tables((pm_ref,), table_ref, weight_ref)
     left = left_lanes()
 
     row = lax.broadcasted_iota(jnp.int32, (ROWS, 128), 0)
@@ -336,6 +333,7 @@
         fields = turned[0:16]
         for number in range(1, 8):
             fields = jnp.where(part == number, turned[16 * number : 16 * number + 16], fields)
+        centre = pm_ref[:, BLK_DEV * ROWS : BLK_DEV * ROWS + ROWS]
         rows = [-fields[0:1]] + [fields[k + 1 : k + 2] - centre[k : k + 1] for k in range(3)]
         rows += [fields[k : k + 1] for k in range(4, NODE_FIELDS)]
         for number, value in enumerate(rows):
@@ -405,15 +403,14 @@
         + [pltpu.VMEM((NODE_FIELDS, 8, 128), f32)] * 2
         + [pltpu.VMEM((ROWS, 3 * 128), f32)] * 2
         + [pltpu.VMEM((3, ROWS, 256), bf16)] * 2,
-        compiler_params=params(24),
+        compiler_params=params(14),
         cost_estimate=pl.CostEstimate(flops=12 * 10**9, bytes_accessed=4 * 10**6, transcendentals=10**6),
         name="node_pull",
     )(rows, parts, pm, local, *shares)
 
 
 def local_kernel(leaf_ref, pm_ref, out_ref, table_ref, weight_ref):
-    centre = mean_position(pm_ref)
-    fill_tables((pm_ref,), centre, table_ref, weight_ref)
+    fill_tables((pm_ref,), table_ref, weight_ref)
     left = left_lanes()
 
     def step(index, carry):
@@ -422,9 +419,8 @@
             block = index * STEP + place
             start = pl.multiple_of(block * ROWS, ROWS)
             leaves = [leaf_ref[k, block] for k in range(LEAF_N)]
-            results.append(
-                pull_block(pm_ref[0:3, pl.ds(start, ROWS)], centre, leaves, table_ref, weight_ref, left)
-            )
+            moved = pm_ref[0:3, pl.ds(start, ROWS)] * -0.5
+            results.append(pull_block(moved, leaves, table_ref, weight_ref, left))
         for place in range(STEP):
             out_ref[index * STEP + place, 0:3] = results[place]
         return carry
@@ -442,7 +438,7 @@
             pltpu.VMEM((BLK_DEV, ROWS, 128), bf16),
             pltpu.VMEM((BLK_DEV, 16, ROWS), bf16),
         ],
-        compiler_params=params(24),
+        compiler_params=params(10),
         cost_estimate=pl.CostEstimate(flops=16 * 10**9, bytes_accessed=10**6, transcendentals=8 * 10**6),
         name="local_pull",
     )(local_leaves, pm)
@@ -501,11 +497,12 @@
     members = lax.axis_size("narrow")
     devices = groups * members
 
-    def group_of(value):
-        found = [value] + [
-            lax.ppermute(value, "narrow", [(i, i ^ flip) for i in range(members)]) for flip in (1, 4, 5)
-        ]
-        return found + [lax.ppermute(other, "wide", [(i, i ^ 1) for i in range(groups)]) for other in found]
+    def same_core(value):
+        flips = [[(i, i ^ flip) for i in range(members)] for flip in (1, 4, 5)]
+        return [value] + [lax.ppermute(value, "narrow", flip) for flip in flips]
+
+    def other_core(values):
+        return values + [lax.ppermute(value, "wide", [(i, i ^ 1) for i in range(groups)]) for value in values]
 
     outgoing, slots, pm, rows, parts = send_blocks(
         devices,
@@ -520,16 +517,17 @@
         node_lists,
     )
     arrived = swap(outgoing)
-    pms = group_of(pm)
+    pms = other_core(same_core(pm))
     local = local_pull(local_leaves.T, pm)
     arrived, local = lax.optimization_barrier((arrived, local))
 
-    shares = group_of(arrived[:, CAP])
+    shares = same_core(arrived[:, CAP])
     visitors = arrived.reshape(devices * (CAP + 1), 4, ROWS)
     visitor_leaves = visitors[:, 3, 0:LEAF_N].astype(jnp.int32).reshape(-1)
     pulls = remote_pull(visitor_leaves, visitors, pms)
-    pulls, local = lax.optimization_barrier((pulls, local))
+    pulls, local, shares = lax.optimization_barrier((pulls, local, shares))
     back = swap(pulls)
+    shares = other_core(shares)
     own = node_pull(rows, parts, pm, local, shares)
     return add_returned(slots, export_block, own, back.reshape(devices * CAP, 4, ROWS))
 

time: 111 us -> 99 us (0.89); the launches traced: 110 us -> 99.7 us
  Pallas kernels: 62.3 us -> 54.3 us
  starting transfers between devices: 32.4 us -> 36.1 us
  local copies, waits for them, and re-layouts: 3.99 us -> 0.88 us
  waiting for transfers between devices: 10.3 us -> 7.61 us
    pallas_call x1, Pallas kernels: 32.4 us -> 26.7 us  [remote_pull(): pl.pallas_call(remote_kernel, out_shape=jax.ShapeDtypeStruct((devices, CA...]
    all_to_all x2, starting transfers between devices: 18.8 us -> 24.5 us  [swap(): return lax.all_to_all(values, AXES, split_axis=0, concat_axis=0, tiled=True)]
    ppermute x14, waiting for transfers between devices: 5.38 us -> 0.04 us  [the longest x8 0.02 us: other_core(): lax.ppermute(value, 'wide', [(i, i ^ 1) for i in range(groups)])]
    unnamed x24 -> x16, local copies, waits for them, and re-layouts: 3.81 us -> 0.7 us
    all_to_all x2, waiting for transfers between devices: 4.95 us -> 7.57 us  [swap(): return lax.all_to_all(values, AXES, split_axis=0, concat_axis=0, tiled=True)]
    ppermute x14, starting transfers between devices: 13.6 us -> 11.6 us  [the longest x6 6.49 us: same_core(): return [value] + [lax.ppermute(value, 'narrow', flip) for flip in flips]]
    pallas_call x1, Pallas kernels: 13.8 us -> 12.4 us  [local_pull(): pl.pallas_call(local_kernel, out_shape=jax.ShapeDtypeStruct((BLK_DEV, 4,...]
    pallas_call x1, Pallas kernels: 10.3 us -> 9.12 us  [node_pull(): pl.pallas_call(node_kernel, out_shape=jax.ShapeDtypeStruct((BLK_DEV, 4, R...]
  transfers between devices with their start and end apart: 16 -> 16, of which waited for: 5 -> 2; matrix products, arithmetic and copies ran while one was open for 1% -> 1% of each run, Pallas kernels for 51% -> 48%
where the time goes in v6:
time: 99 us; the launch traced here: 99.7 us
  Pallas kernels  54.3 us (55%)
  starting transfers between devices  36.1 us (36%)
  waiting for transfers between devices  7.61 us (8%)
    pallas_call x1, Pallas kernels, remote_pull(): pl.pallas_call(remote_kernel, out_shape=jax.ShapeDtypeStruct((devices, CA...  26.7 us
    all_to_all x2, starting transfers between devices, swap(): return lax.all_to_all(values, AXES, split_axis=0, concat_axis=0, tiled=True)  24.5 us
    pallas_call x1, Pallas kernels, local_pull(): pl.pallas_call(local_kernel, out_shape=jax.ShapeDtypeStruct((BLK_DEV, 4,...  12.4 us
    pallas_call x1, Pallas kernels, node_pull(): pl.pallas_call(node_kernel, out_shape=jax.ShapeDtypeStruct((BLK_DEV, 4, R...  9.12 us
    all_to_all x2, waiting for transfers between devices, swap(): return lax.all_to_all(values, AXES, split_axis=0, concat_axis=0, tiled=True)  7.57 us
    ppermute x6, starting transfers between devices, same_core(): return [value] + [lax.ppermute(value, 'narrow', flip) for flip in flips]  6.49 us
    ppermute x8, starting transfers between devices, other_core(): lax.ppermute(value, 'wide', [(i, i ^ 1) for i in range(groups)])  5.07 us
    pallas_call x1, Pallas kernels, send_blocks(): pl.pallas_call(send_kernel, out_shape=(jax.ShapeDtypeStruct((devices, CAP...  4.36 us
  transfers between devices with their start and end apart: 16, of which 2 were waited for; matrix products, arithmetic and copies ran while one was open for 1% of the time, Pallas kernels for 48%

profile of v6, /device:TPU:1, one launch (start us, length us, event | category | flops | bytes accessed | tf_op | source)
XLA Modules:
  0.0 99.7 jit_solution(220303889794062010)
XLA Ops:
  0.0 4.4 %send_blocks.1 = (f32[128,3,4,128]{3,2,1,0:T(4,128)}, s32[128]{0:T(128)}, f32[8,8320]{1,0:T(8,128)}, s32[32,128]{1,0:T(8,128)}, s32[32,128]{1,0:T(8,128)}) custom-call(s32[128]{0:T(128)} %block_ref.1, s32[128]{0:T(128)} %bitcast.16, s32[8,128]{1,0:T(8,128)} %bitcast.14, f32[3,8192]{1,0:T(4,128)} %pos_in.1, f32[1,8192]{1,0:T(1,128)} %bitcast.13, ...), custom_call_target="tpu_custom_call" | custom-call | tf_op jit(solution)/shard_map/send_blocks/pallas_call | solution.py:139
  4.4 2.1 %collective-permute-start = (f32[8,8320]{1,0:T(8,128)}, f32[8,8320]{1,0:T(8,128)S(1)}, u32[]{:S(2)}, u32[]{:S(2)}) collective-permute-start(f32[8,8320]{1,0:T(8,128)} %get-tuple-element.21.pm_ref.refs_0_), channel_id=1, source_target_pairs={{0,1},{1,0},{2,3},{3,2},{4,5},{5,4},{6,7},{7,6},{8,9},{9,8},{10,11... | collective-permute-start | bytes 798728 | tf_op jit(solution)/shard_map/ppermute | solution.py:502
  6.5 1.6 %collective-permute-start.1 = (f32[8,8320]{1,0:T(8,128)}, f32[8,8320]{1,0:T(8,128)S(1)}, u32[]{:S(2)}, u32[]{:S(2)}) collective-permute-start(f32[8,8320]{1,0:T(8,128)} %get-tuple-element.21.pm_ref.refs_0_), channel_id=1, source_target_pairs={{0,4},{1,5},{2,6},{3,7},{4,0},{5,1},{6,2},{7,3},{8,12},{9,13},{10,... | collective-permute-start | bytes 798728 | tf_op jit(solution)/shard_map/ppermute | solution.py:502
  8.1 0.0 collective-permute-start.2
  8.1 1.2 %collective-permute-start.3 = (f32[8,8320]{1,0:T(8,128)}, f32[8,8320]{1,0:T(8,128)S(1)}, u32[]{:S(2)}, u32[]{:S(2)}) collective-permute-start(f32[8,8320]{1,0:T(8,128)} %get-tuple-element.21.pm_ref.refs_0_), channel_id=1, source_target_pairs={{0,16},{16,0},{32,48},{48,32},{64,80},{80,64},{96,112},{112,96},{1... | collective-permute-start | bytes 798728 | tf_op jit(solution)/shard_map/ppermute | solution.py:505
  9.4 10.2 %all-to-all-start = ((f32[128,3,4,128]{3,2,1,0:T(4,128)}), f32[128,3,4,128]{3,2,1,0:T(4,128)S(1)}, u32[]{:S(2)}, u32[]{:S(2)}) async-start(f32[128,3,4,128]{3,2,1,0:T(4,128)} %get-tuple-element.22), calls=%async_computation | async-start | bytes 1572864 | tf_op jit(solution)/shard_map/all_to_all | solution.py:481
  19.6 0.0 copy-done.2
  19.6 0.0 copy-done.5
  19.6 12.4 %local_pull.1.local_ref = f32[64,4,128]{2,1,0:T(4,128)S(1)} custom-call(s32[8,64]{1,0:T(8,128)S(1)} %bitcast.12, f32[8,8320]{1,0:T(8,128)S(1)} %copy-done.2), custom_call_target="tpu_custom_call" | custom-call | flops 16000000000 | bytes 1000000 | tf_op jit(solution)/shard_map/local_pull/pallas_call | solution.py:432
  32.0 0.0 copy-start.6
  32.0 0.0 collective-permute-done.refs_1_
  32.0 1.1 %collective-permute-start.4 = (f32[8,8320]{1,0:T(8,128)S(1)}, f32[8,8320]{1,0:T(8,128)S(1)}, u32[]{:S(2)}, u32[]{:S(2)}) collective-permute-start(f32[8,8320]{1,0:T(8,128)S(1)} %collective-permute-done.refs_1_), channel_id=1, source_target_pairs={{0,16},{16,0},{32,48},{48,32},{64,80},{80,64},{96,112},{112,96},{1... | collective-permute-start | bytes 798728 | tf_op jit(solution)/shard_map/ppermute | solution.py:505
  33.2 0.0 collective-permute-done.1.refs_2_
  33.2 0.1 collective-permute-start.5
  33.3 0.0 collective-permute-done.2.refs_3_
  33.3 0.4 collective-permute-start.6
  33.7 2.6 %all-to-all-done = f32[128,3,4,128]{3,2,1,0:T(4,128)S(1)} async-done(((f32[128,3,4,128]{3,2,1,0:T(4,128)}), f32[128,3,4,128]{3,2,1,0:T(4,128)S(1)}, u32[]{:S(2)}, u32[]{:S(2)}) %all-to-all-start) | async-done | bytes 786464 | tf_op jit(solution)/shard_map/all_to_all | solution.py:481
  36.3 0.7 fusion
  37.0 0.0 copy-done.6
  37.1 0.1 convert_element_type.8.leaf_ref
  37.2 0.4 collective-permute-start.7
  37.7 0.0 collective-permute-done.3.refs_4_
  37.7 0.0 collective-permute-start.8
  37.7 0.0 collective-permute-done.4.refs_5_
  37.7 2.3 %collective-permute-start.9 = (f32[128,4,128]{2,1,0:T(4,128)S(1)}, f32[128,4,128]{2,1,0:T(4,128)}, u32[]{:S(2)}, u32[]{:S(2)}) collective-permute-start(f32[128,4,128]{2,1,0:T(4,128)S(1)} %slice_bitcast_fusion.refs_0_), channel_id=1, source_target_pairs={{0,5},{1,4},{2,7},{3,6},{4,1},{5,0},{6,3},{7,2},{8,13},{9,12},{10,... | collective-permute-start | bytes 786440 | tf_op jit(solution)/shard_map/ppermute | solution.py:502
  40.0 0.0 collective-permute-done.5.refs_6_
  40.0 0.0 collective-permute-done.6.refs_7_
  40.0 26.7 %remote_pull.1 = f32[128,2,4,128]{3,2,1,0:T(4,128)} custom-call(s32[3072]{0:T(1024)S(1)} %convert_element_type.8.leaf_ref, f32[384,4,128]{2,1,0:T(4,128)S(1)} %bitcast.11, f32[8,8320]{1,0:T(8,128)S(1)} %copy-done.2, f32[8,8320]{1,0:T(8,128)S(1)} %collective-permute-done.refs_1_, f32[8,8320]{1,0:T(8,128)S(1)} %collective-permute-done.1.refs_2_, ...), custom_call_target="tpu_custom_call" | custom-call | flops 32000000000 | bytes 10000000 | tf_op jit(solution)/shard_map/remote_pull/pallas_call | solution.py:259
  66.7 0.0 collective-permute-done.7.refs_1_
  66.7 0.0 collective-permute-done.8.refs_2_
  66.7 0.0 collective-permute-done.9.refs_3_
  66.7 1.6 %collective-permute-start.10 = (f32[128,4,128]{2,1,0:T(4,128)S(1)}, f32[128,4,128]{2,1,0:T(4,128)S(1)}, u32[]{:S(2)}, u32[]{:S(2)}) collective-permute-start(f32[128,4,128]{2,1,0:T(4,128)S(1)} %slice_bitcast_fusion.refs_0_), channel_id=1, source_target_pairs={{0,16},{16,0},{32,48},{48,32},{64,80},{80,64},{96,112},{112,96},{1... | collective-permute-start | bytes 786440 | tf_op jit(solution)/shard_map/ppermute | solution.py:505
  68.3 0.1 collective-permute-start.11
  68.3 0.4 collective-permute-start.12
  68.8 0.1 collective-permute-start.13
  68.9 14.4 %all-to-all-start.1 = ((f32[128,2,4,128]{3,2,1,0:T(4,128)}), f32[128,2,4,128]{3,2,1,0:T(4,128)S(1)}, u32[]{:S(2)}, u32[]{:S(2)}) async-start(f32[128,2,4,128]{3,2,1,0:T(4,128)} %remote_pull.1), calls=%async_computation.1 | async-start | bytes 1048576 | tf_op jit(solution)/shard_map/all_to_all | solution.py:481
  83.2 0.0 collective-permute-done.10.refs_4_
  83.2 0.0 collective-permute-done.11.refs_5_
  83.2 0.0 collective-permute-done.12.refs_6_
  83.3 0.0 collective-permute-done.13.refs_7_
  83.3 0.0 copy-done.3
  83.3 0.0 copy-done.4
  83.3 0.0 copy-done.7
  83.3 9.1 %node_pull.1.own_ref = f32[64,4,128]{2,1,0:T(4,128)S(1)} custom-call(s32[32,128]{1,0:T(8,128)S(1)} %copy-done.3, s32[32,128]{1,0:T(8,128)S(1)} %copy-done.4, f32[8,8320]{1,0:T(8,128)S(1)} %copy-done.2, f32[64,4,128]{2,1,0:T(4,128)S(1)} %copy-done.7, f32[128,4,128]{2,1,0:T(4,128)S(1)} %slice_bitcast_fusion.refs_0_, ...), custom_call_target="tpu_custom_call" | custom-call | flops 12000000000 | bytes 4000000 | tf_op jit(solution)/shard_map/node_pull/pallas_call | solution.py:390
  92.4 4.9 %all-to-all-done.1 = f32[128,2,4,128]{3,2,1,0:T(4,128)S(1)} async-done(((f32[128,2,4,128]{3,2,1,0:T(4,128)}), f32[128,2,4,128]{3,2,1,0:T(4,128)S(1)}, u32[]{:S(2)}, u32[]{:S(2)}) %all-to-all-start.1) | async-done | bytes 524320 | tf_op jit(solution)/shard_map/all_to_all | solution.py:481
  97.3 0.7 copy-done
  98.0 0.0 copy-done.1
  98.0 1.7 %add_returned.1 = f32[3,8192]{1,0:T(4,128)} custom-call(s32[128]{0:T(128)S(1)} %copy-done.1, s32[128]{0:T(128)S(1)} %copy-done, f32[64,4,128]{2,1,0:T(4,128)S(1)} %node_pull.1.own_ref, f32[256,4,128]{2,1,0:T(4,128)S(1)} %bitcast.9), custom_call_target="tpu_custom_call" | custom-call | tf_op jit(solution)/shard_map/add_returned/pallas_call | solution.py:469
  (8 shorter events, 0.1 us)
Async XLA Ops:
  4.4 27.7 %collective-permute-start = (f32[8,8320]{1,0:T(8,128)}, f32[8,8320]{1,0:T(8,128)S(1)}, u32[]{:S(2)}, u32[]{:S(2)}) collective-permute-start(f32[8,8320]{1,0:T(8,128)} %get-tuple-element.21.pm_ref.refs_0_), channel_id=1, source_target_pairs={{0,1},{1,0},{2,3},{3,2},{4,5},{5,4},{6,7},{7,6},{8,9},{9,8},{10,11... | collective-permute-start | bytes 798728 | tf_op jit(solution)/shard_map/ppermute | solution.py:502
  6.5 26.7 %collective-permute-start.1 = (f32[8,8320]{1,0:T(8,128)}, f32[8,8320]{1,0:T(8,128)S(1)}, u32[]{:S(2)}, u32[]{:S(2)}) collective-permute-start(f32[8,8320]{1,0:T(8,128)} %get-tuple-element.21.pm_ref.refs_0_), channel_id=1, source_target_pairs={{0,4},{1,5},{2,6},{3,7},{4,0},{5,1},{6,2},{7,3},{8,12},{9,13},{10,... | collective-permute-start | bytes 798728 | tf_op jit(solution)/shard_map/ppermute | solution.py:502
  8.1 25.2 %collective-permute-start.2 = (f32[8,8320]{1,0:T(8,128)}, f32[8,8320]{1,0:T(8,128)S(1)}, u32[]{:S(2)}, u32[]{:S(2)}) collective-permute-start(f32[8,8320]{1,0:T(8,128)} %get-tuple-element.21.pm_ref.refs_0_), channel_id=1, source_target_pairs={{0,5},{1,4},{2,7},{3,6},{4,1},{5,0},{6,3},{7,2},{8,13},{9,12},{10,... | collective-permute-start | bytes 798728 | tf_op jit(solution)/shard_map/ppermute | solution.py:502
  8.1 29.6 %collective-permute-start.3 = (f32[8,8320]{1,0:T(8,128)}, f32[8,8320]{1,0:T(8,128)S(1)}, u32[]{:S(2)}, u32[]{:S(2)}) collective-permute-start(f32[8,8320]{1,0:T(8,128)} %get-tuple-element.21.pm_ref.refs_0_), channel_id=1, source_target_pairs={{0,16},{16,0},{32,48},{48,32},{64,80},{80,64},{96,112},{112,96},{1... | collective-permute-start | bytes 798728 | tf_op jit(solution)/shard_map/ppermute | solution.py:505
  9.4 10.2 %copy-start.2 = (f32[8,8320]{1,0:T(8,128)S(1)}, f32[8,8320]{1,0:T(8,128)}, u32[]{:S(2)}) copy-start(f32[8,8320]{1,0:T(8,128)} %get-tuple-element.21.pm_ref.refs_0_) | copy-start | bytes 798724
  9.4 10.2 %copy-start.5 = (s32[64,8]{0,1:T(8,128)S(1)}, s32[64,8]{0,1:T(8,128)}, u32[]{:S(2)}) copy-start(s32[64,8]{0,1:T(8,128)} %param.15) | copy-start | bytes 6148
  9.4 27.0 %all-to-all-start = ((f32[128,3,4,128]{3,2,1,0:T(4,128)}), f32[128,3,4,128]{3,2,1,0:T(4,128)S(1)}, u32[]{:S(2)}, u32[]{:S(2)}) async-start(f32[128,3,4,128]{3,2,1,0:T(4,128)} %get-tuple-element.22), calls=%async_computation | async-start | bytes 1572864 | tf_op jit(solution)/shard_map/all_to_all | solution.py:481
  32.0 5.0 %copy-start.6 = (f32[64,4,128]{2,1,0:T(4,128)}, f32[64,4,128]{2,1,0:T(4,128)S(1)}, u32[]{:S(2)}) copy-start(f32[64,4,128]{2,1,0:T(4,128)S(1)} %local_pull.1.local_ref) | copy-start | bytes 393220
  32.0 5.7 %collective-permute-start.4 = (f32[8,8320]{1,0:T(8,128)S(1)}, f32[8,8320]{1,0:T(8,128)S(1)}, u32[]{:S(2)}, u32[]{:S(2)}) collective-permute-start(f32[8,8320]{1,0:T(8,128)S(1)} %collective-permute-done.refs_1_), channel_id=1, source_target_pairs={{0,16},{16,0},{32,48},{48,32},{64,80},{80,64},{96,112},{112,96},{1... | collective-permute-start | bytes 798728 | tf_op jit(solution)/shard_map/ppermute | solution.py:505
  33.2 6.8 %collective-permute-start.5 = (f32[8,8320]{1,0:T(8,128)S(1)}, f32[8,8320]{1,0:T(8,128)S(1)}, u32[]{:S(2)}, u32[]{:S(2)}) collective-permute-start(f32[8,8320]{1,0:T(8,128)S(1)} %collective-permute-done.1.refs_2_), channel_id=1, source_target_pairs={{0,16},{16,0},{32,48},{48,32},{64,80},{80,64},{96,112},{112,96},{1... | collective-permute-start | bytes 798728 | tf_op jit(solution)/shard_map/ppermute | solution.py:505
  33.3 6.7 %collective-permute-start.6 = (f32[8,8320]{1,0:T(8,128)S(1)}, f32[8,8320]{1,0:T(8,128)S(1)}, u32[]{:S(2)}, u32[]{:S(2)}) collective-permute-start(f32[8,8320]{1,0:T(8,128)S(1)} %collective-permute-done.2.refs_3_), channel_id=1, source_target_pairs={{0,16},{16,0},{32,48},{48,32},{64,80},{80,64},{96,112},{112,96},{1... | collective-permute-start | bytes 798728 | tf_op jit(solution)/shard_map/ppermute | solution.py:505
  37.2 29.4 %collective-permute-start.7 = (f32[128,4,128]{2,1,0:T(4,128)S(1)}, f32[128,4,128]{2,1,0:T(4,128)S(1)}, u32[]{:S(2)}, u32[]{:S(2)}) collective-permute-start(f32[128,4,128]{2,1,0:T(4,128)S(1)} %slice_bitcast_fusion.refs_0_), channel_id=1, source_target_pairs={{0,1},{1,0},{2,3},{3,2},{4,5},{5,4},{6,7},{7,6},{8,9},{9,8},{10,11... | collective-permute-start | bytes 786440 | tf_op jit(solution)/shard_map/ppermute | solution.py:502
  37.7 29.0 %collective-permute-start.8 = (f32[128,4,128]{2,1,0:T(4,128)S(1)}, f32[128,4,128]{2,1,0:T(4,128)}, u32[]{:S(2)}, u32[]{:S(2)}) collective-permute-start(f32[128,4,128]{2,1,0:T(4,128)S(1)} %slice_bitcast_fusion.refs_0_), channel_id=1, source_target_pairs={{0,4},{1,5},{2,6},{3,7},{4,0},{5,1},{6,2},{7,3},{8,12},{9,13},{10,... | collective-permute-start | bytes 786440 | tf_op jit(solution)/shard_map/ppermute | solution.py:502
  37.7 29.0 %collective-permute-start.9 = (f32[128,4,128]{2,1,0:T(4,128)S(1)}, f32[128,4,128]{2,1,0:T(4,128)}, u32[]{:S(2)}, u32[]{:S(2)}) collective-permute-start(f32[128,4,128]{2,1,0:T(4,128)S(1)} %slice_bitcast_fusion.refs_0_), channel_id=1, source_target_pairs={{0,5},{1,4},{2,7},{3,6},{4,1},{5,0},{6,3},{7,2},{8,13},{9,12},{10,... | collective-permute-start | bytes 786440 | tf_op jit(solution)/shard_map/ppermute | solution.py:502
  66.6 16.6 %copy-start.3 = (s32[32,128]{1,0:T(8,128)S(1)}, s32[32,128]{1,0:T(8,128)}, u32[]{:S(2)}) copy-start(s32[32,128]{1,0:T(8,128)} %get-tuple-element.19.row_ref) | copy-start | bytes 49156
  66.7 16.6 %copy-start.4 = (s32[32,128]{1,0:T(8,128)S(1)}, s32[32,128]{1,0:T(8,128)}, u32[]{:S(2)}) copy-start(s32[32,128]{1,0:T(8,128)} %get-tuple-element.20.part_ref) | copy-start | bytes 49156
  66.7 16.6 %copy-start.7 = (f32[64,4,128]{2,1,0:T(4,128)S(1)}, f32[64,4,128]{2,1,0:T(4,128)}, u32[]{:S(2)}) copy-start(f32[64,4,128]{2,1,0:T(4,128)} %copy-done.6) | copy-start | bytes 393220
  66.7 16.5 %collective-permute-start.10 = (f32[128,4,128]{2,1,0:T(4,128)S(1)}, f32[128,4,128]{2,1,0:T(4,128)S(1)}, u32[]{:S(2)}, u32[]{:S(2)}) collective-permute-start(f32[128,4,128]{2,1,0:T(4,128)S(1)} %slice_bitcast_fusion.refs_0_), channel_id=1, source_target_pairs={{0,16},{16,0},{32,48},{48,32},{64,80},{80,64},{96,112},{112,96},{1... | collective-permute-start | bytes 786440 | tf_op jit(solution)/shard_map/ppermute | solution.py:505
  68.3 15.0 %collective-permute-start.11 = (f32[128,4,128]{2,1,0:T(4,128)S(1)}, f32[128,4,128]{2,1,0:T(4,128)S(1)}, u32[]{:S(2)}, u32[]{:S(2)}) collective-permute-start(f32[128,4,128]{2,1,0:T(4,128)S(1)} %collective-permute-done.7.refs_1_), channel_id=1, source_target_pairs={{0,16},{16,0},{32,48},{48,32},{64,80},{80,64},{96,112},{112,96},{1... | collective-permute-start | bytes 786440 | tf_op jit(solution)/shard_map/ppermute | solution.py:505
  68.3 14.9 %collective-permute-start.12 = (f32[128,4,128]{2,1,0:T(4,128)}, f32[128,4,128]{2,1,0:T(4,128)S(1)}, u32[]{:S(2)}, u32[]{:S(2)}) collective-permute-start(f32[128,4,128]{2,1,0:T(4,128)} %collective-permute-done.8.refs_2_), channel_id=1, source_target_pairs={{0,16},{16,0},{32,48},{48,32},{64,80},{80,64},{96,112},{112,96},{1... | collective-permute-start | bytes 786440 | tf_op jit(solution)/shard_map/ppermute | solution.py:505
  68.8 14.5 %collective-permute-start.13 = (f32[128,4,128]{2,1,0:T(4,128)}, f32[128,4,128]{2,1,0:T(4,128)S(1)}, u32[]{:S(2)}, u32[]{:S(2)}) collective-permute-start(f32[128,4,128]{2,1,0:T(4,128)} %collective-permute-done.9.refs_3_), channel_id=1, source_target_pairs={{0,16},{16,0},{32,48},{48,32},{64,80},{80,64},{96,112},{112,96},{1... | collective-permute-start | bytes 786440 | tf_op jit(solution)/shard_map/ppermute | solution.py:505
  68.9 28.5 %all-to-all-start.1 = ((f32[128,2,4,128]{3,2,1,0:T(4,128)}), f32[128,2,4,128]{3,2,1,0:T(4,128)S(1)}, u32[]{:S(2)}, u32[]{:S(2)}) async-start(f32[128,2,4,128]{3,2,1,0:T(4,128)} %remote_pull.1), calls=%async_computation.1 | async-start | bytes 1048576 | tf_op jit(solution)/shard_map/all_to_all | solution.py:481
  97.3 0.7 copy-start
  97.3 0.7 copy-start.1

commit v7 on v6

--- a/solution.py
+++ b/solution.py
@@ -124,6 +124,7 @@
             target = base + (member & 1) + (member & 2) * 2 + ((member >> 2) << shift)
             distance = (side + up * 2 + core * 4) ^ member
             slot_ref[export] = target * CAP + slot
+            slot_ref[EXP_BLK + export] = block_ref[export]
             start = pl.multiple_of(block_ref[export] * ROWS, ROWS)
             out_ref[target, slot, 0:3, :] = pos_ref[:, pl.ds(start, ROWS)]
             ids = ids_ref[pl.ds(export, 1), 0:LEAF_N]
@@ -140,7 +141,7 @@
         send_kernel,
         out_shape=(
             jax.ShapeDtypeStruct((devices, CAP + 1, 4, ROWS), f32),
-            jax.ShapeDtypeStruct((EXP_BLK,), jnp.int32),
+            jax.ShapeDtypeStruct((2 * EXP_BLK,), jnp.int32),
             jax.ShapeDtypeStruct((8, BLK_DEV * ROWS + ROWS), f32),
             jax.ShapeDtypeStruct(half, jnp.int32),
             jax.ShapeDtypeStruct(half, jnp.int32),
@@ -217,34 +218,37 @@
     return lax.broadcasted_iota(jnp.int32, (ROWS, 128), 1) < 64
 
 
-def remote_kernel(leaf_ref, pos_ref, *refs):
+def remote_kernel(pos_ref, *refs):
     pm_refs = refs[:GROUP]
-    out_ref, list_ref, centre_ref, table_ref, weight_ref = refs[GROUP:]
+    out_ref, list_ref, leaf_ref, centre_ref, table_ref, weight_ref, sem = refs[GROUP:]
     devices = pos_ref.shape[0] // (CAP + 1)
+    copy = pltpu.make_async_copy(pos_ref.at[:, 3], leaf_ref, sem)
+    copy.start()
+    size = BLK_DEV * ROWS
+    for group, pm_ref in enumerate(pm_refs):
+        centre_ref[group] = pm_ref[:, size : size + ROWS]
+    fill_tables(pm_refs, table_ref, weight_ref)
+    copy.wait()
 
     def note(index, found):
         for part in range(8):
             for slot in range(CAP):
                 slot = (index * 8 + part) * (CAP + 1) + slot
                 list_ref[found] = slot
-                found = found + jnp.where(leaf_ref[slot * LEAF_N] >= 0, 1, 0)
+                found = found + jnp.where(leaf_ref[slot, 0] >= 0.0, 1, 0)
         return found
 
     found = lax.fori_loop(0, devices // 8, note, 0)
     last = list_ref[jnp.maximum(found - 1, 0)]
     for place in range(STEP):
         list_ref[found + place] = last
-    size = BLK_DEV * ROWS
-    for group, pm_ref in enumerate(pm_refs):
-        centre_ref[group] = pm_ref[:, size : size + ROWS]
-    fill_tables(pm_refs, table_ref, weight_ref)
     left = left_lanes()
 
     def step(index, carry):
         results = []
         for place in range(STEP):
             slot = list_ref[index * STEP + place]
-            leaves = [leaf_ref[slot * LEAF_N + k] for k in range(LEAF_N)]
+            leaves = [leaf_ref[slot, k].astype(jnp.int32) for k in range(LEAF_N)]
             moved = pos_ref[slot][0:3] - centre_ref[leaves[0] // BLK_DEV][0:3]
             results.append((slot, pull_block(moved, leaves, table_ref, weight_ref, left)))
         for slot, result in results:
@@ -254,23 +258,25 @@
     lax.fori_loop(0, (found + STEP - 1) // STEP, step, 0)
 
 
-def remote_pull(leaves, visitors, pms):
+def remote_pull(visitors, pms):
     devices = visitors.shape[0] // (CAP + 1)
     return pl.pallas_call(
         remote_kernel,
         out_shape=jax.ShapeDtypeStruct((devices, CAP, 4, ROWS), f32),
-        in_specs=[SMEM] + [VMEM] * (1 + GROUP),
+        in_specs=[VMEM] * (1 + GROUP),
         out_specs=VMEM,
         scratch_shapes=[
             pltpu.SMEM((devices * CAP + STEP,), jnp.int32),
+            pltpu.SMEM((visitors.shape[0], ROWS), f32),
             pltpu.VMEM((GROUP, 8, ROWS), f32),
             pltpu.VMEM((GROUP * BLK_DEV, ROWS, 128), bf16),
             pltpu.VMEM((GROUP * BLK_DEV, 16, ROWS), bf16),
+            pltpu.SemaphoreType.DMA,
         ],
         compiler_params=params(28),
         cost_estimate=pl.CostEstimate(flops=32 * 10**9, bytes_accessed=10**7, transcendentals=16 * 10**6),
         name="remote_pull",
-    )(leaves, visitors, *pms)
+    )(visitors, *pms)
 
 
 def node_sum(place, fields):
@@ -444,7 +450,7 @@
     )(local_leaves, pm)
 
 
-def add_kernel(slot_ref, block_ref, own_ref, back_ref, out_ref, *sum_refs):
+def add_kernel(slot_ref, own_ref, back_ref, out_ref, *sum_refs):
     parts = len(sum_refs)
     for part in range(1, parts):
         sum_refs[part][...] = jnp.zeros_like(sum_refs[part])
@@ -453,7 +459,7 @@
     def one(step, carry):
         for part in range(parts):
             export = step * parts + part
-            block = block_ref[export]
+            block = slot_ref[EXP_BLK + export]
             sum_refs[part][block] += back_ref[slot_ref[export]]
         return carry
 
@@ -465,16 +471,16 @@
         out_ref[:, block * ROWS : (block + 1) * ROWS] = total[0:3]
 
 
-def add_returned(slots, export_block, own, back):
+def add_returned(slots, own, back):
     return pl.pallas_call(
         add_kernel,
         out_shape=jax.ShapeDtypeStruct((3, BLK_DEV * ROWS), f32),
-        in_specs=[SMEM, SMEM, VMEM, VMEM],
+        in_specs=[SMEM, VMEM, VMEM],
         out_specs=VMEM,
         scratch_shapes=[pltpu.VMEM((BLK_DEV, 4, ROWS), f32)] * 4,
         compiler_params=params(16),
         name="add_returned",
-    )(slots, export_block, own, back)
+    )(slots, own, back)
 
 
 def swap(values):
@@ -497,12 +503,17 @@
     members = lax.axis_size("narrow")
     devices = groups * members
 
-    def same_core(value):
-        flips = [[(i, i ^ flip) for i in range(members)] for flip in (1, 4, 5)]
-        return [value] + [lax.ppermute(value, "narrow", flip) for flip in flips]
+    def flipped(value, axis, size, bit):
+        return lax.ppermute(value, axis, [(i, i ^ bit) for i in range(size)])
+
+    def along_x(values):
+        return values + [flipped(value, "narrow", members, 1) for value in values]
+
+    def along_z(values):
+        return values + [flipped(value, "narrow", members, 4) for value in values]
 
     def other_core(values):
-        return values + [lax.ppermute(value, "wide", [(i, i ^ 1) for i in range(groups)]) for value in values]
+        return values + [flipped(value, "wide", groups, 1) for value in values]
 
     outgoing, slots, pm, rows, parts = send_blocks(
         devices,
@@ -517,19 +528,18 @@
         node_lists,
     )
     arrived = swap(outgoing)
-    pms = other_core(same_core(pm))
+    pms = other_core([pm] + [flipped(pm, "narrow", members, bit) for bit in (1, 4, 5)])
     local = local_pull(local_leaves.T, pm)
     arrived, local = lax.optimization_barrier((arrived, local))
 
-    shares = same_core(arrived[:, CAP])
+    shares = along_x([arrived[:, CAP]])
     visitors = arrived.reshape(devices * (CAP + 1), 4, ROWS)
-    visitor_leaves = visitors[:, 3, 0:LEAF_N].astype(jnp.int32).reshape(-1)
-    pulls = remote_pull(visitor_leaves, visitors, pms)
+    pulls = remote_pull(visitors, pms)
     pulls, local, shares = lax.optimization_barrier((pulls, local, shares))
     back = swap(pulls)
-    shares = other_core(shares)
+    shares = other_core(along_z(shares))
     own = node_pull(rows, parts, pm, local, shares)
-    return add_returned(slots, export_block, own, back.reshape(devices * CAP, 4, ROWS))
+    return add_returned(slots, own, back.reshape(devices * CAP, 4, ROWS))
 
 
 def solution(mesh):

time: 99 us -> 117 us (1.18); the launches traced: 99.7 us -> 115 us
  starting transfers between devices: 36.1 us -> 42.2 us
  waiting for transfers between devices: 7.61 us -> 13.2 us
  Pallas kernels: 54.3 us -> 57.7 us
    ppermute x14, waiting for transfers between devices: 0.04 us -> 6.26 us  [flipped(): return lax.ppermute(value, axis, [(i, i ^ bit) for i in range(size)])]
    ppermute x14, starting transfers between devices: 11.6 us -> 15.5 us  [flipped(): return lax.ppermute(value, axis, [(i, i ^ bit) for i in range(size)])]
    pallas_call x1, Pallas kernels: 26.7 us -> 30.2 us  [remote_pull(): pl.pallas_call(remote_kernel, out_shape=jax.ShapeDtypeStruct((devices, CA...]
    all_to_all x2, starting transfers between devices: 24.5 us -> 26.8 us  [swap(): return lax.all_to_all(values, AXES, split_axis=0, concat_axis=0, tiled=True)]
  transfers between devices with their start and end apart: 16 -> 16, of which waited for: 2 -> 4; matrix products, arithmetic and copies ran while one was open for 1% -> 0% of each run, Pallas kernels for 48% -> 45%
where the time goes in v7:
time: 117 us; the launch traced here: 115 us
  Pallas kernels  57.7 us (49%)
  starting transfers between devices  42.2 us (36%)
  waiting for transfers between devices  13.2 us (11%)
  local copies, waits for them, and re-layouts  1.39 us (1%)
    pallas_call x1, Pallas kernels, remote_pull(): pl.pallas_call(remote_kernel, out_shape=jax.ShapeDtypeStruct((devices, CA...  30.2 us
    all_to_all x2, starting transfers between devices, swap(): return lax.all_to_all(values, AXES, split_axis=0, concat_axis=0, tiled=True)  26.8 us
    ppermute x14, starting transfers between devices, flipped(): return lax.ppermute(value, axis, [(i, i ^ bit) for i in range(size)])  15.5 us
    pallas_call x1, Pallas kernels, local_pull(): pl.pallas_call(local_kernel, out_shape=jax.ShapeDtypeStruct((BLK_DEV, 4,...  12.4 us
    pallas_call x1, Pallas kernels, node_pull(): pl.pallas_call(node_kernel, out_shape=jax.ShapeDtypeStruct((BLK_DEV, 4, R...  8.93 us
    all_to_all x2, waiting for transfers between devices, swap(): return lax.all_to_all(values, AXES, split_axis=0, concat_axis=0, tiled=True)  6.94 us
    ppermute x14, waiting for transfers between devices, flipped(): return lax.ppermute(value, axis, [(i, i ^ bit) for i in range(size)])  6.26 us
    pallas_call x1, Pallas kernels, send_blocks(): pl.pallas_call(send_kernel, out_shape=(jax.ShapeDtypeStruct((devices, CAP...  4.43 us
  transfers between devices with their start and end apart: 16, of which 4 were waited for; matrix products, arithmetic and copies ran while one was open for 0% of the time, Pallas kernels for 45%

profile of v7, /device:TPU:1, one launch (start us, length us, event | category | flops | bytes accessed | tf_op | source)
XLA Modules:
  0.0 114.7 jit_solution(10277174490667905921)
XLA Ops:
  0.0 4.4 %send_blocks.1 = (f32[128,3,4,128]{3,2,1,0:T(4,128)}, s32[256]{0:T(256)}, f32[8,8320]{1,0:T(8,128)}, s32[32,128]{1,0:T(8,128)}, s32[32,128]{1,0:T(8,128)}) custom-call(s32[128]{0:T(128)} %block_in.1, s32[128]{0:T(128)} %bitcast.15, s32[8,128]{1,0:T(8,128)} %bitcast.13, f32[3,8192]{1,0:T(4,128)} %pos_in.1, f32[1,8192]{1,0:T(1,128)} %bitcast.12, ...), custom_call_target="tpu_custom_call" | custom-call | tf_op jit(solution)/shard_map/send_blocks/pallas_call | solution.py:140
  4.4 2.1 %collective-permute-start = (f32[8,8320]{1,0:T(8,128)}, f32[8,8320]{1,0:T(8,128)S(1)}, u32[]{:S(2)}, u32[]{:S(2)}) collective-permute-start(f32[8,8320]{1,0:T(8,128)} %get-tuple-element.19.pm_ref.refs_0_), channel_id=1, source_target_pairs={{0,1},{1,0},{2,3},{3,2},{4,5},{5,4},{6,7},{7,6},{8,9},{9,8},{10,11... | collective-permute-start | bytes 798728 | tf_op jit(solution)/shard_map/ppermute | solution.py:507
  6.6 1.6 %collective-permute-start.1 = (f32[8,8320]{1,0:T(8,128)}, f32[8,8320]{1,0:T(8,128)S(1)}, u32[]{:S(2)}, u32[]{:S(2)}) collective-permute-start(f32[8,8320]{1,0:T(8,128)} %get-tuple-element.19.pm_ref.refs_0_), channel_id=1, source_target_pairs={{0,4},{1,5},{2,6},{3,7},{4,0},{5,1},{6,2},{7,3},{8,12},{9,13},{10,... | collective-permute-start | bytes 798728 | tf_op jit(solution)/shard_map/ppermute | solution.py:507
  8.2 0.0 collective-permute-start.2
  8.2 1.2 %collective-permute-start.3 = (f32[8,8320]{1,0:T(8,128)}, f32[8,8320]{1,0:T(8,128)S(1)}, u32[]{:S(2)}, u32[]{:S(2)}) collective-permute-start(f32[8,8320]{1,0:T(8,128)} %get-tuple-element.19.pm_ref.refs_0_), channel_id=1, source_target_pairs={{0,16},{16,0},{32,48},{48,32},{64,80},{80,64},{96,112},{112,96},{1... | collective-permute-start | bytes 798728 | tf_op jit(solution)/shard_map/ppermute | solution.py:507
  9.4 10.2 %all-to-all-start = ((f32[128,3,4,128]{3,2,1,0:T(4,128)}), f32[128,3,4,128]{3,2,1,0:T(4,128)S(1)}, u32[]{:S(2)}, u32[]{:S(2)}) async-start(f32[128,3,4,128]{3,2,1,0:T(4,128)} %get-tuple-element.20), calls=%async_computation | async-start | bytes 1572864 | tf_op jit(solution)/shard_map/all_to_all | solution.py:487
  19.6 0.0 collective-permute-done.refs_1_
  19.6 1.1 collective-permute-start.4
  20.8 0.0 collective-permute-done.1.refs_2_
  20.8 0.3 collective-permute-start.5
  21.1 0.0 collective-permute-done.2.refs_3_
  21.1 0.4 collective-permute-start.6
  21.5 0.0 copy-done.1
  21.5 0.0 copy-done.4
  21.5 12.4 %local_pull.1.local_ref = f32[64,4,128]{2,1,0:T(4,128)S(1)} custom-call(s32[8,64]{1,0:T(8,128)S(1)} %bitcast.11, f32[8,8320]{1,0:T(8,128)S(1)} %copy-done.1), custom_call_target="tpu_custom_call" | custom-call | flops 16000000000 | bytes 1000000 | tf_op jit(solution)/shard_map/local_pull/pallas_call | solution.py:438
  33.9 0.0 copy-start.5
  33.9 0.7 copy-done.5
  34.6 1.8 %all-to-all-done = f32[128,3,4,128]{3,2,1,0:T(4,128)S(1)} async-done(((f32[128,3,4,128]{3,2,1,0:T(4,128)}), f32[128,3,4,128]{3,2,1,0:T(4,128)S(1)}, u32[]{:S(2)}, u32[]{:S(2)}) %all-to-all-start) | async-done | bytes 786464 | tf_op jit(solution)/shard_map/all_to_all | solution.py:487
  36.5 0.4 collective-permute-start.7
  36.9 0.0 collective-permute-done.3.refs_4_
  36.9 0.0 collective-permute-done.4.refs_5_
  36.9 0.0 collective-permute-done.5.refs_6_
  36.9 0.0 collective-permute-done.6.refs_7_
  36.9 30.2 %remote_pull.1 = f32[128,2,4,128]{3,2,1,0:T(4,128)} custom-call(f32[384,4,128]{2,1,0:T(4,128)S(1)} %bitcast.10, f32[8,8320]{1,0:T(8,128)S(1)} %copy-done.1, f32[8,8320]{1,0:T(8,128)S(1)} %collective-permute-done.refs_1_, f32[8,8320]{1,0:T(8,128)S(1)} %collective-permute-done.1.refs_2_, f32[8,8320]{1,0:T(8,128)S(1)} %collective-permute-done.2.refs_3_, ...), custom_call_target="tpu_custom_call" | custom-call | flops 32000000000 | bytes 10000000 | tf_op jit(solution)/shard_map/remote_pull/pallas_call | solution.py:263
  67.1 0.0 copy-start.2
  67.2 0.0 copy-start.3
  67.2 0.0 copy-start.6
  67.2 0.0 collective-permute-done.7.refs_1_
  67.2 0.1 collective-permute-start.8
  67.3 1.5 %collective-permute-start.9 = (f32[128,4,128]{2,1,0:T(4,128)S(1)}, f32[128,4,128]{2,1,0:T(4,128)S(1)}, u32[]{:S(2)}, u32[]{:S(2)}) collective-permute-start(f32[128,4,128]{2,1,0:T(4,128)S(1)} %collective-permute-done.7.refs_1_), channel_id=1, source_target_pairs={{0,4},{1,5},{2,6},{3,7},{4,0},{5,1},{6,2},{7,3},{8,12},{9,13},{10,... | collective-permute-start | bytes 786440 | tf_op jit(solution)/shard_map/ppermute | solution.py:507
  68.7 1.5 %collective-permute-start.10 = (f32[128,4,128]{2,1,0:T(4,128)S(1)}, f32[128,4,128]{2,1,0:T(4,128)S(1)}, u32[]{:S(2)}, u32[]{:S(2)}) collective-permute-start(f32[128,4,128]{2,1,0:T(4,128)S(1)} %slice_bitcast_fusion.refs_0_), channel_id=1, source_target_pairs={{0,16},{16,0},{32,48},{48,32},{64,80},{80,64},{96,112},{112,96},{1... | collective-permute-start | bytes 786440 | tf_op jit(solution)/shard_map/ppermute | solution.py:507
  70.2 0.0 collective-permute-start.11
  70.2 3.9 %collective-permute-done.8.refs_2_ = f32[128,4,128]{2,1,0:T(4,128)S(1)} collective-permute-done((f32[128,4,128]{2,1,0:T(4,128)S(1)}, f32[128,4,128]{2,1,0:T(4,128)S(1)}, u32[]{:S(2)}, u32[]{:S(2)}) %collective-permute-start.8) | collective-permute-done | bytes 262176 | tf_op jit(solution)/shard_map/ppermute | solution.py:507
  74.1 3.3 %collective-permute-start.12 = (f32[128,4,128]{2,1,0:T(4,128)S(1)}, f32[128,4,128]{2,1,0:T(4,128)S(1)}, u32[]{:S(2)}, u32[]{:S(2)}) collective-permute-start(f32[128,4,128]{2,1,0:T(4,128)S(1)} %collective-permute-done.8.refs_2_), channel_id=1, source_target_pairs={{0,16},{16,0},{32,48},{48,32},{64,80},{80,64},{96,112},{112,96},{1... | collective-permute-start | bytes 786440 | tf_op jit(solution)/shard_map/ppermute | solution.py:507
  77.4 2.3 %collective-permute-done.9.refs_3_ = f32[128,4,128]{2,1,0:T(4,128)S(1)} collective-permute-done((f32[128,4,128]{2,1,0:T(4,128)S(1)}, f32[128,4,128]{2,1,0:T(4,128)S(1)}, u32[]{:S(2)}, u32[]{:S(2)}) %collective-permute-start.9) | collective-permute-done | bytes 262176 | tf_op jit(solution)/shard_map/ppermute | solution.py:507
  79.8 1.8 %collective-permute-start.13 = (f32[128,4,128]{2,1,0:T(4,128)S(1)}, f32[128,4,128]{2,1,0:T(4,128)S(1)}, u32[]{:S(2)}, u32[]{:S(2)}) collective-permute-start(f32[128,4,128]{2,1,0:T(4,128)S(1)} %collective-permute-done.9.refs_3_), channel_id=1, source_target_pairs={{0,16},{16,0},{32,48},{48,32},{64,80},{80,64},{96,112},{112,96},{1... | collective-permute-start | bytes 786440 | tf_op jit(solution)/shard_map/ppermute | solution.py:507
  81.6 16.6 %all-to-all-start.1 = ((f32[128,2,4,128]{3,2,1,0:T(4,128)}), f32[128,2,4,128]{3,2,1,0:T(4,128)S(1)}, u32[]{:S(2)}, u32[]{:S(2)}) async-start(f32[128,2,4,128]{3,2,1,0:T(4,128)} %remote_pull.1), calls=%async_computation.1 | async-start | bytes 1048576 | tf_op jit(solution)/shard_map/all_to_all | solution.py:487
  98.2 0.0 collective-permute-done.10.refs_4_
  98.2 0.0 collective-permute-done.11.refs_5_
  98.2 0.0 collective-permute-done.12.refs_6_
  98.2 0.0 collective-permute-done.13.refs_7_
  98.2 0.0 copy-done.2
  98.2 0.0 copy-done.3
  98.3 0.0 copy-done.6
  98.3 8.9 %node_pull.1.own_ref = f32[64,4,128]{2,1,0:T(4,128)S(1)} custom-call(s32[32,128]{1,0:T(8,128)S(1)} %copy-done.2, s32[32,128]{1,0:T(8,128)S(1)} %copy-done.3, f32[8,8320]{1,0:T(8,128)S(1)} %copy-done.1, f32[64,4,128]{2,1,0:T(4,128)S(1)} %copy-done.6, f32[128,4,128]{2,1,0:T(4,128)S(1)} %slice_bitcast_fusion.refs_0_, ...), custom_call_target="tpu_custom_call" | custom-call | flops 12000000000 | bytes 4000000 | tf_op jit(solution)/shard_map/node_pull/pallas_call | solution.py:396
  107.2 5.1 %all-to-all-done.1 = f32[128,2,4,128]{3,2,1,0:T(4,128)S(1)} async-done(((f32[128,2,4,128]{3,2,1,0:T(4,128)}), f32[128,2,4,128]{3,2,1,0:T(4,128)S(1)}, u32[]{:S(2)}, u32[]{:S(2)}) %all-to-all-start.1) | async-done | bytes 524320 | tf_op jit(solution)/shard_map/all_to_all | solution.py:487
  112.3 0.7 copy-done
  113.0 1.8 %add_returned.1 = f32[3,8192]{1,0:T(4,128)} custom-call(s32[256]{0:T(256)S(1)} %copy-done, f32[64,4,128]{2,1,0:T(4,128)S(1)} %node_pull.1.own_ref, f32[256,4,128]{2,1,0:T(4,128)S(1)} %bitcast.9), custom_call_target="tpu_custom_call" | custom-call | tf_op jit(solution)/shard_map/add_returned/pallas_call | solution.py:475
  (4 shorter events, 0.1 us)
Async XLA Ops:
  4.4 15.2 %collective-permute-start = (f32[8,8320]{1,0:T(8,128)}, f32[8,8320]{1,0:T(8,128)S(1)}, u32[]{:S(2)}, u32[]{:S(2)}) collective-permute-start(f32[8,8320]{1,0:T(8,128)} %get-tuple-element.19.pm_ref.refs_0_), channel_id=1, source_target_pairs={{0,1},{1,0},{2,3},{3,2},{4,5},{5,4},{6,7},{7,6},{8,9},{9,8},{10,11... | collective-permute-start | bytes 798728 | tf_op jit(solution)/shard_map/ppermute | solution.py:507
  6.6 14.2 %collective-permute-start.1 = (f32[8,8320]{1,0:T(8,128)}, f32[8,8320]{1,0:T(8,128)S(1)}, u32[]{:S(2)}, u32[]{:S(2)}) collective-permute-start(f32[8,8320]{1,0:T(8,128)} %get-tuple-element.19.pm_ref.refs_0_), channel_id=1, source_target_pairs={{0,4},{1,5},{2,6},{3,7},{4,0},{5,1},{6,2},{7,3},{8,12},{9,13},{10,... | collective-permute-start | bytes 798728 | tf_op jit(solution)/shard_map/ppermute | solution.py:507
  8.2 12.9 %collective-permute-start.2 = (f32[8,8320]{1,0:T(8,128)}, f32[8,8320]{1,0:T(8,128)S(1)}, u32[]{:S(2)}, u32[]{:S(2)}) collective-permute-start(f32[8,8320]{1,0:T(8,128)} %get-tuple-element.19.pm_ref.refs_0_), channel_id=1, source_target_pairs={{0,5},{1,4},{2,7},{3,6},{4,1},{5,0},{6,3},{7,2},{8,13},{9,12},{10,... | collective-permute-start | bytes 798728 | tf_op jit(solution)/shard_map/ppermute | solution.py:507
  8.2 28.7 %collective-permute-start.3 = (f32[8,8320]{1,0:T(8,128)}, f32[8,8320]{1,0:T(8,128)S(1)}, u32[]{:S(2)}, u32[]{:S(2)}) collective-permute-start(f32[8,8320]{1,0:T(8,128)} %get-tuple-element.19.pm_ref.refs_0_), channel_id=1, source_target_pairs={{0,16},{16,0},{32,48},{48,32},{64,80},{80,64},{96,112},{112,96},{1... | collective-permute-start | bytes 798728 | tf_op jit(solution)/shard_map/ppermute | solution.py:507
  9.4 12.1 %copy-start.1 = (f32[8,8320]{1,0:T(8,128)S(1)}, f32[8,8320]{1,0:T(8,128)}, u32[]{:S(2)}) copy-start(f32[8,8320]{1,0:T(8,128)} %get-tuple-element.19.pm_ref.refs_0_) | copy-start | bytes 798724
  9.4 12.1 %copy-start.4 = (s32[64,8]{0,1:T(8,128)S(1)}, s32[64,8]{0,1:T(8,128)}, u32[]{:S(2)}) copy-start(s32[64,8]{0,1:T(8,128)} %param.15) | copy-start | bytes 6148
  9.4 27.0 %all-to-all-start = ((f32[128,3,4,128]{3,2,1,0:T(4,128)}), f32[128,3,4,128]{3,2,1,0:T(4,128)S(1)}, u32[]{:S(2)}, u32[]{:S(2)}) async-start(f32[128,3,4,128]{3,2,1,0:T(4,128)} %get-tuple-element.20), calls=%async_computation | async-start | bytes 1572864 | tf_op jit(solution)/shard_map/all_to_all | solution.py:487
  19.6 17.3 %collective-permute-start.4 = (f32[8,8320]{1,0:T(8,128)S(1)}, f32[8,8320]{1,0:T(8,128)S(1)}, u32[]{:S(2)}, u32[]{:S(2)}) collective-permute-start(f32[8,8320]{1,0:T(8,128)S(1)} %collective-permute-done.refs_1_), channel_id=1, source_target_pairs={{0,16},{16,0},{32,48},{48,32},{64,80},{80,64},{96,112},{112,96},{1... | collective-permute-start | bytes 798728 | tf_op jit(solution)/shard_map/ppermute | solution.py:507
  20.8 16.1 %collective-permute-start.5 = (f32[8,8320]{1,0:T(8,128)S(1)}, f32[8,8320]{1,0:T(8,128)S(1)}, u32[]{:S(2)}, u32[]{:S(2)}) collective-permute-start(f32[8,8320]{1,0:T(8,128)S(1)} %collective-permute-done.1.refs_2_), channel_id=1, source_target_pairs={{0,16},{16,0},{32,48},{48,32},{64,80},{80,64},{96,112},{112,96},{1... | collective-permute-start | bytes 798728 | tf_op jit(solution)/shard_map/ppermute | solution.py:507
  21.1 15.8 %collective-permute-start.6 = (f32[8,8320]{1,0:T(8,128)S(1)}, f32[8,8320]{1,0:T(8,128)S(1)}, u32[]{:S(2)}, u32[]{:S(2)}) collective-permute-start(f32[8,8320]{1,0:T(8,128)S(1)} %collective-permute-done.2.refs_3_), channel_id=1, source_target_pairs={{0,16},{16,0},{32,48},{48,32},{64,80},{80,64},{96,112},{112,96},{1... | collective-permute-start | bytes 798728 | tf_op jit(solution)/shard_map/ppermute | solution.py:507
  33.9 0.7 copy-start.5
  36.5 30.7 %collective-permute-start.7 = (f32[128,4,128]{2,1,0:T(4,128)S(1)}, f32[128,4,128]{2,1,0:T(4,128)S(1)}, u32[]{:S(2)}, u32[]{:S(2)}) collective-permute-start(f32[128,4,128]{2,1,0:T(4,128)S(1)} %slice_bitcast_fusion.refs_0_), channel_id=1, source_target_pairs={{0,1},{1,0},{2,3},{3,2},{4,5},{5,4},{6,7},{7,6},{8,9},{9,8},{10,11... | collective-permute-start | bytes 786440 | tf_op jit(solution)/shard_map/ppermute | solution.py:507
  67.1 31.1 %copy-start.2 = (s32[32,128]{1,0:T(8,128)S(1)}, s32[32,128]{1,0:T(8,128)}, u32[]{:S(2)}) copy-start(s32[32,128]{1,0:T(8,128)} %get-tuple-element.17.row_ref) | copy-start | bytes 49156
  67.2 31.1 %copy-start.3 = (s32[32,128]{1,0:T(8,128)S(1)}, s32[32,128]{1,0:T(8,128)}, u32[]{:S(2)}) copy-start(s32[32,128]{1,0:T(8,128)} %get-tuple-element.18.part_ref) | copy-start | bytes 49156
  67.2 31.1 %copy-start.6 = (f32[64,4,128]{2,1,0:T(4,128)S(1)}, f32[64,4,128]{2,1,0:T(4,128)}, u32[]{:S(2)}) copy-start(f32[64,4,128]{2,1,0:T(4,128)} %copy-done.5) | copy-start | bytes 393220
  67.2 7.0 %collective-permute-start.8 = (f32[128,4,128]{2,1,0:T(4,128)S(1)}, f32[128,4,128]{2,1,0:T(4,128)S(1)}, u32[]{:S(2)}, u32[]{:S(2)}) collective-permute-start(f32[128,4,128]{2,1,0:T(4,128)S(1)} %slice_bitcast_fusion.refs_0_), channel_id=1, source_target_pairs={{0,4},{1,5},{2,6},{3,7},{4,0},{5,1},{6,2},{7,3},{8,12},{9,13},{10,... | collective-permute-start | bytes 786440 | tf_op jit(solution)/shard_map/ppermute | solution.py:507
  67.3 12.5 %collective-permute-start.9 = (f32[128,4,128]{2,1,0:T(4,128)S(1)}, f32[128,4,128]{2,1,0:T(4,128)S(1)}, u32[]{:S(2)}, u32[]{:S(2)}) collective-permute-start(f32[128,4,128]{2,1,0:T(4,128)S(1)} %collective-permute-done.7.refs_1_), channel_id=1, source_target_pairs={{0,4},{1,5},{2,6},{3,7},{4,0},{5,1},{6,2},{7,3},{8,12},{9,13},{10,... | collective-permute-start | bytes 786440 | tf_op jit(solution)/shard_map/ppermute | solution.py:507
  68.7 29.5 %collective-permute-start.10 = (f32[128,4,128]{2,1,0:T(4,128)S(1)}, f32[128,4,128]{2,1,0:T(4,128)S(1)}, u32[]{:S(2)}, u32[]{:S(2)}) collective-permute-start(f32[128,4,128]{2,1,0:T(4,128)S(1)} %slice_bitcast_fusion.refs_0_), channel_id=1, source_target_pairs={{0,16},{16,0},{32,48},{48,32},{64,80},{80,64},{96,112},{112,96},{1... | collective-permute-start | bytes 786440 | tf_op jit(solution)/shard_map/ppermute | solution.py:507
  70.2 28.0 %collective-permute-start.11 = (f32[128,4,128]{2,1,0:T(4,128)S(1)}, f32[128,4,128]{2,1,0:T(4,128)S(1)}, u32[]{:S(2)}, u32[]{:S(2)}) collective-permute-start(f32[128,4,128]{2,1,0:T(4,128)S(1)} %collective-permute-done.7.refs_1_), channel_id=1, source_target_pairs={{0,16},{16,0},{32,48},{48,32},{64,80},{80,64},{96,112},{112,96},{1... | collective-permute-start | bytes 786440 | tf_op jit(solution)/shard_map/ppermute | solution.py:507
  74.1 24.1 %collective-permute-start.12 = (f32[128,4,128]{2,1,0:T(4,128)S(1)}, f32[128,4,128]{2,1,0:T(4,128)S(1)}, u32[]{:S(2)}, u32[]{:S(2)}) collective-permute-start(f32[128,4,128]{2,1,0:T(4,128)S(1)} %collective-permute-done.8.refs_2_), channel_id=1, source_target_pairs={{0,16},{16,0},{32,48},{48,32},{64,80},{80,64},{96,112},{112,96},{1... | collective-permute-start | bytes 786440 | tf_op jit(solution)/shard_map/ppermute | solution.py:507
  79.8 18.5 %collective-permute-start.13 = (f32[128,4,128]{2,1,0:T(4,128)S(1)}, f32[128,4,128]{2,1,0:T(4,128)S(1)}, u32[]{:S(2)}, u32[]{:S(2)}) collective-permute-start(f32[128,4,128]{2,1,0:T(4,128)S(1)} %collective-permute-done.9.refs_3_), channel_id=1, source_target_pairs={{0,16},{16,0},{32,48},{48,32},{64,80},{80,64},{96,112},{112,96},{1... | collective-permute-start | bytes 786440 | tf_op jit(solution)/shard_map/ppermute | solution.py:507
  81.6 30.7 %all-to-all-start.1 = ((f32[128,2,4,128]{3,2,1,0:T(4,128)}), f32[128,2,4,128]{3,2,1,0:T(4,128)S(1)}, u32[]{:S(2)}, u32[]{:S(2)}) async-start(f32[128,2,4,128]{3,2,1,0:T(4,128)} %remote_pull.1), calls=%async_computation.1 | async-start | bytes 1048576 | tf_op jit(solution)/shard_map/all_to_all | solution.py:487
  112.3 0.7 copy-start
